TPU v7x, 512 devices: a whole 4x4x16 slice. The times are simulated.
512 devices in a mesh: ref: 32 (over z, core), qry: 16 (over x, y).
Axes of the slice: x: 4, y: 4, z: 16, core: 2. Of those that a mesh axis runs over, the one named last changes fastest.
Arguments:
- queries: bfloat16 [4096, 1024], P('qry'), may hold values from -1 to 1
- ref_panels: bfloat16 [256, 128, 1024], P('ref', 'qry'), may hold values from -1 to 1
- cand_mask: int32 [32, 256], P('qry', 'ref'), may hold values 0 or 1
- panel_time: int32 [256], replicated, may hold values from 0 to 255, as said below
- w_first: float32 [9, 32], replicated, may hold values from -2 to 2
- b_first: float32 [32], replicated, may hold values from -2.5 to 2.5
- w_second: bfloat16 [9, 32], replicated, may hold values from -0.375 to 0.375
Outputs:
- score_map: bfloat16 [4096, 32768], P('qry', 'ref')
Inputs may be any that keep to these rules, and one draw needn't show every extreme that they name: `panel_time`: A permutation of the reference time blocks. The owner of block t is t // 8; every owner has 8 blocks. The 8 panels of one ingest index of ref (panels held by one index) include at most 1 of one owner, and every ingest index has 1 panel of some owner.
All inputs are finite; a program needn't handle non-finite values. No bound on the sum of `cand_mask` on one device may be relied on, other than what follows from the above.
Results may differ from a plain program's by a relative error of at most 0.0059.
Values may be sent and summed in bfloat16 or wider, within the bound.
No kernel may reach another device: no remote copies, remote signals or barrier semaphores. Data moves between devices by JAX's collectives and lax.ppermute only.
A program may use at most 64 MiB of HBM per device.

v0:
```python
import math

import jax
import jax.numpy as jnp
from jax import lax
from jax.sharding import PartitionSpec as P

FRAMES = 256


def with_halo(cells, sides, width):
    for axis, dim in sides:
        count = lax.axis_size(axis)
        ends = count - 1
        head = lax.slice_in_dim(cells, 0, width, axis=dim)
        tail = lax.slice_in_dim(cells, cells.shape[dim] - width, cells.shape[dim], axis=dim)
        cells = jnp.concatenate(
            [
                lax.ppermute(tail, axis, [(i, (i + 1) % count) for i in range(ends)]),
                cells,
                lax.ppermute(head, axis, [((i + 1) % count, i) for i in range(ends)]),
            ],
            axis=dim,
        )
    return cells


def layer_one(strip_cols, w_first, b_first):
    height = strip_cols.shape[0]
    widths = strip_cols.shape[1] - 2
    padded = jnp.pad(strip_cols.astype(jnp.float32), ((1, 1), (0, 0)))
    summed = jnp.broadcast_to(b_first[:, None, None], (b_first.shape[0], height, widths))
    for row_shift in range(3):
        for col_shift in range(3):
            summed = (
                summed
                + w_first[3 * row_shift + col_shift][:, None, None]
                * padded[row_shift : row_shift + height, col_shift : col_shift + widths][None]
            )
    return jnp.maximum(summed, 0.0).astype(jnp.bfloat16)


def layer_two(hidden, w_second):
    height = hidden.shape[1]
    widths = hidden.shape[2] - 2
    padded = jnp.pad(hidden, ((0, 0), (1, 1), (0, 0)))
    summed = jnp.zeros((height, widths), jnp.float32)
    for row_shift in range(3):
        for col_shift in range(3):
            summed = summed + jnp.einsum(
                "c,chw->hw",
                w_second[3 * row_shift + col_shift],
                padded[:, row_shift : row_shift + height, col_shift : col_shift + widths],
                preferred_element_type=jnp.float32,
            )
    return summed


def shards(queries, ref_panels, cand_mask, panel_time, w_first, b_first, w_second):
    owners_count = lax.axis_size("ref")
    my_owner = lax.axis_index("ref")
    blocks_dev = ref_panels.shape[0]
    frames_dev = queries.shape[0]
    videos = frames_dev // FRAMES
    slot_count = max(1, (2 * blocks_dev + owners_count - 1) // owners_count)
    times = panel_time.reshape(owners_count, blocks_dev)
    owner_ids = times // blocks_dev
    within = times % blocks_dev
    earlier = jnp.arange(blocks_dev)[None, :] < jnp.arange(blocks_dev)[:, None]
    same_owner = owner_ids[:, :, None] == owner_ids[:, None, :]
    ranks = jnp.sum((same_owner & earlier[None]).astype(jnp.int32), axis=2)
    owner_mine = lax.dynamic_index_in_dim(owner_ids, my_owner, 0, keepdims=False)
    rank_mine = lax.dynamic_index_in_dim(ranks, my_owner, 0, keepdims=False)
    dest_ids = jnp.arange(owners_count)
    slot_ids = jnp.arange(slot_count)
    select = (
        (owner_mine[None, None, :] == dest_ids[:, None, None])
        & (rank_mine[None, None, :] == slot_ids[None, :, None])
    ).astype(jnp.bfloat16)
    outgoing = jnp.einsum(
        "oki,ird->okrd", select, ref_panels, preferred_element_type=jnp.float32
    ).astype(jnp.bfloat16)
    incoming = lax.all_to_all(outgoing, "ref", split_axis=0, concat_axis=0, tiled=True)
    placing = (
        (owner_ids == my_owner)[None, :, None, :]
        & (ranks[None, :, None, :] == slot_ids[None, None, :, None])
        & (within[None, :, None, :] == jnp.arange(blocks_dev)[:, None, None, None])
    )
    placement = jnp.sum(placing.astype(jnp.int32), axis=3).astype(jnp.bfloat16)
    owned = jnp.einsum(
        "tsk,skrd->trd", placement, incoming, preferred_element_type=jnp.float32
    ).astype(jnp.bfloat16)
    tiles = jnp.einsum(
        "qd,brd->qbr",
        queries,
        lax.all_gather(owned, "qry", axis=1, tiled=True),
        preferred_element_type=jnp.float32,
    ).astype(jnp.bfloat16)
    panel_len = tiles.shape[2]
    ref_cols = blocks_dev * panel_len
    qblock_count = cand_mask.shape[0]
    keeper = cand_mask.astype(jnp.bfloat16)[:, None, :, None]
    sims = (
        tiles.reshape(qblock_count, frames_dev // qblock_count, blocks_dev, panel_len) * keeper
    ).reshape(videos, FRAMES, ref_cols)
    first_layer = jax.vmap(layer_one, in_axes=(0, None, None))
    second_layer = jax.vmap(layer_two, in_axes=(0, None))
    single = with_halo(sims, (("ref", 2),), 1)
    spread = jnp.pad(single, ((0, 0), (0, 0), (1, 1)))
    first_col = first_layer(spread[:, :, 1:4], w_first, b_first)[:, :, :, 0]
    last_col = first_layer(spread[:, :, ref_cols : ref_cols + 3], w_first, b_first)[:, :, :, 0]
    edge_pair = jnp.stack([first_col, last_col])
    near_cols = with_halo(edge_pair, (("ref", 0),), 1)
    left_fill = near_cols[0]
    right_fill = near_cols[3]
    left_use = my_owner >= 0
    right_use = my_owner >= 0
    block_cols = math.gcd(256, ref_cols)
    count = ref_cols // block_cols

    def one_block(block_index):
        strip_cols = lax.dynamic_slice_in_dim(spread, block_index * block_cols, block_cols + 4, 2)
        hidden = first_layer(strip_cols, w_first, b_first)
        first = jnp.where((block_index == 0) & left_use, left_fill, hidden[:, :, :, 0])
        final = jnp.where((block_index == count - 1) & right_use, right_fill, hidden[:, :, :, -1])
        hidden = hidden.at[:, :, :, 0].set(first).at[:, :, :, -1].set(final)
        return second_layer(hidden, w_second).astype(jnp.bfloat16)

    blocks_out = lax.map(one_block, jnp.arange(count, dtype=jnp.int32))
    return jnp.transpose(blocks_out, (1, 2, 0, 3)).reshape(frames_dev, ref_cols)


def solution(mesh):
    placed = (P("qry", None), P("ref", "qry", None), P("qry", "ref"), P(), P(), P(), P())
    return jax.shard_map(
        shards, mesh=mesh, in_specs=placed, out_specs=P("qry", "ref"), check_vma=False
    )
```

profile of v0, /device:TPU:1, one launch (start us, length us, event | category | flops | bytes accessed | tf_op | source)
XLA Modules:
  0.0 399.4 jit_solution(5966374788965295155)
XLA Ops:
  10.3 16.7 %all-to-all-start = ((bf16[32,1,8,1024]{3,2,1,0:T(8,128)(2,1)}), bf16[32,1,8,1024]{3,2,1,0:T(8,128)(2,1)S(1)}, u32[]{:S(2)}, u32[]{:S(2)}) async-start(bf16[32,1,8,1024]{3,2,1,0:T(8,128)(2,1)} %copy.95), calls=%async_computation | async-start | bytes 1048576 | tf_op jit(solution)/shard_map/all_to_all | solution.py:83
  27.2 33.4 %all-to-all-done = bf16[32,1,8,1024]{3,2,1,0:T(8,128)(2,1)S(1)} async-done(((bf16[32,1,8,1024]{3,2,1,0:T(8,128)(2,1)}), bf16[32,1,8,1024]{3,2,1,0:T(8,128)(2,1)S(1)}, u32[]{:S(2)}, u32[]{:S(2)}) %all-to-all-start) | async-done | bytes 524320 | tf_op jit(solution)/shard_map/all_to_all | solution.py:83
  63.0 49.9 %all-gather.2.cloned.1.call-done = bf16[8,128,1024]{2,0,1:T(8,128)(2,1)} async-done(((bf16[8,8,1024]{2,0,1:T(8,128)(2,1)}), bf16[8,128,1024]{2,0,1:T(8,128)(2,1)}) %all-gather.2.cloned.1.call-update) | async-done | bytes 2097168 | tf_op jit(solution)/shard_map/all_gather | solution.py:96
  112.8 4.0 fusion.52
  117.4 4.6 %collective-permute-start = (bf16[1,256,1]{2,1,0:T(8,128)(2,1)S(1)}, bf16[1,256,1]{2,1,0:T(8,128)(2,1)S(1)}, u32[]{:S(2)}, u32[]{:S(2)}) collective-permute-start(bf16[1,256,1]{2,1,0:T(8,128)(2,1)S(1)} %get-tuple-element.254), channel_id=1, source_target_pairs={{0,16},{16,32},{32,48},{48,64},{64,80},{80,96},{96,112},{112,128},... | collective-permute-start | bytes 1544 | tf_op jit(solution)/shard_map/ppermute | solution.py:19
  123.9 3.6 collective-permute-done.1
  132.3 3.6 collective-permute-start.2
  138.3 251.9 %while.15 = (s32[]{:T(128)}, bf16[4,1,256,256]{3,2,1,0:T(8,128)(2,1)}, f32[32]{0:T(128)}, f32[9,32]{1,0:T(8,128)S(1)}, s32[4]{0:T(128)}, /*index=5*/bf16[1,256,1...) while((s32[]{:T(128)}, ...), condition=%wide.region_3.4_spmd, body=%wide.region_2.3_spmd.sunk | while | flops 80692224 | bytes 88695848 | solution.py:129
  147.5 14.2 %maximum_convert_fusion.4 = bf16[1,32,256,258]{2,1,3,0:T(8,128)(2,1)S(1)} fusion(f32[256,258]{0,1:T(8,128)S(1)} %copy.138, f32[32]{0:T(128)S(1)} %get-tuple-element.355, f32[256,258]{0,1:T(8,128)} %copy.139, f32[32]{0:T(128)S(1)} %get-tuple-element.357, f32[256,258]{0,1:T(8,128)} %copy.140, f32[32]{0:T(128)S(1)} %get-tuple-element.359, ...), kind=kLoop, calls=%fused_computation.clone.1 | loop fusion | flops 42270720 | bytes 6606080 | tf_op jit(solution)/shard_map/while/body/eval_jaxpr/vmap()/convert_element_type | solution.py:40
  189.2 3.6 fusion.124
  193.0 3.6 fusion.125
  196.7 3.6 fusion.126
  210.5 14.2 %maximum_convert_fusion.4 = bf16[1,32,256,258]{2,1,3,0:T(8,128)(2,1)S(1)} fusion(f32[256,258]{0,1:T(8,128)S(1)} %copy.138, f32[32]{0:T(128)S(1)} %get-tuple-element.355, f32[256,258]{0,1:T(8,128)} %copy.139, f32[32]{0:T(128)S(1)} %get-tuple-element.357, f32[256,258]{0,1:T(8,128)} %copy.140, f32[32]{0:T(128)S(1)} %get-tuple-element.359, ...), kind=kLoop, calls=%fused_computation.clone.1 | loop fusion | flops 42270720 | bytes 6606080 | tf_op jit(solution)/shard_map/while/body/eval_jaxpr/vmap()/convert_element_type | solution.py:40
  252.2 3.6 fusion.124
  255.9 3.6 fusion.125
  259.7 3.6 fusion.126
  273.5 14.2 %maximum_convert_fusion.4 = bf16[1,32,256,258]{2,1,3,0:T(8,128)(2,1)S(1)} fusion(f32[256,258]{0,1:T(8,128)S(1)} %copy.138, f32[32]{0:T(128)S(1)} %get-tuple-element.355, f32[256,258]{0,1:T(8,128)} %copy.139, f32[32]{0:T(128)S(1)} %get-tuple-element.357, f32[256,258]{0,1:T(8,128)} %copy.140, f32[32]{0:T(128)S(1)} %get-tuple-element.359, ...), kind=kLoop, calls=%fused_computation.clone.1 | loop fusion | flops 42270720 | bytes 6606080 | tf_op jit(solution)/shard_map/while/body/eval_jaxpr/vmap()/convert_element_type | solution.py:40
  315.2 3.6 fusion.124
  318.9 3.6 fusion.125
  322.7 3.6 fusion.126
  336.5 14.2 %maximum_convert_fusion.4 = bf16[1,32,256,258]{2,1,3,0:T(8,128)(2,1)S(1)} fusion(f32[256,258]{0,1:T(8,128)S(1)} %copy.138, f32[32]{0:T(128)S(1)} %get-tuple-element.355, f32[256,258]{0,1:T(8,128)} %copy.139, f32[32]{0:T(128)S(1)} %get-tuple-element.357, f32[256,258]{0,1:T(8,128)} %copy.140, f32[32]{0:T(128)S(1)} %get-tuple-element.359, ...), kind=kLoop, calls=%fused_computation.clone.1 | loop fusion | flops 42270720 | bytes 6606080 | tf_op jit(solution)/shard_map/while/body/eval_jaxpr/vmap()/convert_element_type | solution.py:40
  378.2 3.6 fusion.124
  381.9 3.6 fusion.125
  385.6 3.6 fusion.126
  (184 shorter events, 160.9 us)
Async XLA Ops:
  6.5 106.3 %copy-start = (bf16[256,1024]{1,0:T(8,128)(2,1)S(1)}, bf16[256,1024]{1,0:T(8,128)(2,1)}, u32[]{:S(2)}) copy-start(bf16[256,1024]{1,0:T(8,128)(2,1)} %param.13) | copy-start | bytes 1572868
  10.3 50.3 %all-to-all-start = ((bf16[32,1,8,1024]{3,2,1,0:T(8,128)(2,1)}), bf16[32,1,8,1024]{3,2,1,0:T(8,128)(2,1)S(1)}, u32[]{:S(2)}, u32[]{:S(2)}) async-start(bf16[32,1,8,1024]{3,2,1,0:T(8,128)(2,1)} %copy.95), calls=%async_computation | async-start | bytes 1048576 | tf_op jit(solution)/shard_map/all_to_all | solution.py:83
  27.1 85.8 %all-gather.2.cloned.1.call-start = ((), (), s32[]{:S(2)}) async-start(), calls=%async_computation.1 | async-start | bytes 2228224 | tf_op jit(solution)/shard_map/all_gather | solution.py:96
  62.7 61.1 %copy-start.2 = (f32[9,32]{1,0:T(8,128)S(1)}, f32[9,32]{1,0:T(8,128)}, u32[]{:S(2)}) copy-start(f32[9,32]{1,0:T(8,128)} %param.17) | copy-start | bytes 3460
  117.4 6.5 %collective-permute-start = (bf16[1,256,1]{2,1,0:T(8,128)(2,1)S(1)}, bf16[1,256,1]{2,1,0:T(8,128)(2,1)S(1)}, u32[]{:S(2)}, u32[]{:S(2)}) collective-permute-start(bf16[1,256,1]{2,1,0:T(8,128)(2,1)S(1)} %get-tuple-element.254), channel_id=1, source_target_pairs={{0,16},{16,32},{32,48},{48,64},{64,80},{80,96},{96,112},{112,128},... | collective-permute-start | bytes 1544 | tf_op jit(solution)/shard_map/ppermute | solution.py:19
  121.9 5.6 %collective-permute-start.1 = (bf16[1,256,1]{2,1,0:T(8,128)(2,1)S(1)}, bf16[1,256,1]{2,1,0:T(8,128)(2,1)S(1)}, u32[]{:S(2)}, u32[]{:S(2)}) collective-permute-start(bf16[1,256,1]{2,1,0:T(8,128)(2,1)S(1)} %get-tuple-element.253), channel_id=1, source_target_pairs={{16,0},{32,16},{48,32},{64,48},{80,64},{96,80},{112,96},{128,112},... | collective-permute-start | bytes 1544 | tf_op jit(solution)/shard_map/ppermute | solution.py:21
  129.6 8.1 %collective-permute-start.3 = (bf16[1,1,32,256]{3,2,1,0:T(8,128)(2,1)S(1)}, bf16[1,1,32,256]{3,2,1,0:T(8,128)(2,1)}, u32[]{:S(2)}, u32[]{:S(2)}) collective-permute-start(bf16[1,1,32,256]{3,2,1,0:T(8,128)(2,1)S(1)} %maximum_convert_fusion.1), channel_id=1, source_target_pairs={{16,0},{32,16},{48,32},{64,48},{80,64},{96,80},{112,96},{128,112},... | collective-permute-start | bytes 49160 | tf_op jit(solution)/shard_map/ppermute | solution.py:21
  132.3 5.4 %collective-permute-start.2 = (bf16[1,1,32,256]{3,2,1,0:T(8,128)(2,1)S(1)}, bf16[1,1,32,256]{3,2,1,0:T(8,128)(2,1)}, u32[]{:S(2)}, u32[]{:S(2)}) collective-permute-start(bf16[1,1,32,256]{3,2,1,0:T(8,128)(2,1)S(1)} %maximum_convert_fusion.2), channel_id=1, source_target_pairs={{0,16},{16,32},{32,48},{48,64},{64,80},{80,96},{96,112},{112,128},... | collective-permute-start | bytes 49160 | tf_op jit(solution)/shard_map/ppermute | solution.py:19
  161.8 3.2 copy-start.1
  161.8 7.3 %copy-start.3 = (bf16[9,32]{1,0:T(8,128)(2,1)S(1)}, bf16[9,32]{1,0:T(8,128)(2,1)}, u32[]{:S(2)}) copy-start(bf16[9,32]{1,0:T(8,128)(2,1)} %get-tuple-element.413) | copy-start | bytes 1732 | tf_op jit(solution)/shard_map/while
  224.8 3.2 copy-start.1
  224.8 7.3 %copy-start.3 = (bf16[9,32]{1,0:T(8,128)(2,1)S(1)}, bf16[9,32]{1,0:T(8,128)(2,1)}, u32[]{:S(2)}) copy-start(bf16[9,32]{1,0:T(8,128)(2,1)} %get-tuple-element.413) | copy-start | bytes 1732 | tf_op jit(solution)/shard_map/while
  287.8 3.2 copy-start.1
  287.8 7.3 %copy-start.3 = (bf16[9,32]{1,0:T(8,128)(2,1)S(1)}, bf16[9,32]{1,0:T(8,128)(2,1)}, u32[]{:S(2)}) copy-start(bf16[9,32]{1,0:T(8,128)(2,1)} %get-tuple-element.413) | copy-start | bytes 1732 | tf_op jit(solution)/shard_map/while
  350.7 3.2 copy-start.1
  350.7 7.3 %copy-start.3 = (bf16[9,32]{1,0:T(8,128)(2,1)S(1)}, bf16[9,32]{1,0:T(8,128)(2,1)}, u32[]{:S(2)}) copy-start(bf16[9,32]{1,0:T(8,128)(2,1)} %get-tuple-element.413) | copy-start | bytes 1732 | tf_op jit(solution)/shard_map/while
Sparse Core Ops, SparseCore 0:
  62.1 50.7 all-gather.1
where the time goes:
time: 404 us; the launch traced here: 399 us
  matrix products  127 us (31%)
  waiting for transfers between devices  86.9 us (22%)
  other arithmetic  78.1 us (19%)
  local copies, waits for them, and re-layouts  56.3 us (14%)
  starting transfers between devices  28.8 us (7%)
  between operations  13.6 us (3%)
  loops' own time  8.92 us (2%)
    dot_general x36, matrix products, layer_two(): jnp.einsum('c,chw->hw', w_second[3 * row_shift + col_shift], padded[:, ro...  120 us
    convert_element_type x6, other arithmetic, layer_one(): return jnp.maximum(summed, 0.0).astype(jnp.bfloat16)  58.4 us
    all_gather x1, waiting for transfers between devices, shards(): lax.all_gather(owned, 'qry', axis=1, tiled=True)  49.9 us
    all_to_all x1, waiting for transfers between devices, shards(): lax.all_to_all(outgoing, 'ref', split_axis=0, concat_axis=0, tiled=True)  33.4 us
    mul x44, local copies, waits for them, and re-layouts, layer_one(): w_first[3 * row_shift + col_shift][:, None, None]  24.6 us
    all_to_all x1, starting transfers between devices, shards(): lax.all_to_all(outgoing, 'ref', split_axis=0, concat_axis=0, tiled=True)  16.7 us
    while x20, local copies, waits for them, and re-layouts  12.8 us
    scatter x8, other arithmetic, one_block(): hidden = hidden.at[:, :, :, 0].set(first).at[:, :, :, -1].set(final)  10.9 us
  transfers between devices with their start and end apart: 6, of which 3 were waited for; matrix products, arithmetic and copies ran while one was open for 1% of the time, Pallas kernels for 0%

commit v1 on v0

v1 whole, which is shorter than its diff:
```python
import functools

import jax
import jax.numpy as jnp
import numpy as np
from jax import lax
from jax.experimental import pallas as pl
from jax.experimental.pallas import tpu as pltpu
from jax.sharding import PartitionSpec as P

BF = jnp.bfloat16
F = jnp.float32
I = jnp.int32
NT = (((1,), (1,)), ((), ()))
ROWS = 256
COLS = 1024
BLOCKS = 8
LANES = 128
WIN = 32
BPI = 4


def from_above(v):
    row = lax.broadcasted_iota(I, v.shape, 0)
    return jnp.where(row == 0, 0.0, pltpu.roll(v, 1, 0))


def from_below(v):
    row = lax.broadcasted_iota(I, v.shape, 0)
    n = v.shape[0]
    return jnp.where(row == n - 1, 0.0, pltpu.roll(v, n - 1, 0))


def quarters(lane, four):
    return jnp.where(
        lane < 64,
        jnp.where(lane < 32, four[0], four[1]),
        jnp.where(lane < 96, four[2], four[3]),
    )


def refine_body(
    mask_ref, slab_ref, q_hbm, sel1_hbm, w1_hbm, w2_hbm, sel2_hbm,
    out_ref, own_ref, part_ref, sims, gg, xs, hs, acc, ee, q_ref, sel1_ref, w1_ref, w2_ref, sel2_ref, sems,
):
    loads = [
        pltpu.make_async_copy(src, dst, sems.at[n])
        for n, (src, dst) in enumerate(
            zip((q_hbm, sel1_hbm, w1_hbm, w2_hbm, sel2_hbm), (q_ref, sel1_ref, w1_ref, w2_ref, sel2_ref))
        )
    ]
    for load in loads:
        load.start()
    loads[0].wait()
    loads[1].wait()
    lane = lax.broadcasted_iota(I, (ROWS, LANES), 1)
    top = lax.broadcasted_iota(I, (ROWS, LANES), 0) < ROWS // 2
    q = q_ref[...]
    g0 = jnp.zeros((ROWS, 2 * LANES), F)
    for t in range(0, BLOCKS, 2):
        slab = slab_ref[:, t : t + 2].swapaxes(0, 1).reshape(2 * LANES, q.shape[1])
        s = lax.dot_general(q, slab, NT, preferred_element_type=F)
        for u in range(2):
            keep = jnp.where(top, mask_ref[0, t + u], mask_ref[1, t + u]).astype(F)
            v = s[:, LANES * u : LANES * (u + 1)].astype(BF).astype(F) * keep
            sims[t + u] = v
            g0 = g0 + jnp.dot(
                v.astype(BF), sel1_ref[LANES * (t + u) : LANES * (t + u + 1), :], preferred_element_type=F
            )
    own_ref[...] = g0[:, :LANES]
    g = g0 + pltpu.roll(from_above(g0), 2 * LANES - 1, 1) + pltpu.roll(from_below(g0), 1, 1)
    gg[0] = g[:, :LANES]
    gg[1] = g[:, LANES:]
    ee[...] = jnp.zeros((2, ROWS, LANES), F)
    group = ROWS * BPI
    for load in loads[2:]:
        load.wait()

    def step(it, carry):
        for b in range(BPI):
            k = it * BPI + b
            s = sims[k]
            up = from_above(s)
            dn = from_below(s)
            ge = gg[k // 4]
            base = lax.rem(k, 4) * 24
            for w in range(4):
                e = pltpu.roll(ge, lax.rem(96 - 6 * w + LANES - base, LANES), 1)
                parts = (
                    pltpu.roll(up, (LANES - WIN * w) % LANES, 1) if w else up,
                    pltpu.roll(s, (LANES + WIN - WIN * w) % LANES, 1) if w != 1 else s,
                    pltpu.roll(dn, (LANES + 2 * WIN - WIN * w) % LANES, 1) if w != 2 else dn,
                    jnp.where(lane < 102, e, 1.0),
                )
                x = quarters(lane, parts).astype(BF)
                at = group * w + ROWS * b
                xs[at : at + ROWS, 0:LANES] = x
                xs[at : at + ROWS, LANES : 2 * LANES] = x
        x = xs[...]
        for n in range(4):
            h = jnp.dot(x, w1_ref[:, 256 * n : 256 * (n + 1)], preferred_element_type=F)
            hs[:, 256 * n : 256 * (n + 1)] = jnp.maximum(h.astype(BF), jnp.zeros((), BF))

        @pl.when(it == 0)
        def _():
            hs[0:ROWS, 0:32] = jnp.zeros((ROWS, 32), BF)

        @pl.when(it == BLOCKS // BPI - 1)
        def _():
            hs[4 * group - ROWS : 4 * group, WIN * 32 - 32 : WIN * 32] = jnp.zeros((ROWS, 32), BF)

        p = [
            jnp.dot(
                hs[group * w : group * (w + 1), :], w2_ref[:, LANES * w : LANES * (w + 1)], preferred_element_type=F
            )
            for w in range(4)
        ]
        for b in range(BPI):
            k = it * BPI + b
            pb = [p[w][ROWS * b : ROWS * (b + 1)] for w in range(4)]
            a0 = quarters(lane, pb)
            a1 = pltpu.roll(quarters(lane, [pb[3], pb[0], pb[1], pb[2]]), LANES - WIN, 1)
            a2 = pltpu.roll(quarters(lane, [pb[2], pb[3], pb[0], pb[1]]), LANES - 2 * WIN, 1)
            acc[k] = a1 + from_above(a0) + from_below(a2)
            base = lax.rem(k, 4) * 24
            tot = ee[k // 4]
            for w in range(4):
                moved = pltpu.roll(pb[w], lax.rem(base + 6 * w + LANES - WIN * ((w + 3) % 4), LANES), 1)
                tot = jnp.where((lane >= base + 6 * w) & (lane < base + 6 * w + 6), moved, tot)
            ee[k // 4] = tot
        return carry

    lax.fori_loop(0, BLOCKS // BPI, step, 0)
    kind = lax.rem(lane, 3)
    his, los = [], []
    for half in range(2):
        hi, lo = settle(kind, ee[half])
        his.append(hi)
        los.append(lo)
    hi = jnp.concatenate(his, axis=1)
    lo = jnp.concatenate(los, axis=1)
    for k in range(0, BLOCKS, 2):
        pick = sel2_ref[:, LANES * k : LANES * (k + 2)]
        extra = jnp.dot(hi, pick, preferred_element_type=F) + jnp.dot(lo, pick, preferred_element_type=F)
        for u in range(2):
            total = acc[k + u] + extra[:, LANES * u : LANES * (u + 1)]
            if k + u == 0:
                part_ref[0] = total
            elif k + u == BLOCKS - 1:
                part_ref[1] = total
            else:
                out_ref[:, LANES * (k + u) : LANES * (k + u + 1)] = total.astype(BF)


def settle(kind, v):
    c = jnp.where(kind == 0, from_above(v), jnp.where(kind == 1, v, from_below(v)))
    hi = c.astype(BF)
    return hi, (c - hi.astype(F)).astype(BF)


def sides_body(
    ends_ref, q_ref, left_ref, right_ref, own_ref, part_ref, w1x_ref, w2x_ref, selx_ref, sel3_ref, old_ref,
    out_ref, held, sems,
):
    del old_ref
    lane = lax.broadcasted_iota(I, (ROWS, LANES), 1)
    edge = jnp.concatenate([left_ref[...], right_ref[...]], axis=0)
    se = lax.dot_general(q_ref[...], edge, NT, preferred_element_type=F).astype(BF).astype(F)
    top = lax.broadcasted_iota(I, (ROWS, 16), 0) < ROWS // 2
    left = lax.broadcasted_iota(I, (ROWS, 16), 1) < 8
    bits = edge.astype(F)
    keep = jnp.where(
        top, jnp.where(left, bits[2:3, 0:1], bits[10:11, 0:1]), jnp.where(left, bits[3:4, 0:1], bits[11:12, 0:1])
    )
    g0 = jnp.where(lane >= 96, own_ref[...], 0.0)
    g0 = g0 + jnp.dot((se * keep).astype(BF), selx_ref[...], preferred_element_type=F)
    g = g0 + pltpu.roll(from_above(g0), LANES - 1, 1) + pltpu.roll(from_below(g0), 1, 1)
    xw = jnp.where((lane >= 120) & (lane < 123), 1.0, g).astype(BF)
    hx = jnp.dot(xw, w1x_ref[0:LANES, :], preferred_element_type=F)
    hx = hx + jnp.dot(xw, w1x_ref[LANES : 2 * LANES, :], preferred_element_type=F)
    live = jnp.where(lane < 32, ends_ref[0], jnp.where(lane >= 96, ends_ref[1], 1))
    hx = jnp.maximum(hx, 0.0) * live.astype(F)
    sums = jnp.dot(hx.astype(BF), w2x_ref[...], preferred_element_type=F)
    hi, lo = settle(lax.rem(lane, 3), sums)
    extra = jnp.dot(hi, sel3_ref[...], preferred_element_type=F) + jnp.dot(lo, sel3_ref[...], preferred_element_type=F)
    copies = []
    for side in range(2):
        held[side] = (part_ref[side] + extra[:, LANES * side : LANES * (side + 1)]).astype(BF)
        block = out_ref.at[:, pl.ds(side * (COLS - LANES), LANES)]
        copies.append(pltpu.make_async_copy(held.at[side], block, sems.at[side]))
        copies[-1].start()
    for copy in copies:
        copy.wait()


def iotas(rows, cols):
    return lax.broadcasted_iota(I, (rows, cols), 0), lax.broadcasted_iota(I, (rows, cols), 1)


def weights(w_first, b_first, w_second):
    coarse = functools.partial(lax.reduce_precision, exponent_bits=8, mantissa_bits=7)
    hi = coarse(w_first)
    mid = w_first - hi
    b0 = coarse(b_first)
    b1 = coarse(b_first - b0)
    b2 = b_first - b0 - b1
    second = w_second.astype(F)
    rows = jnp.concatenate([hi, mid, jnp.stack([b0, b1, b2])])
    wide = jnp.tile(rows, (1, WIN))
    tall = jnp.tile(second.T, (WIN, 1))
    width = WIN * 32
    row, col = iotas(LANES, width)
    pos = col // 32
    shift, inner = row // WIN, row % WIN
    halves = []
    for part in range(2):
        total = jnp.zeros((LANES, width), F)
        for a in range(3):
            for b in range(3):
                tap = wide[9 * part + 3 * a + b][None, :]
                hit = (shift == a) & (inner == pos + b - 1)
                if b == 0:
                    hit = hit | ((row == 96 + a) & (pos == 0))
                if b == 2:
                    hit = hit | ((row == 99 + a) & (pos == WIN - 1))
                total = total + jnp.where(hit, tap, 0.0)
        if part == 0:
            for j in range(3):
                total = total + jnp.where(row == 102 + j, wide[18 + j][None, :], 0.0)
        halves.append(total.astype(BF))
    w1 = jnp.concatenate(halves)
    row, col = iotas(width, 4 * LANES)
    pos = row // 32
    w = col // LANES
    a_of = ((col % LANES) // WIN + 4 - w) % 4
    inner = col % WIN
    total = jnp.zeros((width, 4 * LANES), F)
    for a in range(3):
        for b in range(3):
            hit = (a_of == a) & (inner == pos + 1 - b)
            if b == 2:
                hit = hit | ((a_of == 3) & (inner == a) & (pos == 0))
            if b == 0:
                hit = hit | ((a_of == 3) & (inner == 3 + a) & (pos == WIN - 1))
            total = total + jnp.where(hit, tall[:, 3 * a + b][:, None], 0.0)
    w2 = total.astype(BF)
    row, col = iotas(LANES, LANES)
    halves = []
    for part in range(2):
        total = jnp.zeros((LANES, LANES), F)
        for a in range(3):
            for b in range(3):
                tap = wide[9 * part + 3 * a + b, :LANES][None, :]
                hit = jnp.zeros((LANES, LANES), jnp.bool_)
                for h in range(4):
                    hit = hit | ((col // 32 == h) & (row == SIDE_LANE[SIDE_HIDDEN[h] + b - 1] - 1 + a))
                total = total + jnp.where(hit, tap, 0.0)
        if part == 0:
            for j in range(3):
                total = total + jnp.where(row == 120 + j, wide[18 + j, :LANES][None, :], 0.0)
        halves.append(total.astype(BF))
    w1x = jnp.concatenate(halves)
    total = jnp.zeros((LANES, LANES), F)
    for a in range(3):
        for b in range(3):
            hit = jnp.zeros((LANES, LANES), jnp.bool_)
            for h in range(4):
                for j, out in enumerate((0, 1, COLS - 2, COLS - 1)):
                    if SIDE_HIDDEN[h] == out + b - 1:
                        hit = hit | ((row // 32 == h) & (col == 3 * j + a))
            total = total + jnp.where(hit, tall[:LANES, 3 * a + b][:, None], 0.0)
    return w1, w2, w1x, total.astype(BF)


SIDE_LANE = {0: 97, 1: 100, COLS - 2: 103, COLS - 1: 106, -2: 109, -1: 112, COLS: 115, COLS + 1: 118}
SIDE_HIDDEN = (-1, 0, COLS - 1, COLS)


def selectors():
    i, l = np.indices((COLS, 2 * LANES))
    m, s = 16 * (l // LANES) + (l % LANES) // 6, (l % LANES) % 6
    fit = l % LANES < 96
    hit = (fit & (s == 1) & (i == WIN * m - 1)) | (fit & (s == 4) & (i == WIN * m + WIN))
    for c in (0, 1, COLS - 2, COLS - 1):
        hit = hit | ((l == SIDE_LANE[c]) & (i == c))
    sel1 = hit.astype(BF)
    i, l = np.indices((16, LANES))
    hit = np.zeros((16, LANES), bool)
    for row, c in ((0, -2), (1, -1), (8, COLS), (9, COLS + 1)):
        hit = hit | ((i == row) & (l == SIDE_LANE[c]))
    selx = hit.astype(BF)
    l, j = np.indices((2 * LANES, COLS))
    m, s = 16 * (l // LANES) + (l % LANES) // 6, (l % LANES) % 6
    fit = l % LANES < 96
    sel2 = ((fit & (s < 3) & (j == WIN * m - 1)) | (fit & (s >= 3) & (j == WIN * m + WIN))).astype(BF)
    l, j = np.indices((LANES, 2 * LANES))
    hit = np.zeros((LANES, 2 * LANES), bool)
    for n, c in enumerate((0, 1, 2 * LANES - 2, 2 * LANES - 1)):
        hit = hit | ((l // 3 == n) & (j == c))
    return sel1, sel2, selx, hit.astype(BF)


def refine(mask, queries, slab, tables):
    vmem = pl.BlockSpec(memory_space=pltpu.VMEM)
    hbm = pl.BlockSpec(memory_space=pltpu.HBM)
    arrays = (queries,) + tables
    return pl.pallas_call(
        refine_body,
        out_shape=(
            jax.ShapeDtypeStruct((ROWS, COLS), BF),
            jax.ShapeDtypeStruct((ROWS, LANES), F),
            jax.ShapeDtypeStruct((2, ROWS, LANES), F),
        ),
        in_specs=[pl.BlockSpec(memory_space=pltpu.SMEM), vmem] + [hbm] * len(arrays),
        out_specs=(vmem, vmem, vmem),
        scratch_shapes=[
            pltpu.VMEM((BLOCKS, ROWS, LANES), F),
            pltpu.VMEM((2, ROWS, LANES), F),
            pltpu.VMEM((4 * ROWS * BPI, 2 * LANES), BF),
            pltpu.VMEM((4 * ROWS * BPI, WIN * 32), BF),
            pltpu.VMEM((BLOCKS, ROWS, LANES), F),
            pltpu.VMEM((2, ROWS, LANES), F),
        ]
        + [pltpu.VMEM(array.shape, BF) for array in arrays]
        + [pltpu.SemaphoreType.DMA((len(arrays),))],
        compiler_params=pltpu.CompilerParams(vmem_limit_bytes=36 * 1024 * 1024),
        cost_estimate=pl.CostEstimate(flops=9_400_000_000, bytes_accessed=8_000_000, transcendentals=0),
        name="refine",
    )(mask, slab, *arrays)


def sides(ends, queries, left, right, own, part, tables, out):
    vmem = pl.BlockSpec(memory_space=pltpu.VMEM)
    any_space = pl.BlockSpec(memory_space=pl.ANY)
    return pl.pallas_call(
        sides_body,
        out_shape=jax.ShapeDtypeStruct((ROWS, COLS), BF),
        in_specs=[pl.BlockSpec(memory_space=pltpu.SMEM)] + [vmem] * 9 + [any_space],
        out_specs=any_space,
        scratch_shapes=[pltpu.VMEM((2, ROWS, LANES), BF), pltpu.SemaphoreType.DMA((2,))],
        input_output_aliases={10: 0},
        compiler_params=pltpu.CompilerParams(vmem_limit_bytes=8 * 1024 * 1024),
        cost_estimate=pl.CostEstimate(flops=60_000_000, bytes_accessed=1_500_000, transcendentals=0),
        name="sides",
    )(ends, queries, left, right, own, part, *tables, out)


def pack_body(me_ref, time_ref, panels_ref, out_ref, sems):
    me = me_ref[0]
    first = me - lax.rem(me, 2)
    jobs = []
    for i in range(2 * BLOCKS):
        owner = time_ref[first * BLOCKS + i] // BLOCKS
        slot = owner - lax.rem(owner, 2) + i // BLOCKS
        copy = pltpu.make_async_copy(panels_ref.at[i], out_ref.at[slot], sems.at[i])
        jobs.append((lax.rem(owner, 2) == lax.rem(me, 2), copy))
    for wanted, copy in jobs:
        pl.when(wanted)(copy.start)
    for wanted, copy in jobs:
        pl.when(wanted)(copy.wait)


def pack(me, panel_time, panels, owners):
    any_space = pl.BlockSpec(memory_space=pl.ANY)
    smem = pl.BlockSpec(memory_space=pltpu.SMEM)
    return pl.pallas_call(
        pack_body,
        out_shape=jax.ShapeDtypeStruct((owners,) + panels.shape[1:], BF),
        in_specs=[smem, smem, any_space],
        out_specs=any_space,
        scratch_shapes=[pltpu.SemaphoreType.DMA((2 * BLOCKS,))],
        compiler_params=pltpu.CompilerParams(vmem_limit_bytes=4 * 1024 * 1024),
        cost_estimate=pl.CostEstimate(flops=0, bytes_accessed=600_000, transcendentals=0),
        name="pack",
    )(me, panel_time, panels)


def place_body(source_ref, incoming_ref, *rest):
    out_ref, held, in_sems, out_sems = rest[-4:]
    gets = [
        pltpu.make_async_copy(incoming_ref.at[source_ref[k]], held.at[k], in_sems.at[k]) for k in range(BLOCKS)
    ]
    for copy in gets:
        copy.start()
    for copy in gets:
        copy.wait()
    puts = [pltpu.make_async_copy(held, out_ref.at[d], out_sems.at[d]) for d in range(out_ref.shape[0])]
    for copy in puts:
        copy.start()
    for copy in puts:
        copy.wait()


def place(source, incoming, copies, ready):
    any_space = pl.BlockSpec(memory_space=pl.ANY)
    piece = incoming.shape[1:]
    return pl.pallas_call(
        place_body,
        out_shape=jax.ShapeDtypeStruct((copies, BLOCKS) + piece, BF),
        in_specs=[pl.BlockSpec(memory_space=pltpu.SMEM)] + [any_space] * (1 + len(ready)),
        out_specs=any_space,
        scratch_shapes=[
            pltpu.VMEM((BLOCKS,) + piece, BF),
            pltpu.SemaphoreType.DMA((BLOCKS,)),
            pltpu.SemaphoreType.DMA((copies,)),
        ],
        compiler_params=pltpu.CompilerParams(vmem_limit_bytes=4 * 1024 * 1024),
        cost_estimate=pl.CostEstimate(flops=0, bytes_accessed=2_400_000, transcendentals=0),
        name="place",
    )(source, incoming, *ready)


def shards(queries, ref_panels, cand_mask, panel_time, w_first, b_first, w_second):
    owners = lax.axis_size("ref")
    fan = lax.axis_size("qry")
    me = lax.axis_index("ref")
    up = [(i, i + 1) for i in range(owners - 1)]
    down = [(i + 1, i) for i in range(owners - 1)]
    pairs = [[2 * z, 2 * z + 1] for z in range(owners // 2)]
    lines = [[2 * z + c for z in range(owners // 2)] for c in range(2)]
    chip = lax.all_gather(ref_panels, "ref", axis=0, tiled=True, axis_index_groups=pairs)
    packed = pack(me[None], panel_time, chip, owners)
    incoming = lax.all_to_all(packed, "ref", 0, 0, tiled=True, axis_index_groups=lines)

    holder = jnp.arange(owners * BLOCKS, dtype=I) // BLOCKS
    mine = panel_time[None, :] == me * BLOCKS + jnp.arange(BLOCKS, dtype=I)[:, None]
    source = jnp.sum(jnp.where(mine, holder[None, :], 0), axis=1)
    ends = jnp.stack([(me > 0).astype(I), (me < owners - 1).astype(I)])
    w1, w2, w1x, w2x = weights(w_first, b_first, w_second)
    sel1, sel2, selx, sel3 = selectors()

    marks = [
        jnp.broadcast_to(cand_mask[:, c : c + 1].astype(BF)[None], (3, 2, queries.shape[1])).reshape(6, -1)
        for c in (0, BLOCKS - 1)
    ]
    ready = (w1, w2, w1x, w2x, ends) + tuple(marks)
    slab = lax.all_to_all(place(source, incoming, fan, ready), "qry", 0, 0, tiled=True)
    head = jnp.concatenate([slab[0, 0, 0:2], marks[0]])
    tail = jnp.concatenate([slab[fan - 1, BLOCKS - 1, 6:8], marks[1]])
    from_left = lax.ppermute(tail, "ref", up)
    from_right = lax.ppermute(head, "ref", down)
    out, own, part = refine(cand_mask, queries, slab, (sel1, w1, w2, sel2))
    return sides(ends, queries, from_left, from_right, own, part, (w1x, w2x, selx, sel3), out)


def solution(mesh):
    placed = (P("qry", None), P("ref", "qry", None), P("qry", "ref"), P(), P(), P(), P())
    return jax.shard_map(
        shards, mesh=mesh, in_specs=placed, out_specs=P("qry", "ref"), check_vma=False
    )
```

time: 404 us -> 109 us (0.27); the launches traced: 399 us -> 109 us
  matrix products: 127 us -> 0 us
  waiting for transfers between devices: 86.9 us -> 11 us
  other arithmetic: 78.1 us -> 8.82 us
  local copies, waits for them, and re-layouts: 56.3 us -> 3.47 us
  blocking collectives: 0 us -> 36.1 us
  Pallas kernels: 0 us -> 21.9 us
  between operations: 13.6 us -> 0.74 us
  loops' own time: 8.92 us -> 0 us
    dot_general x39 -> x0, matrix products: 127 us -> none  [the longest x36 120 us: layer_two(): jnp.einsum('c,chw->hw', w_second[3 * row_shift + col_shift], padded[:, ro...]
    convert_element_type x12 -> x6, other arithmetic: 63.5 us -> 8.29 us  [the longest x1 4.4 us: weights(): w2 = total.astype(BF)]
    all_gather x1 -> x0, waiting for transfers between devices: 49.9 us -> none  [shards(): lax.all_gather(owned, 'qry', axis=1, tiled=True)]
    all_to_all x0 -> x1, blocking collectives: none -> 27.3 us  [shards(): lax.all_to_all(place(source, incoming, fan, ready), 'qry', 0, 0, tiled=True)]
    mul x46 -> x0, local copies, waits for them, and re-layouts: 24.9 us -> none  [the longest x44 24.6 us: layer_one(): w_first[3 * row_shift + col_shift][:, None, None]]
    all_to_all x1, waiting for transfers between devices: 33.4 us -> 11 us  [shards(): lax.all_to_all(packed, 'ref', 0, 0, tiled=True, axis_index_groups=lines)]
    pallas_call x0 -> x4, Pallas kernels: none -> 21.9 us  [the longest x1 14.5 us: refine(): pl.pallas_call(refine_body, out_shape=(jax.ShapeDtypeStruct((ROWS, COLS),...]
    while x20 -> x0, local copies, waits for them, and re-layouts: 12.8 us -> none
  transfers between devices with their start and end apart: 6 -> 3, of which waited for: 3 -> 1; matrix products, arithmetic and copies ran while one was open for 1% -> 10% of each run, Pallas kernels for 0% -> 13%
where the time goes in v1:
time: 109 us
  blocking collectives  36.1 us (33%)
  starting transfers between devices  26.5 us (24%)
  Pallas kernels  21.9 us (20%)
  waiting for transfers between devices  11 us (10%)
  other arithmetic  8.82 us (8%)
  local copies, waits for them, and re-layouts  3.47 us (3%)
    all_to_all x1, blocking collectives, shards(): lax.all_to_all(place(source, incoming, fan, ready), 'qry', 0, 0, tiled=True)  27.3 us
    ppermute x1, starting transfers between devices, shards(): from_left = lax.ppermute(tail, 'ref', up)  14.8 us
    pallas_call x1, Pallas kernels, refine(): pl.pallas_call(refine_body, out_shape=(jax.ShapeDtypeStruct((ROWS, COLS),...  14.5 us
    all_to_all x1, waiting for transfers between devices, shards(): lax.all_to_all(packed, 'ref', 0, 0, tiled=True, axis_index_groups=lines)  11 us
    all_to_all x1, starting transfers between devices, shards(): lax.all_to_all(packed, 'ref', 0, 0, tiled=True, axis_index_groups=lines)  9.57 us
    all_gather x1, blocking collectives, shards(): lax.all_gather(ref_panels, 'ref', axis=0, tiled=True, axis_index_groups=p...  8.83 us
    convert_element_type x1, other arithmetic, weights(): w2 = total.astype(BF)  4.4 us
    pallas_call x1, Pallas kernels, place(): pl.pallas_call(place_body, out_shape=jax.ShapeDtypeStruct((copies, BLOCKS...  3.67 us
  transfers between devices with their start and end apart: 3, of which 1 were waited for; matrix products, arithmetic and copies ran while one was open for 10% of the time, Pallas kernels for 13%

profile of v1, /device:TPU:1, one launch (start us, length us, event | category | flops | bytes accessed | tf_op | source)
XLA Modules:
  0.0 108.5 jit_solution(10075483002018390706)
XLA Ops:
  0.0 8.8 %all_gather.3.panels_ref = bf16[16,8,1024]{2,1,0:T(8,128)(2,1)S(1)} all-gather(bf16[8,8,1024]{2,1,0:T(8,128)(2,1)} %param.12), channel_id=1, replica_groups={{0,16},{32,48},{64,80},{96,112},{128,144},{160,176},{192,208},{224,240}..., dimensions={0}, use_global_device_ids=true | all-gather | bytes 393216 | tf_op jit(solution)/shard_map/all_gather | solution.py:421
  8.9 0.7 copy-done.3
  9.6 1.4 %pack.1 = bf16[32,8,1024]{2,1,0:T(8,128)(2,1)} custom-call(s32[1]{0:T(128)} %bitcast.2.me_ref, s32[256]{0:T(256)S(1)} %copy-done.3, bf16[16,8,1024]{2,1,0:T(8,128)(2,1)S(1)} %all_gather.3.panels_ref), custom_call_target="tpu_custom_call" | custom-call | bytes 600000 | tf_op jit(solution)/shard_map/pack/pallas_call | solution.py:366
  11.1 9.6 %all-to-all-start = ((bf16[32,8,1024]{2,1,0:T(8,128)(2,1)}), bf16[32,8,1024]{2,1,0:T(8,128)(2,1)S(1)}, u32[]{:S(2)}, u32[]{:S(2)}) async-start(bf16[32,8,1024]{2,1,0:T(8,128)(2,1)} %pack.1), calls=%async_computation | async-start | bytes 1048576 | tf_op jit(solution)/shard_map/all_to_all | solution.py:423
  21.1 0.1 concatenate.16
  21.3 0.2 tile.147
  21.5 0.2 slice_reduce_fusion.1
  21.7 0.1 broadcast_in_dim.609
  21.8 0.1 broadcast_in_dim.613
  23.5 0.1 tile.145
  23.7 0.2 select_reduce_fusion.source_ref
  23.9 1.3 %add_convert_fusion.1 = bf16[128,1024]{1,0:T(8,128)(2,1)S(1)} fusion(f32[1024]{0:T(1024)S(1)} %tile.143, f32[1024]{0:T(1024)S(1)} %tile.141, f32[1024]{0:T(1024)S(1)} %tile.139, f32[1024]{0:T(1024)S(1)} %tile.137, f32[1024]{0:T(1024)S(1)} %tile.135, f32[1024]{0:T(1024)S(1)} %tile.133, f32[1024]{0:T(1024)S(1)} %tile.131, f32[1024]{0:T(1024)S(1)} %tile.129, ...), kind=kLoop, calls=%fused_computation.78 | loop fusion | flops 6815744 | bytes 311296 | tf_op jit(solution)/shard_map/convert_element_type | solution.py:230
  25.2 1.3 %add_convert_fusion.2 = bf16[128,1024]{1,0:T(8,128)(2,1)S(1)} fusion(f32[1024]{0:T(1024)S(1)} %tile.125, f32[1024]{0:T(1024)S(1)} %tile.123, f32[1024]{0:T(1024)S(1)} %tile.121, f32[1024]{0:T(1024)S(1)} %tile.119, f32[1024]{0:T(1024)S(1)} %tile.117, f32[1024]{0:T(1024)S(1)} %tile.115, f32[1024]{0:T(1024)S(1)} %tile.113, f32[1024]{0:T(1024)S(1)} %tile.111, ...), kind=kLoop, calls=%fused_computation.79 | loop fusion | flops 7602176 | bytes 323968 | tf_op jit(solution)/shard_map/convert_element_type | solution.py:230
  26.6 0.5 add_convert_fusion.4
  27.1 0.5 add_convert_fusion.5
  27.6 0.3 add_convert_fusion.3.rest_3_.w2x_ref
  28.0 4.4 %add_convert_fusion.rest_1_.w2_hbm = bf16[1024,512]{1,0:T(8,128)(2,1)S(1)} fusion(f32[1024]{0:T(1024)S(1)} %bitcast.122, f32[1024]{0:T(1024)S(1)} %bitcast.123, f32[1024]{0:T(1024)S(1)} %bitcast.124, f32[1024]{0:T(1024)S(1)} %bitcast.125, f32[1024]{0:T(1024)S(1)} %bitcast.126, f32[1024]{0:T(1024)S(1)} %bitcast.127, f32[1024]{0:T(1024)S(1)} %bitcast.128, ...), kind=kLoop, calls=%fused_computation.36 | loop fusion | flops 49283072 | bytes 1108480 | tf_op jit(solution)/shard_map/convert_element_type | solution.py:246
  32.4 11.0 %all-to-all-done.incoming_ref = bf16[32,8,1024]{2,1,0:T(8,128)(2,1)S(1)} async-done(((bf16[32,8,1024]{2,1,0:T(8,128)(2,1)}), bf16[32,8,1024]{2,1,0:T(8,128)(2,1)S(1)}, u32[]{:S(2)}, u32[]{:S(2)}) %all-to-all-start) | async-done | bytes 524320 | tf_op jit(solution)/shard_map/all_to_all | solution.py:423
  43.5 3.7 %place.1 = bf16[16,8,8,1024]{3,2,1,0:T(8,128)(2,1)S(1)} custom-call(s32[8]{0:T(128)S(1)} %select_reduce_fusion.source_ref, bf16[32,8,1024]{2,1,0:T(8,128)(2,1)S(1)} %all-to-all-done.incoming_ref, bf16[256,1024]{1,0:T(8,128)(2,1)S(1)} %pad_maximum_fusion.rest_0_.w1_hbm, bf16[1024,512]{1,0:T(8,128)(2,1)S(1)} %add_convert_fusion.rest_1_.w2_hbm, ...), custom_call_target="tpu_custom_call" | custom-call | bytes 2400000 | tf_op jit(solution)/shard_map/place/pallas_call | solution.py:397
  47.2 27.3 %all_to_all.10.slab_ref = bf16[16,8,8,1024]{3,2,1,0:T(8,128)(2,1)S(1)} all-to-all(bf16[16,8,8,1024]{3,2,1,0:T(8,128)(2,1)S(1)} %place.1), channel_id=1, replica_groups=mesh['ref'=32,'qry'=16] {'qry'}, dimensions={0} | all-to-all | bytes 4194304 | tf_op jit(solution)/shard_map/all_to_all | solution.py:437
  74.6 14.8 %collective-permute-start = (bf16[8,1024]{1,0:T(8,128)(2,1)S(1)}, bf16[8,1024]{1,0:T(8,128)(2,1)S(1)}, u32[]{:S(2)}, u32[]{:S(2)}) collective-permute-start(bf16[8,1024]{1,0:T(8,128)(2,1)S(1)} %pad_maximum_fusion.2), channel_id=1, source_target_pairs={{0,16},{16,32},{32,48},{48,64},{64,80},{80,96},{96,112},{112,128},... | collective-permute-start | bytes 49160 | tf_op jit(solution)/shard_map/ppermute | solution.py:440
  89.4 2.1 %collective-permute-start.1 = (bf16[8,1024]{1,0:T(8,128)(2,1)S(1)}, bf16[8,1024]{1,0:T(8,128)(2,1)S(1)}, u32[]{:S(2)}, u32[]{:S(2)}) collective-permute-start(bf16[8,1024]{1,0:T(8,128)(2,1)S(1)} %pad_maximum_fusion.3), channel_id=1, source_target_pairs={{16,0},{32,16},{48,32},{64,48},{80,64},{96,80},{112,96},{128,112},... | collective-permute-start | bytes 49160 | tf_op jit(solution)/shard_map/ppermute | solution.py:441
  91.5 14.5 %refine.1 = (bf16[256,1024]{1,0:T(8,128)(2,1)}, f32[256,128]{1,0:T(8,128)S(1)}, f32[2,256,128]{2,1,0:T(8,128)S(1)}) custom-call(s32[2,8]{1,0:T(2,128)S(1)} %copy-done.5, bf16[16,8,8,1024]{3,2,1,0:T(8,128)(2,1)S(1)} %all_to_all.10.slab_ref, bf16[256,1024]{1,0:T(8,128)(2,1)S(1)} %copy-done, bf16[1024,256]{1,0:T(8,128)(2,1)S(1)} %copy-done.7, ...), custom_call_target="tpu_custom_call" | custom-call | flops 9400000512 | bytes 8000000 | tf_op jit(solution)/shard_map/refine/pallas_call | solution.py:307
  106.0 2.4 %sides.1 = bf16[256,1024]{1,0:T(8,128)(2,1)} custom-call(s32[2]{0:T(128)S(1)} %add_convert_fusion.6.rest_4_.ends_ref, bf16[256,1024]{1,0:T(8,128)(2,1)S(1)} %copy-done, bf16[8,1024]{1,0:T(8,128)(2,1)S(1)} %collective-permute-done.left_ref, bf16[8,1024]{1,0:T(8,128)(2,1)S(1)} %collective-permute-done.1.right_ref, ...), custom_call_target="tpu_custom_call", output_to_operand_aliasing={{}: (10, {})} | custom-call | flops 60000000 | bytes 1500000 | tf_op jit(solution)/shard_map/sides/pallas_call | solution.py:335
  (118 shorter events, 2.3 us)
Async XLA Ops:
  0.0 21.0 %copy-start.10 = (f32[32]{0:T(128)S(1)}, f32[32]{0:T(128)}, u32[]{:S(2)}) copy-start(f32[32]{0:T(128)} %param.16) | copy-start | bytes 388
  0.0 21.0 %copy-start.8 = (f32[9,32]{1,0:T(8,128)S(1)}, f32[9,32]{1,0:T(8,128)}, u32[]{:S(2)}) copy-start(f32[9,32]{1,0:T(8,128)} %param.15) | copy-start | bytes 3460
  0.0 21.5 %copy-start.5 = (s32[2,8]{1,0:T(2,128)S(1)}, s32[2,8]{1,0:T(2,128)}, u32[]{:S(2)}) copy-start(s32[2,8]{1,0:T(2,128)} %mask_ref.1) | copy-start | bytes 196
  0.0 21.9 %copy-start.9 = (bf16[9,32]{1,0:T(8,128)(2,1)S(1)}, bf16[9,32]{1,0:T(8,128)(2,1)}, u32[]{:S(2)}) copy-start(bf16[9,32]{1,0:T(8,128)(2,1)} %param.17) | copy-start | bytes 1732
  8.9 14.9 %copy-start.4 = (s32[256]{0:T(256)S(1)}, s32[256]{0:T(256)}, u32[]{:S(2)}) copy-start(s32[256]{0:T(256)} %time_ref.1) | copy-start | bytes 3076
  8.9 0.8 copy-start.3
  11.1 32.3 %all-to-all-start = ((bf16[32,8,1024]{2,1,0:T(8,128)(2,1)}), bf16[32,8,1024]{2,1,0:T(8,128)(2,1)S(1)}, u32[]{:S(2)}, u32[]{:S(2)}) async-start(bf16[32,8,1024]{2,1,0:T(8,128)(2,1)} %pack.1), calls=%async_computation | async-start | bytes 1048576 | tf_op jit(solution)/shard_map/all_to_all | solution.py:423
  47.2 44.3 %copy-start = (bf16[256,1024]{1,0:T(8,128)(2,1)S(1)}, bf16[256,1024]{1,0:T(8,128)(2,1)}, u32[]{:S(2)}) copy-start(bf16[256,1024]{1,0:T(8,128)(2,1)} %q_ref.1) | copy-start | bytes 1572868
  47.2 44.3 %copy-start.6 = (bf16[256,1024]{1,0:T(8,128)(2,1)S(1)}, bf16[256,1024]{1,0:T(8,128)(2,1)}, u32[]{:S(2)}) copy-start(bf16[256,1024]{1,0:T(8,128)(2,1)} %constant.438.clone.sel2_hbm) | copy-start | bytes 1572868
  47.2 44.3 %copy-start.7 = (bf16[1024,256]{1,0:T(8,128)(2,1)S(1)}, bf16[1024,256]{1,0:T(8,128)(2,1)}, u32[]{:S(2)}) copy-start(bf16[1024,256]{1,0:T(8,128)(2,1)} %constant.437.clone.sel1_hbm) | copy-start | bytes 1572868
  74.5 31.5 %copy-start.1 = (bf16[128,256]{1,0:T(8,128)(2,1)S(1)}, bf16[128,256]{1,0:T(8,128)(2,1)}, u32[]{:S(2)}) copy-start(bf16[128,256]{1,0:T(8,128)(2,1)} %constant.440.clone.sel3_ref) | copy-start | bytes 196612
  74.5 31.5 %copy-start.2 = (bf16[16,128]{1,0:T(8,128)(2,1)S(1)}, bf16[16,128]{1,0:T(8,128)(2,1)}, u32[]{:S(2)}) copy-start(bf16[16,128]{1,0:T(8,128)(2,1)} %constant.439.clone.selx_ref) | copy-start | bytes 12292
  74.6 31.4 %collective-permute-start = (bf16[8,1024]{1,0:T(8,128)(2,1)S(1)}, bf16[8,1024]{1,0:T(8,128)(2,1)S(1)}, u32[]{:S(2)}, u32[]{:S(2)}) collective-permute-start(bf16[8,1024]{1,0:T(8,128)(2,1)S(1)} %pad_maximum_fusion.2), channel_id=1, source_target_pairs={{0,16},{16,32},{32,48},{48,64},{64,80},{80,96},{96,112},{112,128},... | collective-permute-start | bytes 49160 | tf_op jit(solution)/shard_map/ppermute | solution.py:440
  89.4 16.6 %collective-permute-start.1 = (bf16[8,1024]{1,0:T(8,128)(2,1)S(1)}, bf16[8,1024]{1,0:T(8,128)(2,1)S(1)}, u32[]{:S(2)}, u32[]{:S(2)}) collective-permute-start(bf16[8,1024]{1,0:T(8,128)(2,1)S(1)} %pad_maximum_fusion.3), channel_id=1, source_target_pairs={{16,0},{32,16},{48,32},{64,48},{80,64},{96,80},{112,96},{128,112},... | collective-permute-start | bytes 49160 | tf_op jit(solution)/shard_map/ppermute | solution.py:441

commit v2 on v1

--- a/solution.py
+++ b/solution.py
@@ -40,56 +40,50 @@
 
 
 def refine_body(
-    mask_ref, slab_ref, q_hbm, sel1_hbm, w1_hbm, w2_hbm, sel2_hbm,
-    out_ref, own_ref, part_ref, sims, gg, xs, hs, acc, ee, q_ref, sel1_ref, w1_ref, w2_ref, sel2_ref, sems,
+    mask_ref, score_ref, sel1_hbm, w1_hbm, w2_hbm, sel2_hbm,
+    out_ref, own_ref, part_ref, sims, gg, xs, hs, acc, ee, sel1_ref, w1_ref, w2_ref, sel2_ref, sems,
 ):
     loads = [
         pltpu.make_async_copy(src, dst, sems.at[n])
         for n, (src, dst) in enumerate(
-            zip((q_hbm, sel1_hbm, w1_hbm, w2_hbm, sel2_hbm), (q_ref, sel1_ref, w1_ref, w2_ref, sel2_ref))
+            zip((sel1_hbm, w1_hbm, w2_hbm, sel2_hbm), (sel1_ref, w1_ref, w2_ref, sel2_ref))
         )
     ]
     for load in loads:
         load.start()
-    loads[0].wait()
-    loads[1].wait()
     lane = lax.broadcasted_iota(I, (ROWS, LANES), 1)
     top = lax.broadcasted_iota(I, (ROWS, LANES), 0) < ROWS // 2
-    q = q_ref[...]
+    keep = []
+    for half in range(2):
+        rows = [quarters(lane, [mask_ref[r, 4 * half + j] for j in range(4)]) for r in range(2)]
+        keep.append(jnp.where(top, rows[0], rows[1]).astype(F))
+    loads[0].wait()
     g0 = jnp.zeros((ROWS, 2 * LANES), F)
-    for t in range(0, BLOCKS, 2):
-        slab = slab_ref[:, t : t + 2].swapaxes(0, 1).reshape(2 * LANES, q.shape[1])
-        s = lax.dot_general(q, slab, NT, preferred_element_type=F)
-        for u in range(2):
-            keep = jnp.where(top, mask_ref[0, t + u], mask_ref[1, t + u]).astype(F)
-            v = s[:, LANES * u : LANES * (u + 1)].astype(BF).astype(F) * keep
-            sims[t + u] = v
-            g0 = g0 + jnp.dot(
-                v.astype(BF), sel1_ref[LANES * (t + u) : LANES * (t + u + 1), :], preferred_element_type=F
-            )
+    for n in range(BLOCKS):
+        half = n % 2
+        v = score_ref[n // 2, :, LANES * half : LANES * (half + 1)].astype(F) * keep[half]
+        sims[n] = v
+        g0 = g0 + jnp.dot(v.astype(BF), sel1_ref[LANES * n : LANES * (n + 1), :], preferred_element_type=F)
     own_ref[...] = g0[:, :LANES]
     g = g0 + pltpu.roll(from_above(g0), 2 * LANES - 1, 1) + pltpu.roll(from_below(g0), 1, 1)
     gg[0] = g[:, :LANES]
     gg[1] = g[:, LANES:]
-    ee[...] = jnp.zeros((2, ROWS, LANES), F)
     group = ROWS * BPI
-    for load in loads[2:]:
+    for load in loads[1:]:
         load.wait()
 
     def step(it, carry):
-        for b in range(BPI):
-            k = it * BPI + b
-            s = sims[k]
+        ge = gg[it]
+        for w in range(4):
+            s = sims[2 * w + it]
             up = from_above(s)
             dn = from_below(s)
-            ge = gg[k // 4]
-            base = lax.rem(k, 4) * 24
-            for w in range(4):
-                e = pltpu.roll(ge, lax.rem(96 - 6 * w + LANES - base, LANES), 1)
+            for b in range(BPI):
+                e = pltpu.roll(ge, (96 - 6 * (4 * b + w)) % LANES, 1)
                 parts = (
-                    pltpu.roll(up, (LANES - WIN * w) % LANES, 1) if w else up,
-                    pltpu.roll(s, (LANES + WIN - WIN * w) % LANES, 1) if w != 1 else s,
-                    pltpu.roll(dn, (LANES + 2 * WIN - WIN * w) % LANES, 1) if w != 2 else dn,
+                    pltpu.roll(up, (LANES - WIN * b) % LANES, 1) if b else up,
+                    pltpu.roll(s, (LANES + WIN - WIN * b) % LANES, 1) if b != 1 else s,
+                    pltpu.roll(dn, (LANES + 2 * WIN - WIN * b) % LANES, 1) if b != 2 else dn,
                     jnp.where(lane < 102, e, 1.0),
                 )
                 x = quarters(lane, parts).astype(BF)
@@ -115,6 +109,7 @@
             )
             for w in range(4)
         ]
+        tot = jnp.zeros((ROWS, LANES), F)
         for b in range(BPI):
             k = it * BPI + b
             pb = [p[w][ROWS * b : ROWS * (b + 1)] for w in range(4)]
@@ -122,12 +117,11 @@
             a1 = pltpu.roll(quarters(lane, [pb[3], pb[0], pb[1], pb[2]]), LANES - WIN, 1)
             a2 = pltpu.roll(quarters(lane, [pb[2], pb[3], pb[0], pb[1]]), LANES - 2 * WIN, 1)
             acc[k] = a1 + from_above(a0) + from_below(a2)
-            base = lax.rem(k, 4) * 24
-            tot = ee[k // 4]
             for w in range(4):
-                moved = pltpu.roll(pb[w], lax.rem(base + 6 * w + LANES - WIN * ((w + 3) % 4), LANES), 1)
-                tot = jnp.where((lane >= base + 6 * w) & (lane < base + 6 * w + 6), moved, tot)
-            ee[k // 4] = tot
+                at = 6 * (4 * b + w)
+                moved = pltpu.roll(pb[w], (at + LANES - WIN * ((w + 3) % 4)) % LANES, 1)
+                tot = jnp.where((lane >= at) & (lane < at + 6), moved, tot)
+        ee[it] = tot
         return carry
 
     lax.fori_loop(0, BLOCKS // BPI, step, 0)
@@ -159,21 +153,13 @@
 
 
 def sides_body(
-    ends_ref, q_ref, left_ref, right_ref, own_ref, part_ref, w1x_ref, w2x_ref, selx_ref, sel3_ref, old_ref,
+    ends_ref, left_ref, right_ref, own_ref, part_ref, w1x_ref, w2x_ref, selx_ref, sel3_ref, old_ref,
     out_ref, held, sems,
 ):
     del old_ref
     lane = lax.broadcasted_iota(I, (ROWS, LANES), 1)
-    edge = jnp.concatenate([left_ref[...], right_ref[...]], axis=0)
-    se = lax.dot_general(q_ref[...], edge, NT, preferred_element_type=F).astype(BF).astype(F)
-    top = lax.broadcasted_iota(I, (ROWS, 16), 0) < ROWS // 2
-    left = lax.broadcasted_iota(I, (ROWS, 16), 1) < 8
-    bits = edge.astype(F)
-    keep = jnp.where(
-        top, jnp.where(left, bits[2:3, 0:1], bits[10:11, 0:1]), jnp.where(left, bits[3:4, 0:1], bits[11:12, 0:1])
-    )
-    g0 = jnp.where(lane >= 96, own_ref[...], 0.0)
-    g0 = g0 + jnp.dot((se * keep).astype(BF), selx_ref[...], preferred_element_type=F)
+    near = jnp.concatenate([left_ref[...], right_ref[...]], axis=1)
+    g0 = jnp.where(lane >= 96, own_ref[...], 0.0) + jnp.dot(near, selx_ref[...], preferred_element_type=F)
     g = g0 + pltpu.roll(from_above(g0), LANES - 1, 1) + pltpu.roll(from_below(g0), 1, 1)
     xw = jnp.where((lane >= 120) & (lane < 123), 1.0, g).astype(BF)
     hx = jnp.dot(xw, w1x_ref[0:LANES, :], preferred_element_type=F)
@@ -278,15 +264,16 @@
 
 def selectors():
     i, l = np.indices((COLS, 2 * LANES))
+    i = i % WIN + WIN * (i // (BLOCKS * WIN)) + LANES * (i // WIN % BLOCKS)
     m, s = 16 * (l // LANES) + (l % LANES) // 6, (l % LANES) % 6
     fit = l % LANES < 96
     hit = (fit & (s == 1) & (i == WIN * m - 1)) | (fit & (s == 4) & (i == WIN * m + WIN))
     for c in (0, 1, COLS - 2, COLS - 1):
         hit = hit | ((l == SIDE_LANE[c]) & (i == c))
     sel1 = hit.astype(BF)
-    i, l = np.indices((16, LANES))
-    hit = np.zeros((16, LANES), bool)
-    for row, c in ((0, -2), (1, -1), (8, COLS), (9, COLS + 1)):
+    i, l = np.indices((2 * LANES, LANES))
+    hit = np.zeros((2 * LANES, LANES), bool)
+    for row, c in ((LANES - 2, -2), (LANES - 1, -1), (LANES, COLS), (LANES + 1, COLS + 1)):
         hit = hit | ((i == row) & (l == SIDE_LANE[c]))
     selx = hit.astype(BF)
     l, j = np.indices((2 * LANES, COLS))
@@ -300,10 +287,10 @@
     return sel1, sel2, selx, hit.astype(BF)
 
 
-def refine(mask, queries, slab, tables):
+def refine(mask, scores, tables):
     vmem = pl.BlockSpec(memory_space=pltpu.VMEM)
     hbm = pl.BlockSpec(memory_space=pltpu.HBM)
-    arrays = (queries,) + tables
+    arrays = tables
     return pl.pallas_call(
         refine_body,
         out_shape=(
@@ -326,26 +313,48 @@
         compiler_params=pltpu.CompilerParams(vmem_limit_bytes=36 * 1024 * 1024),
         cost_estimate=pl.CostEstimate(flops=9_400_000_000, bytes_accessed=8_000_000, transcendentals=0),
         name="refine",
-    )(mask, slab, *arrays)
-
-
-def sides(ends, queries, left, right, own, part, tables, out):
+    )(mask, scores, *arrays)
+
+
+def sides(ends, left, right, own, part, tables, out):
     vmem = pl.BlockSpec(memory_space=pltpu.VMEM)
     any_space = pl.BlockSpec(memory_space=pl.ANY)
     return pl.pallas_call(
         sides_body,
         out_shape=jax.ShapeDtypeStruct((ROWS, COLS), BF),
-        in_specs=[pl.BlockSpec(memory_space=pltpu.SMEM)] + [vmem] * 9 + [any_space],
+        in_specs=[pl.BlockSpec(memory_space=pltpu.SMEM)] + [vmem] * 8 + [any_space],
         out_specs=any_space,
         scratch_shapes=[pltpu.VMEM((2, ROWS, LANES), BF), pltpu.SemaphoreType.DMA((2,))],
-        input_output_aliases={10: 0},
+        input_output_aliases={9: 0},
         compiler_params=pltpu.CompilerParams(vmem_limit_bytes=8 * 1024 * 1024),
         cost_estimate=pl.CostEstimate(flops=60_000_000, bytes_accessed=1_500_000, transcendentals=0),
         name="sides",
-    )(ends, queries, left, right, own, part, *tables, out)
-
-
-def pack_body(me_ref, time_ref, panels_ref, out_ref, sems):
+    )(ends, left, right, own, part, *tables, out)
+
+
+def score_body(seat_ref, slab_ref, *rest):
+    q_refs, out_ref = rest[:-1], rest[-1]
+    side = len(q_refs)
+    slab = slab_ref[...].swapaxes(0, 1).reshape(BLOCKS * WIN, slab_ref.shape[3])
+    for step, q_ref in enumerate(q_refs):
+        v = lax.rem(seat_ref[0] + side - step, side)
+        out_ref[v] = lax.dot_general(q_ref[...], slab, NT, preferred_element_type=F).astype(BF)
+
+
+def score(seat, slab, videos):
+    vmem = pl.BlockSpec(memory_space=pltpu.VMEM)
+    return pl.pallas_call(
+        score_body,
+        out_shape=jax.ShapeDtypeStruct((len(videos), ROWS, BLOCKS * WIN), BF),
+        in_specs=[pl.BlockSpec(memory_space=pltpu.SMEM), vmem] + [vmem] * len(videos),
+        out_specs=vmem,
+        compiler_params=pltpu.CompilerParams(vmem_limit_bytes=12 * 1024 * 1024),
+        cost_estimate=pl.CostEstimate(flops=540_000_000, bytes_accessed=3_100_000, transcendentals=0),
+        name="score",
+    )(seat, slab, *videos)
+
+
+def pack_body(me_ref, time_ref, panels_ref, out_ref, zero_ref, sems):
     me = me_ref[0]
     first = me - lax.rem(me, 2)
     jobs = []
@@ -356,6 +365,7 @@
         jobs.append((lax.rem(owner, 2) == lax.rem(me, 2), copy))
     for wanted, copy in jobs:
         pl.when(wanted)(copy.start)
+    zero_ref[...] = jnp.zeros(zero_ref.shape, F)
     for wanted, copy in jobs:
         pl.when(wanted)(copy.wait)
 
@@ -365,14 +375,35 @@
     smem = pl.BlockSpec(memory_space=pltpu.SMEM)
     return pl.pallas_call(
         pack_body,
-        out_shape=jax.ShapeDtypeStruct((owners,) + panels.shape[1:], BF),
+        out_shape=(
+            jax.ShapeDtypeStruct((owners,) + panels.shape[1:], BF),
+            jax.ShapeDtypeStruct((8, LANES), F),
+        ),
         in_specs=[smem, smem, any_space],
-        out_specs=any_space,
+        out_specs=(any_space, pl.BlockSpec(memory_space=pltpu.VMEM)),
         scratch_shapes=[pltpu.SemaphoreType.DMA((2 * BLOCKS,))],
         compiler_params=pltpu.CompilerParams(vmem_limit_bytes=4 * 1024 * 1024),
         cost_estimate=pl.CostEstimate(flops=0, bytes_accessed=600_000, transcendentals=0),
         name="pack",
     )(me, panel_time, panels)
+
+
+def share_body(q_ref, *rest):
+    out_ref = rest[-1]
+    out_ref[...] = q_ref[...]
+
+
+def share(queries, after):
+    vmem = pl.BlockSpec(memory_space=pltpu.VMEM)
+    return pl.pallas_call(
+        share_body,
+        out_shape=jax.ShapeDtypeStruct(queries.shape, BF),
+        in_specs=[vmem] + [pl.BlockSpec(memory_space=pl.ANY)] * len(after),
+        out_specs=vmem,
+        compiler_params=pltpu.CompilerParams(vmem_limit_bytes=4 * 1024 * 1024),
+        cost_estimate=pl.CostEstimate(flops=0, bytes_accessed=1_000_000, transcendentals=0),
+        name="share",
+    )(queries, *after)
 
 
 def place_body(source_ref, incoming_ref, *rest):
@@ -405,7 +436,7 @@
             pltpu.SemaphoreType.DMA((copies,)),
         ],
         compiler_params=pltpu.CompilerParams(vmem_limit_bytes=4 * 1024 * 1024),
-        cost_estimate=pl.CostEstimate(flops=0, bytes_accessed=2_400_000, transcendentals=0),
+        cost_estimate=pl.CostEstimate(flops=0, bytes_accessed=400_000_000, transcendentals=0),
         name="place",
     )(source, incoming, *ready)
 
@@ -418,10 +449,12 @@
     down = [(i + 1, i) for i in range(owners - 1)]
     pairs = [[2 * z, 2 * z + 1] for z in range(owners // 2)]
     lines = [[2 * z + c for z in range(owners // 2)] for c in range(2)]
+    side = LANES // WIN
+    outer = [[i + side * j for j in range(side)] for i in range(fan // side)]
+    inner = [[side * j + i for i in range(side)] for j in range(fan // side)]
     chip = lax.all_gather(ref_panels, "ref", axis=0, tiled=True, axis_index_groups=pairs)
-    packed = pack(me[None], panel_time, chip, owners)
+    packed, zero = pack(me[None], panel_time, chip, owners)
     incoming = lax.all_to_all(packed, "ref", 0, 0, tiled=True, axis_index_groups=lines)
-
     holder = jnp.arange(owners * BLOCKS, dtype=I) // BLOCKS
     mine = panel_time[None, :] == me * BLOCKS + jnp.arange(BLOCKS, dtype=I)[:, None]
     source = jnp.sum(jnp.where(mine, holder[None, :], 0), axis=1)
@@ -429,18 +462,27 @@
     w1, w2, w1x, w2x = weights(w_first, b_first, w_second)
     sel1, sel2, selx, sel3 = selectors()
 
-    marks = [
-        jnp.broadcast_to(cand_mask[:, c : c + 1].astype(BF)[None], (3, 2, queries.shape[1])).reshape(6, -1)
-        for c in (0, BLOCKS - 1)
+    shared = share(queries, (zero, w1, w2, w1x, w2x))
+    videos = [shared] + [
+        lax.ppermute(
+            shared, "qry", [(g[i], g[(i + step) % side]) for g in outer for i in range(side)]
+        )
+        for step in range(1, side)
     ]
-    ready = (w1, w2, w1x, w2x, ends) + tuple(marks)
-    slab = lax.all_to_all(place(source, incoming, fan, ready), "qry", 0, 0, tiled=True)
-    head = jnp.concatenate([slab[0, 0, 0:2], marks[0]])
-    tail = jnp.concatenate([slab[fan - 1, BLOCKS - 1, 6:8], marks[1]])
+    seat = lax.axis_index("qry") // (fan // side)
+
+    rows = [jnp.repeat(cand_mask[:, c].astype(BF), ROWS // 2)[:, None] for c in (0, BLOCKS - 1)]
+    ready = (w1, w2, w1x, w2x, ends) + tuple(rows)
+    slab = lax.all_to_all(
+        place(source, incoming, side, ready), "qry", 0, 0, tiled=True, axis_index_groups=inner
+    )
+    scores = lax.all_to_all(score(seat[None], slab, videos), "qry", 0, 0, tiled=True, axis_index_groups=outer)
+    head = scores[0, :, :LANES] * rows[0]
+    tail = scores[side - 1, :, LANES:] * rows[1]
     from_left = lax.ppermute(tail, "ref", up)
     from_right = lax.ppermute(head, "ref", down)
-    out, own, part = refine(cand_mask, queries, slab, (sel1, w1, w2, sel2))
-    return sides(ends, queries, from_left, from_right, own, part, (w1x, w2x, selx, sel3), out)
+    out, own, part = refine(cand_mask, scores, (sel1, w1, w2, sel2))
+    return sides(ends, from_left, from_right, own, part, (w1x, w2x, selx, sel3), out)
 
 
 def solution(mesh):

time: 109 us -> 101 us (0.927)
  blocking collectives: 36.1 us -> 19.2 us
  waiting for transfers between devices: 11 us -> 16.9 us
  starting transfers between devices: 26.5 us -> 31.1 us
  Pallas kernels: 21.9 us -> 20.5 us
    all_to_all x1, blocking collectives: 27.3 us -> 10.3 us  [shards(): lax.all_to_all(score(seat[None], slab, videos), 'qry', 0, 0, tiled=True,...]
    ppermute x0 -> x3, waiting for transfers between devices: none -> 15.5 us  [shards(): lax.ppermute(shared, 'qry', [(g[i], g[(i + step) % side]) for g in outer...]
    ppermute x1, starting transfers between devices: 14.8 us -> 3.48 us  [shards(): from_left = lax.ppermute(tail, 'ref', up)]
    all_to_all x1, waiting for transfers between devices: 11 us -> 1.39 us  [shards(): lax.all_to_all(packed, 'ref', 0, 0, tiled=True, axis_index_groups=lines)]
    ppermute x0 -> x3, starting transfers between devices: none -> 9.33 us  [shards(): lax.ppermute(shared, 'qry', [(g[i], g[(i + step) % side]) for g in outer...]
    all_to_all x0 -> x1, starting transfers between devices: none -> 4.2 us  [shards(): lax.all_to_all(place(source, incoming, side, ready), 'qry', 0, 0, tiled=T...]
    ppermute x1, starting transfers between devices: 2.1 us -> 4.54 us  [shards(): from_right = lax.ppermute(head, 'ref', down)]
    pallas_call x1, Pallas kernels: 3.67 us -> 1.62 us  [place(): pl.pallas_call(place_body, out_shape=jax.ShapeDtypeStruct((copies, BLOCKS...]
  transfers between devices with their start and end apart: 3 -> 7, of which waited for: 1 -> 3; matrix products, arithmetic and copies ran while one was open for 10% -> 11% of each run, Pallas kernels for 13% -> 15%
where the time goes in v2:
time: 101 us
  starting transfers between devices  31.1 us (31%)
  Pallas kernels  20.5 us (20%)
  blocking collectives  19.2 us (19%)
  waiting for transfers between devices  16.9 us (17%)
  other arithmetic  8.89 us (9%)
  local copies, waits for them, and re-layouts  3.42 us (3%)
    ppermute x3, waiting for transfers between devices, shards(): lax.ppermute(shared, 'qry', [(g[i], g[(i + step) % side]) for g in outer...  15.5 us
    pallas_call x1, Pallas kernels, refine(): pl.pallas_call(refine_body, out_shape=(jax.ShapeDtypeStruct((ROWS, COLS),...  13.5 us
    all_to_all x1, blocking collectives, shards(): lax.all_to_all(score(seat[None], slab, videos), 'qry', 0, 0, tiled=True,...  10.3 us
    all_to_all x1, starting transfers between devices, shards(): lax.all_to_all(packed, 'ref', 0, 0, tiled=True, axis_index_groups=lines)  9.58 us
    ppermute x3, starting transfers between devices, shards(): lax.ppermute(shared, 'qry', [(g[i], g[(i + step) % side]) for g in outer...  9.33 us
    all_gather x1, blocking collectives, shards(): lax.all_gather(ref_panels, 'ref', axis=0, tiled=True, axis_index_groups=p...  8.84 us
    ppermute x1, starting transfers between devices, shards(): from_right = lax.ppermute(head, 'ref', down)  4.54 us
    convert_element_type x1, other arithmetic, weights(): w2 = total.astype(BF)  4.37 us
  transfers between devices with their start and end apart: 7, of which 3 were waited for; matrix products, arithmetic and copies ran while one was open for 11% of the time, Pallas kernels for 15%

profile of v2, /device:TPU:1, one launch (start us, length us, event | category | flops | bytes accessed | tf_op | source)
XLA Modules:
  0.0 100.8 jit_solution(8488740077562297535)
XLA Ops:
  0.0 8.8 %all_gather.3.panels_ref = bf16[16,8,1024]{2,1,0:T(8,128)(2,1)S(1)} all-gather(bf16[8,8,1024]{2,1,0:T(8,128)(2,1)} %param.12), channel_id=1, replica_groups={{0,16},{32,48},{64,80},{96,112},{128,144},{160,176},{192,208},{224,240}..., dimensions={0}, use_global_device_ids=true | all-gather | bytes 393216 | tf_op jit(solution)/shard_map/all_gather | solution.py:455
  8.9 0.7 copy-done.3
  9.5 1.4 %pack.1 = (bf16[32,8,1024]{2,1,0:T(8,128)(2,1)}, f32[8,128]{1,0:T(8,128)S(1)}) custom-call(s32[1]{0:T(128)} %bitcast.3.me_ref, s32[256]{0:T(256)S(1)} %copy-done.3, bf16[16,8,1024]{2,1,0:T(8,128)(2,1)S(1)} %all_gather.3.panels_ref), custom_call_target="tpu_custom_call" | custom-call | bytes 600000 | tf_op jit(solution)/shard_map/pack/pallas_call | solution.py:376
  11.0 9.6 %all-to-all-start = ((bf16[32,8,1024]{2,1,0:T(8,128)(2,1)}), bf16[32,8,1024]{2,1,0:T(8,128)(2,1)S(1)}, u32[]{:S(2)}, u32[]{:S(2)}) async-start(bf16[32,8,1024]{2,1,0:T(8,128)(2,1)} %get-tuple-element.10), calls=%async_computation | async-start | bytes 1048576 | tf_op jit(solution)/shard_map/all_to_all | solution.py:457
  23.2 1.3 %add_convert_fusion.1 = bf16[128,1024]{1,0:T(8,128)(2,1)S(1)} fusion(f32[1024]{0:T(1024)S(1)} %tile.143, f32[1024]{0:T(1024)S(1)} %tile.141, f32[1024]{0:T(1024)S(1)} %tile.139, f32[1024]{0:T(1024)S(1)} %tile.137, f32[1024]{0:T(1024)S(1)} %tile.135, f32[1024]{0:T(1024)S(1)} %tile.133, f32[1024]{0:T(1024)S(1)} %tile.131, f32[1024]{0:T(1024)S(1)} %tile.129, ...), kind=kLoop, calls=%fused_computation.78 | loop fusion | flops 6815744 | bytes 311296 | tf_op jit(solution)/shard_map/convert_element_type | solution.py:216
  24.5 1.3 %add_convert_fusion.2 = bf16[128,1024]{1,0:T(8,128)(2,1)S(1)} fusion(f32[1024]{0:T(1024)S(1)} %tile.125, f32[1024]{0:T(1024)S(1)} %tile.123, f32[1024]{0:T(1024)S(1)} %tile.121, f32[1024]{0:T(1024)S(1)} %tile.119, f32[1024]{0:T(1024)S(1)} %tile.117, f32[1024]{0:T(1024)S(1)} %tile.115, f32[1024]{0:T(1024)S(1)} %tile.113, f32[1024]{0:T(1024)S(1)} %tile.111, ...), kind=kLoop, calls=%fused_computation.79 | loop fusion | flops 7602176 | bytes 323968 | tf_op jit(solution)/shard_map/convert_element_type | solution.py:216
  25.8 0.5 add_convert_fusion.4
  26.3 0.5 add_convert_fusion.5
  26.9 0.3 add_convert_fusion.3.rest_3_.rest_4_.w2x_ref
  27.2 4.4 %add_convert_fusion.rest_1_.rest_2_.w2_hbm = bf16[1024,512]{1,0:T(8,128)(2,1)S(1)} fusion(f32[1024]{0:T(1024)S(1)} %bitcast.147, f32[1024]{0:T(1024)S(1)} %bitcast.148, f32[1024]{0:T(1024)S(1)} %bitcast.149, f32[1024]{0:T(1024)S(1)} %bitcast.150, f32[1024]{0:T(1024)S(1)} %bitcast.151, f32[1024]{0:T(1024)S(1)} %bitcast.152, f32[1024]{0:T(1024)S(1)} %bitcast.153, ...), kind=kLoop, calls=%fused_computation.36 | loop fusion | flops 49283072 | bytes 1108480 | tf_op jit(solution)/shard_map/convert_element_type | solution.py:232
  31.6 4.4 %collective-permute-start.2 = (bf16[256,1024]{1,0:T(8,128)(2,1)S(1)}, bf16[256,1024]{1,0:T(8,128)(2,1)S(1)}, u32[]{:S(2)}, u32[]{:S(2)}) collective-permute-start(bf16[256,1024]{1,0:T(8,128)(2,1)S(1)} %share.1.rest_0_), channel_id=1, source_target_pairs={{0,12},{4,0},{8,4},{12,8},{1,13},{5,1},{9,5},{13,9},{2,14},{6,2},{... | collective-permute-start | bytes 1572872 | tf_op jit(solution)/shard_map/ppermute | solution.py:467
  36.0 2.4 %collective-permute-start.1 = (bf16[256,1024]{1,0:T(8,128)(2,1)S(1)}, bf16[256,1024]{1,0:T(8,128)(2,1)}, u32[]{:S(2)}, u32[]{:S(2)}) collective-permute-start(bf16[256,1024]{1,0:T(8,128)(2,1)S(1)} %share.1.rest_0_), channel_id=1, source_target_pairs={{0,8},{4,12},{8,0},{12,4},{1,9},{5,13},{9,1},{13,5},{2,10},{6,14},... | collective-permute-start | bytes 1572872 | tf_op jit(solution)/shard_map/ppermute | solution.py:467
  38.5 2.5 %collective-permute-start = (bf16[256,1024]{1,0:T(8,128)(2,1)S(1)}, bf16[256,1024]{1,0:T(8,128)(2,1)}, u32[]{:S(2)}, u32[]{:S(2)}) collective-permute-start(bf16[256,1024]{1,0:T(8,128)(2,1)S(1)} %share.1.rest_0_), channel_id=1, source_target_pairs={{0,4},{4,8},{8,12},{12,0},{1,5},{5,9},{9,13},{13,1},{2,6},{6,10},{... | collective-permute-start | bytes 1572872 | tf_op jit(solution)/shard_map/ppermute | solution.py:467
  41.9 1.4 %all-to-all-done.incoming_ref = bf16[32,8,1024]{2,1,0:T(8,128)(2,1)S(1)} async-done(((bf16[32,8,1024]{2,1,0:T(8,128)(2,1)}), bf16[32,8,1024]{2,1,0:T(8,128)(2,1)S(1)}, u32[]{:S(2)}, u32[]{:S(2)}) %all-to-all-start) | async-done | bytes 524320 | tf_op jit(solution)/shard_map/all_to_all | solution.py:457
  43.3 1.6 %place.1 = bf16[4,8,8,1024]{3,2,1,0:T(8,128)(2,1)} custom-call(s32[8]{0:T(128)S(1)} %select_reduce_fusion.source_ref, bf16[32,8,1024]{2,1,0:T(8,128)(2,1)S(1)} %all-to-all-done.incoming_ref, bf16[256,1024]{1,0:T(8,128)(2,1)S(1)} %pad_maximum_fusion.rest_0_.rest_1_.w1_hbm, bf16[1024,512]{1,0:T(8,128)(2,1)S(1)} %add_convert_fusion.rest_1_.rest_2_.w2_hbm, ...), custom_call_target="tpu_custom_call" | custom-call | bytes 400000000 | tf_op jit(solution)/shard_map/place/pallas_call | solution.py:428
  44.9 4.2 %all-to-all-start.1 = ((bf16[4,8,8,1024]{3,2,1,0:T(8,128)(2,1)}), bf16[4,8,8,1024]{3,2,1,0:T(8,128)(2,1)S(1)}, u32[]{:S(2)}, u32[]{:S(2)}) async-start(bf16[4,8,8,1024]{3,2,1,0:T(8,128)(2,1)} %place.1), calls=%async_computation.1 | async-start | bytes 1048576 | tf_op jit(solution)/shard_map/all_to_all | solution.py:476
  49.1 3.0 %collective-permute-done.1.rest_2_ = bf16[256,1024]{1,0:T(8,128)(2,1)} collective-permute-done((bf16[256,1024]{1,0:T(8,128)(2,1)S(1)}, bf16[256,1024]{1,0:T(8,128)(2,1)}, u32[]{:S(2)}, u32[]{:S(2)}) %collective-permute-start.1) | collective-permute-done | bytes 524320 | tf_op jit(solution)/shard_map/ppermute | solution.py:467
  52.1 12.5 %collective-permute-done.rest_1_ = bf16[256,1024]{1,0:T(8,128)(2,1)} collective-permute-done((bf16[256,1024]{1,0:T(8,128)(2,1)S(1)}, bf16[256,1024]{1,0:T(8,128)(2,1)}, u32[]{:S(2)}, u32[]{:S(2)}) %collective-permute-start) | collective-permute-done | bytes 524320 | tf_op jit(solution)/shard_map/ppermute | solution.py:467
  64.6 1.9 %score.1 = bf16[4,256,256]{2,1,0:T(8,128)(2,1)S(1)} custom-call(s32[1]{0:T(128)} %bitcast.2.seat_ref, bf16[4,8,8,1024]{3,2,1,0:T(8,128)(2,1)S(1)} %all-to-all-done.1.slab_ref, bf16[256,1024]{1,0:T(8,128)(2,1)S(1)} %share.1.rest_0_, bf16[256,1024]{1,0:T(8,128)(2,1)} %collective-permute-done.rest_1_, bf16[256,1024]{1,0:T(8,128)(2,1)} %collective-permute-done.1.rest_2_, ...), custom_call_target="tpu_custom_call" | custom-call | flops 540000000 | bytes 3100000 | tf_op jit(solution)/shard_map/score/pallas_call | solution.py:346
  66.6 10.3 %all_to_all.15.score_ref = bf16[4,256,256]{2,1,0:T(8,128)(2,1)S(1)} all-to-all(bf16[4,256,256]{2,1,0:T(8,128)(2,1)S(1)} %score.1), channel_id=1, replica_groups={{0,4,8,12},{1,5,9,13},{2,6,10,14},{3,7,11,15},{16,20,24,28},{17,21,25,2..., dimensions={0} | all-to-all | bytes 1048576 | tf_op jit(solution)/shard_map/all_to_all | solution.py:479
  77.1 4.5 %collective-permute-start.4 = (bf16[256,128]{1,0:T(8,128)(2,1)S(1)}, bf16[256,128]{1,0:T(8,128)(2,1)S(1)}, u32[]{:S(2)}, u32[]{:S(2)}) collective-permute-start(bf16[256,128]{1,0:T(8,128)(2,1)S(1)} %get-tuple-element.17), channel_id=1, source_target_pairs={{16,0},{32,16},{48,32},{64,48},{80,64},{96,80},{112,96},{128,112},... | collective-permute-start | bytes 196616 | tf_op jit(solution)/shard_map/ppermute | solution.py:483
  81.6 3.5 %collective-permute-start.3 = (bf16[256,128]{1,0:T(8,128)(2,1)S(1)}, bf16[256,128]{1,0:T(8,128)(2,1)S(1)}, u32[]{:S(2)}, u32[]{:S(2)}) collective-permute-start(bf16[256,128]{1,0:T(8,128)(2,1)S(1)} %get-tuple-element.18), channel_id=1, source_target_pairs={{0,16},{16,32},{32,48},{48,64},{64,80},{80,96},{96,112},{112,128},... | collective-permute-start | bytes 196616 | tf_op jit(solution)/shard_map/ppermute | solution.py:482
  85.1 13.5 %refine.1 = (bf16[256,1024]{1,0:T(8,128)(2,1)}, f32[256,128]{1,0:T(8,128)S(1)}, f32[2,256,128]{2,1,0:T(8,128)S(1)}) custom-call(s32[2,8]{1,0:T(2,128)S(1)} %copy-done.5, bf16[4,256,256]{2,1,0:T(8,128)(2,1)S(1)} %all_to_all.15.score_ref, bf16[1024,256]{1,0:T(8,128)(2,1)S(1)} %copy-done.7, bf16[256,1024]{1,0:T(8,128)(2,1)S(1)} %pad_maximum_fusion.rest_0_.rest_1_.w1_hbm, ...), custom_call_target="tpu_custom_call" | custom-call | flops 9400000512 | bytes 8000000 | tf_op jit(solution)/shard_map/refine/pallas_call | solution.py:294
  98.7 2.0 %sides.1 = bf16[256,1024]{1,0:T(8,128)(2,1)} custom-call(s32[2]{0:T(128)S(1)} %add_convert_fusion.6.rest_4_.ends_ref, bf16[256,128]{1,0:T(8,128)(2,1)S(1)} %collective-permute-done.3.left_ref, bf16[256,128]{1,0:T(8,128)(2,1)S(1)} %collective-permute-done.4.right_ref, f32[256,128]{1,0:T(8,128)S(1)} %get-tuple-element.12.own_ref, ...), custom_call_target="tpu_custom_call", output_to_operand_aliasing={{}: (9, {})} | custom-call | flops 60000000 | bytes 1500000 | tf_op jit(solution)/shard_map/sides/pallas_call | solution.py:322
  (125 shorter events, 3.4 us)
Async XLA Ops:
  0.0 20.9 %copy-start.9 = (bf16[9,32]{1,0:T(8,128)(2,1)S(1)}, bf16[9,32]{1,0:T(8,128)(2,1)}, u32[]{:S(2)}) copy-start(bf16[9,32]{1,0:T(8,128)(2,1)} %param.17) | copy-start | bytes 1732
  0.0 21.1 %copy-start.10 = (f32[32]{0:T(128)S(1)}, f32[32]{0:T(128)}, u32[]{:S(2)}) copy-start(f32[32]{0:T(128)} %param.16) | copy-start | bytes 388
  0.0 21.1 %copy-start.8 = (f32[9,32]{1,0:T(8,128)S(1)}, f32[9,32]{1,0:T(8,128)}, u32[]{:S(2)}) copy-start(f32[9,32]{1,0:T(8,128)} %param.15) | copy-start | bytes 3460
  8.8 0.7 copy-start.3
  11.0 32.3 %all-to-all-start = ((bf16[32,8,1024]{2,1,0:T(8,128)(2,1)}), bf16[32,8,1024]{2,1,0:T(8,128)(2,1)S(1)}, u32[]{:S(2)}, u32[]{:S(2)}) async-start(bf16[32,8,1024]{2,1,0:T(8,128)(2,1)} %get-tuple-element.10), calls=%async_computation | async-start | bytes 1048576 | tf_op jit(solution)/shard_map/all_to_all | solution.py:457
  25.8 5.8 %copy-start = (bf16[256,1024]{1,0:T(8,128)(2,1)S(1)}, bf16[256,1024]{1,0:T(8,128)(2,1)}, u32[]{:S(2)}) copy-start(bf16[256,1024]{1,0:T(8,128)(2,1)} %q_ref.1) | copy-start | bytes 1572868
  31.6 9.4 %copy-start.5 = (s32[2,8]{1,0:T(2,128)S(1)}, s32[2,8]{1,0:T(2,128)}, u32[]{:S(2)}) copy-start(s32[2,8]{1,0:T(2,128)} %mask_ref.1) | copy-start | bytes 196
  31.6 10.1 %copy-start.4 = (s32[256]{0:T(256)S(1)}, s32[256]{0:T(256)}, u32[]{:S(2)}) copy-start(s32[256]{0:T(256)} %time_ref.1) | copy-start | bytes 3076
  31.6 17.5 %collective-permute-start.2 = (bf16[256,1024]{1,0:T(8,128)(2,1)S(1)}, bf16[256,1024]{1,0:T(8,128)(2,1)S(1)}, u32[]{:S(2)}, u32[]{:S(2)}) collective-permute-start(bf16[256,1024]{1,0:T(8,128)(2,1)S(1)} %share.1.rest_0_), channel_id=1, source_target_pairs={{0,12},{4,0},{8,4},{12,8},{1,13},{5,1},{9,5},{13,9},{2,14},{6,2},{... | collective-permute-start | bytes 1572872 | tf_op jit(solution)/shard_map/ppermute | solution.py:467
  36.0 16.1 %collective-permute-start.1 = (bf16[256,1024]{1,0:T(8,128)(2,1)S(1)}, bf16[256,1024]{1,0:T(8,128)(2,1)}, u32[]{:S(2)}, u32[]{:S(2)}) collective-permute-start(bf16[256,1024]{1,0:T(8,128)(2,1)S(1)} %share.1.rest_0_), channel_id=1, source_target_pairs={{0,8},{4,12},{8,0},{12,4},{1,9},{5,13},{9,1},{13,5},{2,10},{6,14},... | collective-permute-start | bytes 1572872 | tf_op jit(solution)/shard_map/ppermute | solution.py:467
  38.5 26.1 %collective-permute-start = (bf16[256,1024]{1,0:T(8,128)(2,1)S(1)}, bf16[256,1024]{1,0:T(8,128)(2,1)}, u32[]{:S(2)}, u32[]{:S(2)}) collective-permute-start(bf16[256,1024]{1,0:T(8,128)(2,1)S(1)} %share.1.rest_0_), channel_id=1, source_target_pairs={{0,4},{4,8},{8,12},{12,0},{1,5},{5,9},{9,13},{13,1},{2,6},{6,10},{... | collective-permute-start | bytes 1572872 | tf_op jit(solution)/shard_map/ppermute | solution.py:467
  44.9 19.7 %all-to-all-start.1 = ((bf16[4,8,8,1024]{3,2,1,0:T(8,128)(2,1)}), bf16[4,8,8,1024]{3,2,1,0:T(8,128)(2,1)S(1)}, u32[]{:S(2)}, u32[]{:S(2)}) async-start(bf16[4,8,8,1024]{3,2,1,0:T(8,128)(2,1)} %place.1), calls=%async_computation.1 | async-start | bytes 1048576 | tf_op jit(solution)/shard_map/all_to_all | solution.py:476
  66.6 18.6 %copy-start.6 = (bf16[256,1024]{1,0:T(8,128)(2,1)S(1)}, bf16[256,1024]{1,0:T(8,128)(2,1)}, u32[]{:S(2)}) copy-start(bf16[256,1024]{1,0:T(8,128)(2,1)} %constant.451.clone.sel2_hbm) | copy-start | bytes 1572868
  66.6 18.5 %copy-start.7 = (bf16[1024,256]{1,0:T(8,128)(2,1)S(1)}, bf16[1024,256]{1,0:T(8,128)(2,1)}, u32[]{:S(2)}) copy-start(bf16[1024,256]{1,0:T(8,128)(2,1)} %constant.450.clone.sel1_hbm) | copy-start | bytes 1572868
  77.1 21.6 %collective-permute-start.4 = (bf16[256,128]{1,0:T(8,128)(2,1)S(1)}, bf16[256,128]{1,0:T(8,128)(2,1)S(1)}, u32[]{:S(2)}, u32[]{:S(2)}) collective-permute-start(bf16[256,128]{1,0:T(8,128)(2,1)S(1)} %get-tuple-element.17), channel_id=1, source_target_pairs={{16,0},{32,16},{48,32},{64,48},{80,64},{96,80},{112,96},{128,112},... | collective-permute-start | bytes 196616 | tf_op jit(solution)/shard_map/ppermute | solution.py:483
  81.6 17.0 %copy-start.1 = (bf16[128,256]{1,0:T(8,128)(2,1)S(1)}, bf16[128,256]{1,0:T(8,128)(2,1)}, u32[]{:S(2)}) copy-start(bf16[128,256]{1,0:T(8,128)(2,1)} %constant.453.clone.sel3_ref) | copy-start | bytes 196612
  81.6 17.0 %copy-start.2 = (bf16[256,128]{1,0:T(8,128)(2,1)S(1)}, bf16[256,128]{1,0:T(8,128)(2,1)}, u32[]{:S(2)}) copy-start(bf16[256,128]{1,0:T(8,128)(2,1)} %constant.452.clone.selx_ref) | copy-start | bytes 196612
  81.6 17.0 %collective-permute-start.3 = (bf16[256,128]{1,0:T(8,128)(2,1)S(1)}, bf16[256,128]{1,0:T(8,128)(2,1)S(1)}, u32[]{:S(2)}, u32[]{:S(2)}) collective-permute-start(bf16[256,128]{1,0:T(8,128)(2,1)S(1)} %get-tuple-element.18), channel_id=1, source_target_pairs={{0,16},{16,32},{32,48},{48,64},{64,80},{80,96},{96,112},{112,128},... | collective-permute-start | bytes 196616 | tf_op jit(solution)/shard_map/ppermute | solution.py:482

commit v3 on v2

--- a/solution.py
+++ b/solution.py
@@ -179,85 +179,6 @@
         copy.wait()
 
 
-def iotas(rows, cols):
-    return lax.broadcasted_iota(I, (rows, cols), 0), lax.broadcasted_iota(I, (rows, cols), 1)
-
-
-def weights(w_first, b_first, w_second):
-    coarse = functools.partial(lax.reduce_precision, exponent_bits=8, mantissa_bits=7)
-    hi = coarse(w_first)
-    mid = w_first - hi
-    b0 = coarse(b_first)
-    b1 = coarse(b_first - b0)
-    b2 = b_first - b0 - b1
-    second = w_second.astype(F)
-    rows = jnp.concatenate([hi, mid, jnp.stack([b0, b1, b2])])
-    wide = jnp.tile(rows, (1, WIN))
-    tall = jnp.tile(second.T, (WIN, 1))
-    width = WIN * 32
-    row, col = iotas(LANES, width)
-    pos = col // 32
-    shift, inner = row // WIN, row % WIN
-    halves = []
-    for part in range(2):
-        total = jnp.zeros((LANES, width), F)
-        for a in range(3):
-            for b in range(3):
-                tap = wide[9 * part + 3 * a + b][None, :]
-                hit = (shift == a) & (inner == pos + b - 1)
-                if b == 0:
-                    hit = hit | ((row == 96 + a) & (pos == 0))
-                if b == 2:
-                    hit = hit | ((row == 99 + a) & (pos == WIN - 1))
-                total = total + jnp.where(hit, tap, 0.0)
-        if part == 0:
-            for j in range(3):
-                total = total + jnp.where(row == 102 + j, wide[18 + j][None, :], 0.0)
-        halves.append(total.astype(BF))
-    w1 = jnp.concatenate(halves)
-    row, col = iotas(width, 4 * LANES)
-    pos = row // 32
-    w = col // LANES
-    a_of = ((col % LANES) // WIN + 4 - w) % 4
-    inner = col % WIN
-    total = jnp.zeros((width, 4 * LANES), F)
-    for a in range(3):
-        for b in range(3):
-            hit = (a_of == a) & (inner == pos + 1 - b)
-            if b == 2:
-                hit = hit | ((a_of == 3) & (inner == a) & (pos == 0))
-            if b == 0:
-                hit = hit | ((a_of == 3) & (inner == 3 + a) & (pos == WIN - 1))
-            total = total + jnp.where(hit, tall[:, 3 * a + b][:, None], 0.0)
-    w2 = total.astype(BF)
-    row, col = iotas(LANES, LANES)
-    halves = []
-    for part in range(2):
-        total = jnp.zeros((LANES, LANES), F)
-        for a in range(3):
-            for b in range(3):
-                tap = wide[9 * part + 3 * a + b, :LANES][None, :]
-                hit = jnp.zeros((LANES, LANES), jnp.bool_)
-                for h in range(4):
-                    hit = hit | ((col // 32 == h) & (row == SIDE_LANE[SIDE_HIDDEN[h] + b - 1] - 1 + a))
-                total = total + jnp.where(hit, tap, 0.0)
-        if part == 0:
-            for j in range(3):
-                total = total + jnp.where(row == 120 + j, wide[18 + j, :LANES][None, :], 0.0)
-        halves.append(total.astype(BF))
-    w1x = jnp.concatenate(halves)
-    total = jnp.zeros((LANES, LANES), F)
-    for a in range(3):
-        for b in range(3):
-            hit = jnp.zeros((LANES, LANES), jnp.bool_)
-            for h in range(4):
-                for j, out in enumerate((0, 1, COLS - 2, COLS - 1)):
-                    if SIDE_HIDDEN[h] == out + b - 1:
-                        hit = hit | ((row // 32 == h) & (col == 3 * j + a))
-            total = total + jnp.where(hit, tall[:LANES, 3 * a + b][:, None], 0.0)
-    return w1, w2, w1x, total.astype(BF)
-
-
 SIDE_LANE = {0: 97, 1: 100, COLS - 2: 103, COLS - 1: 106, -2: 109, -1: 112, COLS: 115, COLS + 1: 118}
 SIDE_HIDDEN = (-1, 0, COLS - 1, COLS)
 
@@ -287,6 +208,113 @@
     return sel1, sel2, selx, hit.astype(BF)
 
 
+def patterns():
+    width = WIN * 32
+    rows1, hit1, rowsx, hitx, lanes2, hit2, lanesy, hity = ([] for _ in range(8))
+    for b in range(3):
+        k, n = np.indices((LANES, width))
+        pos, inner = n // 32, k % WIN
+        hit1.append(
+            ((k < 96) & (inner == pos + b - 1))
+            | ((b == 0) & (k >= 96) & (k < 99) & (pos == 0))
+            | ((b == 2) & (k >= 99) & (k < 102) & (pos == WIN - 1))
+            | ((b == 1) & (k >= 102) & (k < 105))
+        )
+        k, tap = np.indices((LANES, 16))
+        rows1.append(
+            ((k < 96) & (tap == 3 * (k // WIN) + b))
+            | ((b == 0) & (k >= 96) & (k < 99) & (tap == 3 * (k - 96)))
+            | ((b == 2) & (k >= 99) & (k < 102) & (tap == 3 * (k - 99) + 2))
+            | ((b == 1) & (k >= 102) & (k < 105) & (tap == k - 102 + 9))
+        )
+        k, n = np.indices((LANES, LANES))
+        hit = (b == 1) & (k >= 120) & (k < 123)
+        for h, c in enumerate(SIDE_HIDDEN):
+            first = SIDE_LANE[c + b - 1] - 1
+            hit = hit | ((n // 32 == h) & (k >= first) & (k < first + 3))
+        hitx.append(hit)
+        k, tap = np.indices((LANES, 16))
+        row = (b == 1) & (k >= 120) & (k < 123) & (tap == k - 120 + 9)
+        for middle in SIDE_LANE.values():
+            row = row | ((k >= middle - 1) & (k <= middle + 1) & (tap == 3 * (k - middle + 1) + b))
+        rowsx.append(row)
+        n, l = np.indices((width, LANES))
+        pos, inner = n // 32, l % WIN
+        hit2.append(
+            ((l < 96) & (inner == pos + 1 - b))
+            | ((b == 2) & (l >= 96) & (l < 99) & (pos == 0))
+            | ((b == 0) & (l >= 99) & (l < 102) & (pos == WIN - 1))
+        )
+        tap, l = np.indices((16, LANES))
+        lanes2.append(
+            ((l < 96) & (tap == 3 * (l // WIN) + b))
+            | ((b == 2) & (l >= 96) & (l < 99) & (tap == 3 * (l - 96) + 2))
+            | ((b == 0) & (l >= 99) & (l < 102) & (tap == 3 * (l - 99)))
+        )
+        n, l = np.indices((LANES, LANES))
+        hit = np.zeros((LANES, LANES), bool)
+        for h, c in enumerate(SIDE_HIDDEN):
+            for j, out in enumerate((0, 1, COLS - 2, COLS - 1)):
+                if c == out + b - 1:
+                    hit = hit | ((n // 32 == h) & (l // 3 == j))
+        hity.append(hit)
+        tap, l = np.indices((16, LANES))
+        lanesy.append((l < 12) & (tap == 3 * (l % 3) + b))
+    i, n = np.indices((32, width))
+    spread = i == n % 32
+    groups = (rows1, hit1, rowsx, hitx, lanes2, hit2, lanesy, hity)
+    return (spread.astype(BF), spread.T.astype(BF)) + tuple(np.stack(g).astype(BF) for g in groups)
+
+
+def tables_body(
+    first_ref, second_ref, spread_ref, tall_ref, rows1, hit1, rowsx, hitx, lanes2, hit2, lanesy, hity,
+    w1_ref, w2_ref, w1x_ref, w2x_ref,
+):
+    dot = functools.partial(jnp.dot, preferred_element_type=F)
+    raw = first_ref[...]
+    hi = raw.astype(BF).astype(F)
+    mid = (raw - hi).astype(BF).astype(F)
+    low = raw - hi - mid
+    row = lax.broadcasted_iota(I, raw.shape, 0)
+    parts = (
+        jnp.where(row == 10, mid, jnp.where(row == 11, low, hi)),
+        jnp.where(row < 9, mid, 0.0),
+    )
+    for n, part in enumerate(parts):
+        wide = dot(part.astype(BF), spread_ref[...]).astype(BF)
+        at = slice(LANES * n, LANES * (n + 1))
+        w1_ref[at, :] = sum(hit1[b].astype(F) * dot(rows1[b], wide) for b in range(3)).astype(BF)
+        w1x_ref[at, :] = sum(hitx[b].astype(F) * dot(rowsx[b], wide[:, :LANES]) for b in range(3)).astype(BF)
+    second = second_ref[...]
+    tall = tall_ref[...]
+    base = sum(
+        hit2[b].astype(F) * dot(tall, dot(second, lanes2[b]).astype(BF)) for b in range(3)
+    )
+    for w in range(4):
+        turned = pltpu.roll(base, WIN * w, 1) if w else base
+        w2_ref[:, LANES * w : LANES * (w + 1)] = turned.astype(BF)
+    w2x_ref[...] = sum(
+        hity[b].astype(F) * dot(tall[:LANES], dot(second, lanesy[b]).astype(BF)) for b in range(3)
+    ).astype(BF)
+
+
+def weights(w_first, b_first, w_second):
+    first = jnp.concatenate([w_first, jnp.broadcast_to(b_first[None], (3, 32)), jnp.zeros((4, 32), F)])
+    second = jnp.pad(w_second.T, ((0, 0), (0, 7)))
+    consts = patterns()
+    vmem = pl.BlockSpec(memory_space=pltpu.VMEM)
+    shapes = ((2 * LANES, WIN * 32), (WIN * 32, 4 * LANES), (2 * LANES, LANES), (LANES, LANES))
+    return pl.pallas_call(
+        tables_body,
+        out_shape=tuple(jax.ShapeDtypeStruct(shape, BF) for shape in shapes),
+        in_specs=[vmem] * (2 + len(consts)),
+        out_specs=(vmem,) * 4,
+        compiler_params=pltpu.CompilerParams(vmem_limit_bytes=24 * 1024 * 1024),
+        cost_estimate=pl.CostEstimate(flops=0, bytes_accessed=60_000_000, transcendentals=0),
+        name="tables",
+    )(first, second, *consts)
+
+
 def refine(mask, scores, tables):
     vmem = pl.BlockSpec(memory_space=pltpu.VMEM)
     hbm = pl.BlockSpec(memory_space=pltpu.HBM)
@@ -360,7 +388,9 @@
     jobs = []
     for i in range(2 * BLOCKS):
         owner = time_ref[first * BLOCKS + i] // BLOCKS
-        slot = owner - lax.rem(owner, 2) + i // BLOCKS
+        chip = owner // 2
+        chip = jnp.where(lax.rem(me, 2) == 0, chip, out_ref.shape[0] // 2 - 1 - chip)
+        slot = 2 * chip + i // BLOCKS
         copy = pltpu.make_async_copy(panels_ref.at[i], out_ref.at[slot], sems.at[i])
         jobs.append((lax.rem(owner, 2) == lax.rem(me, 2), copy))
     for wanted, copy in jobs:
@@ -448,7 +478,7 @@
     up = [(i, i + 1) for i in range(owners - 1)]
     down = [(i + 1, i) for i in range(owners - 1)]
     pairs = [[2 * z, 2 * z + 1] for z in range(owners // 2)]
-    lines = [[2 * z + c for z in range(owners // 2)] for c in range(2)]
+    lines = [[2 * z + c for z in range(owners // 2)][:: 1 - 2 * c] for c in range(2)]
     side = LANES // WIN
     outer = [[i + side * j for j in range(side)] for i in range(fan // side)]
     inner = [[side * j + i for i in range(side)] for j in range(fan // side)]
@@ -458,6 +488,7 @@
     holder = jnp.arange(owners * BLOCKS, dtype=I) // BLOCKS
     mine = panel_time[None, :] == me * BLOCKS + jnp.arange(BLOCKS, dtype=I)[:, None]
     source = jnp.sum(jnp.where(mine, holder[None, :], 0), axis=1)
+    source = jnp.where(me % 2 == 0, source, owners - 2 - source + 2 * (source % 2))
     ends = jnp.stack([(me > 0).astype(I), (me < owners - 1).astype(I)])
     w1, w2, w1x, w2x = weights(w_first, b_first, w_second)
     sel1, sel2, selx, sel3 = selectors()

time: 101 us -> 99.5 us (0.985)
  other arithmetic: 8.89 us -> 0.48 us
  waiting for transfers between devices: 16.9 us -> 19.7 us
  local copies, waits for them, and re-layouts: 3.42 us -> 5.65 us
  Pallas kernels: 20.5 us -> 22.1 us
  blocking collectives: 19.2 us -> 20.7 us
  starting transfers between devices: 31.1 us -> 29.9 us
    ppermute x3, waiting for transfers between devices: 15.5 us -> 5.7 us  [shards(): lax.ppermute(shared, 'qry', [(g[i], g[(i + step) % side]) for g in outer...]
    all_to_all x1, waiting for transfers between devices: 1.39 us -> 10.5 us  [shards(): lax.all_to_all(packed, 'ref', 0, 0, tiled=True, axis_index_groups=lines)]
    convert_element_type x6 -> x0, other arithmetic: 8.25 us -> none  [the longest x1 4.37 us: weights(): w2 = total.astype(BF)]
    unnamed x26 -> x45, local copies, waits for them, and re-layouts: 1.04 us -> 5.3 us
    all_to_all x1, waiting for transfers between devices: 0.01 us -> 3.45 us  [shards(): lax.all_to_all(place(source, incoming, side, ready), 'qry', 0, 0, tiled=T...]
    another operation x46 -> x0, local copies, waits for them, and re-layouts: 1.91 us -> none  [the longest x44 1.79 us: weights(): wide = jnp.tile(rows, (1, WIN))]
    pallas_call x0 -> x1, Pallas kernels: none -> 1.53 us  [weights(): pl.pallas_call(tables_body, out_shape=tuple((jax.ShapeDtypeStruct(shape,...]
    all_to_all x1, blocking collectives: 10.3 us -> 11.9 us  [shards(): lax.all_to_all(score(seat[None], slab, videos), 'qry', 0, 0, tiled=True,...]
  transfers between devices with their start and end apart: 7 -> 7, of which waited for: 3 -> 3; matrix products, arithmetic and copies ran while one was open for 11% -> 1% of each run, Pallas kernels for 15% -> 17%
where the time goes in v3:
time: 99.5 us; the launch traced here: 98.8 us
  starting transfers between devices  29.9 us (30%)
  Pallas kernels  22.1 us (22%)
  blocking collectives  20.7 us (21%)
  waiting for transfers between devices  19.7 us (20%)
  local copies, waits for them, and re-layouts  5.65 us (6%)
    pallas_call x1, Pallas kernels, refine(): pl.pallas_call(refine_body, out_shape=(jax.ShapeDtypeStruct((ROWS, COLS),...  13.5 us
    all_to_all x1, blocking collectives, shards(): lax.all_to_all(score(seat[None], slab, videos), 'qry', 0, 0, tiled=True,...  11.9 us
    all_to_all x1, waiting for transfers between devices, shards(): lax.all_to_all(packed, 'ref', 0, 0, tiled=True, axis_index_groups=lines)  10.5 us
    all_to_all x1, starting transfers between devices, shards(): lax.all_to_all(packed, 'ref', 0, 0, tiled=True, axis_index_groups=lines)  9.88 us
    ppermute x3, starting transfers between devices, shards(): lax.ppermute(shared, 'qry', [(g[i], g[(i + step) % side]) for g in outer...  9.32 us
    all_gather x1, blocking collectives, shards(): lax.all_gather(ref_panels, 'ref', axis=0, tiled=True, axis_index_groups=p...  8.84 us
    ppermute x3, waiting for transfers between devices, shards(): lax.ppermute(shared, 'qry', [(g[i], g[(i + step) % side]) for g in outer...  5.7 us
    unnamed x45, local copies, waits for them, and re-layouts  5.3 us
  transfers between devices with their start and end apart: 7, of which 3 were waited for; matrix products, arithmetic and copies ran while one was open for 1% of the time, Pallas kernels for 17%

profile of v3, /device:TPU:1, one launch (start us, length us, event | category | flops | bytes accessed | tf_op | source)
XLA Modules:
  0.0 98.8 jit_solution(9059843364993419803)
XLA Ops:
  0.0 8.8 %all_gather.3.panels_ref = bf16[16,8,1024]{2,1,0:T(8,128)(2,1)S(1)} all-gather(bf16[8,8,1024]{2,1,0:T(8,128)(2,1)} %param.22), channel_id=1, replica_groups={{0,16},{32,48},{64,80},{96,112},{128,144},{160,176},{192,208},{224,240}..., dimensions={0}, use_global_device_ids=true | all-gather | bytes 393216 | tf_op jit(solution)/shard_map/all_gather | solution.py:485
  8.8 1.5 %pack.1 = (bf16[32,8,1024]{2,1,0:T(8,128)(2,1)}, f32[8,128]{1,0:T(8,128)S(1)}) custom-call(s32[1]{0:T(128)} %bitcast.3.me_ref, s32[256]{0:T(256)S(1)} %copy-done.13, bf16[16,8,1024]{2,1,0:T(8,128)(2,1)S(1)} %all_gather.3.panels_ref), custom_call_target="tpu_custom_call" | custom-call | bytes 600000 | tf_op jit(solution)/shard_map/pack/pallas_call | solution.py:406
  10.4 9.9 %all-to-all-start = ((bf16[32,8,1024]{2,1,0:T(8,128)(2,1)}), bf16[32,8,1024]{2,1,0:T(8,128)(2,1)S(1)}, u32[]{:S(2)}, u32[]{:S(2)}) async-start(bf16[32,8,1024]{2,1,0:T(8,128)(2,1)} %get-tuple-element.14), calls=%async_computation | async-start | bytes 1048576 | tf_op jit(solution)/shard_map/all_to_all | solution.py:487
  20.5 0.6 copy-done.19
  21.3 0.6 copy-done.11
  21.9 1.1 %copy-done.1 = bf16[3,128,1024]{2,1,0:T(8,128)(2,1)S(1)} copy-done((bf16[3,128,1024]{2,1,0:T(8,128)(2,1)S(1)}, bf16[3,128,1024]{2,1,0:T(8,128)(2,1)}, u32[]{:S(2)}) %copy-start.1) | copy-done | bytes 786456
  23.0 0.9 copy-done.6
  23.9 0.9 copy-done.7
  24.8 1.5 %tables.1 = (bf16[256,1024]{1,0:T(8,128)(2,1)S(1)}, bf16[1024,512]{1,0:T(8,128)(2,1)S(1)}, bf16[256,128]{1,0:T(8,128)(2,1)S(1)}, bf16[128,128]{1,0:T(8,128)(2,1)S(1)}) custom-call(f32[16,32]{1,0:T(8,128)S(1)} %maximum_maximum_fusion.first_ref, bf16[32,16]{1,0:T(8,128)(2,1)S(1)} %pad.4.second_ref, bf16[32,1024]{1,0:T(8,128)(2,1)S(1)} %copy-done.10, ...), custom_call_target="tpu_custom_call" | custom-call | bytes 60000000 | tf_op jit(solution)/shard_map/tables/pallas_call | solution.py:307
  26.4 4.4 %collective-permute-start.2 = (bf16[256,1024]{1,0:T(8,128)(2,1)S(1)}, bf16[256,1024]{1,0:T(8,128)(2,1)S(1)}, u32[]{:S(2)}, u32[]{:S(2)}) collective-permute-start(bf16[256,1024]{1,0:T(8,128)(2,1)S(1)} %share.1.rest_0_), channel_id=1, source_target_pairs={{0,12},{4,0},{8,4},{12,8},{1,13},{5,1},{9,5},{13,9},{2,14},{6,2},{... | collective-permute-start | bytes 1572872 | tf_op jit(solution)/shard_map/ppermute | solution.py:498
  30.8 2.4 %collective-permute-start.1 = (bf16[256,1024]{1,0:T(8,128)(2,1)S(1)}, bf16[256,1024]{1,0:T(8,128)(2,1)}, u32[]{:S(2)}, u32[]{:S(2)}) collective-permute-start(bf16[256,1024]{1,0:T(8,128)(2,1)S(1)} %share.1.rest_0_), channel_id=1, source_target_pairs={{0,8},{4,12},{8,0},{12,4},{1,9},{5,13},{9,1},{13,5},{2,10},{6,14},... | collective-permute-start | bytes 1572872 | tf_op jit(solution)/shard_map/ppermute | solution.py:498
  33.2 2.5 %collective-permute-start = (bf16[256,1024]{1,0:T(8,128)(2,1)S(1)}, bf16[256,1024]{1,0:T(8,128)(2,1)}, u32[]{:S(2)}, u32[]{:S(2)}) collective-permute-start(bf16[256,1024]{1,0:T(8,128)(2,1)S(1)} %share.1.rest_0_), channel_id=1, source_target_pairs={{0,4},{4,8},{8,12},{12,0},{1,5},{5,9},{9,13},{13,1},{2,6},{6,10},{... | collective-permute-start | bytes 1572872 | tf_op jit(solution)/shard_map/ppermute | solution.py:498
  35.7 0.7 copy-done.14
  37.3 10.5 %all-to-all-done.incoming_ref = bf16[32,8,1024]{2,1,0:T(8,128)(2,1)S(1)} async-done(((bf16[32,8,1024]{2,1,0:T(8,128)(2,1)}), bf16[32,8,1024]{2,1,0:T(8,128)(2,1)S(1)}, u32[]{:S(2)}, u32[]{:S(2)}) %all-to-all-start) | async-done | bytes 524320 | tf_op jit(solution)/shard_map/all_to_all | solution.py:487
  47.8 1.6 %place.1 = bf16[4,8,8,1024]{3,2,1,0:T(8,128)(2,1)} custom-call(s32[8]{0:T(128)S(1)} %broadcast_select_fusion.source_ref, bf16[32,8,1024]{2,1,0:T(8,128)(2,1)S(1)} %all-to-all-done.incoming_ref, bf16[256,1024]{1,0:T(8,128)(2,1)S(1)} %get-tuple-element.15.rest_0_.rest_1_.w1_hbm, bf16[1024,512]{1,0:T(8,128)(2,1)S(1)} %get-tuple-element.16.rest_1_.rest_2_.w2_hbm, ...), custom_call_target="tpu_custom_call" | custom-call | bytes 400000000 | tf_op jit(solution)/shard_map/place/pallas_call | solution.py:458
  49.4 4.2 %all-to-all-start.1 = ((bf16[4,8,8,1024]{3,2,1,0:T(8,128)(2,1)}), bf16[4,8,8,1024]{3,2,1,0:T(8,128)(2,1)S(1)}, u32[]{:S(2)}, u32[]{:S(2)}) async-start(bf16[4,8,8,1024]{3,2,1,0:T(8,128)(2,1)} %place.1), calls=%async_computation.1 | async-start | bytes 1048576 | tf_op jit(solution)/shard_map/all_to_all | solution.py:507
  53.6 5.7 %collective-permute-done.rest_1_ = bf16[256,1024]{1,0:T(8,128)(2,1)} collective-permute-done((bf16[256,1024]{1,0:T(8,128)(2,1)S(1)}, bf16[256,1024]{1,0:T(8,128)(2,1)}, u32[]{:S(2)}, u32[]{:S(2)}) %collective-permute-start) | collective-permute-done | bytes 524320 | tf_op jit(solution)/shard_map/ppermute | solution.py:498
  59.3 3.4 %all-to-all-done.1.slab_ref = bf16[4,8,8,1024]{3,2,1,0:T(8,128)(2,1)S(1)} async-done(((bf16[4,8,8,1024]{3,2,1,0:T(8,128)(2,1)}), bf16[4,8,8,1024]{3,2,1,0:T(8,128)(2,1)S(1)}, u32[]{:S(2)}, u32[]{:S(2)}) %all-to-all-start.1) | async-done | bytes 524320 | tf_op jit(solution)/shard_map/all_to_all | solution.py:507
  62.8 1.9 %score.1 = bf16[4,256,256]{2,1,0:T(8,128)(2,1)S(1)} custom-call(s32[1]{0:T(128)} %bitcast.2.seat_ref, bf16[4,8,8,1024]{3,2,1,0:T(8,128)(2,1)S(1)} %all-to-all-done.1.slab_ref, bf16[256,1024]{1,0:T(8,128)(2,1)S(1)} %share.1.rest_0_, bf16[256,1024]{1,0:T(8,128)(2,1)} %collective-permute-done.rest_1_, bf16[256,1024]{1,0:T(8,128)(2,1)} %collective-permute-done.1.rest_2_, ...), custom_call_target="tpu_custom_call" | custom-call | flops 540000000 | bytes 3100000 | tf_op jit(solution)/shard_map/score/pallas_call | solution.py:374
  64.8 11.9 %all_to_all.15.score_ref = bf16[4,256,256]{2,1,0:T(8,128)(2,1)S(1)} all-to-all(bf16[4,256,256]{2,1,0:T(8,128)(2,1)S(1)} %score.1), channel_id=1, replica_groups={{0,4,8,12},{1,5,9,13},{2,6,10,14},{3,7,11,15},{16,20,24,28},{17,21,25,2..., dimensions={0} | all-to-all | bytes 1048576 | tf_op jit(solution)/shard_map/all_to_all | solution.py:510
  76.7 4.4 %collective-permute-start.4 = (bf16[256,128]{1,0:T(8,128)(2,1)S(1)}, bf16[256,128]{1,0:T(8,128)(2,1)S(1)}, u32[]{:S(2)}, u32[]{:S(2)}) collective-permute-start(bf16[256,128]{1,0:T(8,128)(2,1)S(1)} %get-tuple-element.25), channel_id=1, source_target_pairs={{16,0},{32,16},{48,32},{64,48},{80,64},{96,80},{112,96},{128,112},... | collective-permute-start | bytes 196616 | tf_op jit(solution)/shard_map/ppermute | solution.py:514
  81.2 2.1 %collective-permute-start.3 = (bf16[256,128]{1,0:T(8,128)(2,1)S(1)}, bf16[256,128]{1,0:T(8,128)(2,1)S(1)}, u32[]{:S(2)}, u32[]{:S(2)}) collective-permute-start(bf16[256,128]{1,0:T(8,128)(2,1)S(1)} %get-tuple-element.26), channel_id=1, source_target_pairs={{0,16},{16,32},{32,48},{48,64},{64,80},{80,96},{96,112},{112,128},... | collective-permute-start | bytes 196616 | tf_op jit(solution)/shard_map/ppermute | solution.py:513
  83.3 13.5 %refine.1 = (bf16[256,1024]{1,0:T(8,128)(2,1)}, f32[256,128]{1,0:T(8,128)S(1)}, f32[2,256,128]{2,1,0:T(8,128)S(1)}) custom-call(s32[2,8]{1,0:T(2,128)S(1)} %copy-done.14, bf16[4,256,256]{2,1,0:T(8,128)(2,1)S(1)} %all_to_all.15.score_ref, bf16[1024,256]{1,0:T(8,128)(2,1)S(1)} %copy-done.16, bf16[256,1024]{1,0:T(8,128)(2,1)S(1)} %get-tuple-element.15.rest_0_.rest_1_.w1_hbm, ...), custom_call_target="tpu_custom_call" | custom-call | flops 9400000512 | bytes 8000000 | tf_op jit(solution)/shard_map/refine/pallas_call | solution.py:322
  96.8 2.0 %sides.1 = bf16[256,1024]{1,0:T(8,128)(2,1)} custom-call(s32[2]{0:T(128)S(1)} %add_convert_fusion.rest_4_.ends_ref, bf16[256,128]{1,0:T(8,128)(2,1)S(1)} %collective-permute-done.3.left_ref, bf16[256,128]{1,0:T(8,128)(2,1)S(1)} %collective-permute-done.4.right_ref, f32[256,128]{1,0:T(8,128)S(1)} %get-tuple-element.20.own_ref, ...), custom_call_target="tpu_custom_call", output_to_operand_aliasing={{}: (9, {})} | custom-call | flops 60000000 | bytes 1500000 | tf_op jit(solution)/shard_map/sides/pallas_call | solution.py:350
  (58 shorter events, 1.4 us)
Async XLA Ops:
  0.0 8.8 %copy-start.13 = (s32[256]{0:T(256)S(1)}, s32[256]{0:T(256)}, u32[]{:S(2)}) copy-start(s32[256]{0:T(256)} %time_ref.1) | copy-start | bytes 3076
  0.0 21.2 %copy-start = (bf16[3,1024,128]{2,1,0:T(8,128)(2,1)S(1)}, bf16[3,1024,128]{2,1,0:T(8,128)(2,1)}, u32[]{:S(2)}) copy-start(bf16[3,1024,128]{2,1,0:T(8,128)(2,1)} %constant.103.clone.hit2) | copy-start | bytes 2359300
  10.3 9.9 %copy-start.18 = (bf16[9,32]{1,0:T(8,128)(2,1)S(1)}, bf16[9,32]{1,0:T(8,128)(2,1)}, u32[]{:S(2)}) copy-start(bf16[9,32]{1,0:T(8,128)(2,1)} %param.27) | copy-start | bytes 1732
  10.4 10.9 %copy-start.3 = (bf16[1024,32]{1,0:T(8,128)(2,1)S(1)}, bf16[1024,32]{1,0:T(8,128)(2,1)}, u32[]{:S(2)}) copy-start(bf16[1024,32]{1,0:T(8,128)(2,1)} %constant.97.clone.tall_ref) | copy-start | bytes 196612
  10.4 10.9 %copy-start.4 = (bf16[3,128,128]{2,1,0:T(8,128)(2,1)S(1)}, bf16[3,128,128]{2,1,0:T(8,128)(2,1)}, u32[]{:S(2)}) copy-start(bf16[3,128,128]{2,1,0:T(8,128)(2,1)} %constant.105.clone.hity) | copy-start | bytes 294916
  10.4 10.9 %copy-start.5 = (bf16[3,128,128]{2,1,0:T(8,128)(2,1)S(1)}, bf16[3,128,128]{2,1,0:T(8,128)(2,1)}, u32[]{:S(2)}) copy-start(bf16[3,128,128]{2,1,0:T(8,128)(2,1)} %constant.101.clone.hitx) | copy-start | bytes 294916
  10.4 10.9 %copy-start.10 = (bf16[32,1024]{1,0:T(8,128)(2,1)S(1)}, bf16[32,1024]{1,0:T(8,128)(2,1)}, u32[]{:S(2)}) copy-start(bf16[32,1024]{1,0:T(8,128)(2,1)} %constant.96.clone.spread_ref) | copy-start | bytes 196612
  10.4 37.4 %all-to-all-start = ((bf16[32,8,1024]{2,1,0:T(8,128)(2,1)}), bf16[32,8,1024]{2,1,0:T(8,128)(2,1)S(1)}, u32[]{:S(2)}, u32[]{:S(2)}) async-start(bf16[32,8,1024]{2,1,0:T(8,128)(2,1)} %get-tuple-element.14), calls=%async_computation | async-start | bytes 1048576 | tf_op jit(solution)/shard_map/all_to_all | solution.py:487
  20.3 0.9 copy-start.17
  20.5 0.8 copy-start.12
  21.9 1.1 %copy-start.1 = (bf16[3,128,1024]{2,1,0:T(8,128)(2,1)S(1)}, bf16[3,128,1024]{2,1,0:T(8,128)(2,1)}, u32[]{:S(2)}) copy-start(bf16[3,128,1024]{2,1,0:T(8,128)(2,1)} %constant.99.clone.hit1) | copy-start | bytes 2359300
  23.0 0.9 copy-start.6
  23.9 0.9 copy-start.7
  24.8 1.5 %copy-start.2 = (bf16[256,1024]{1,0:T(8,128)(2,1)S(1)}, bf16[256,1024]{1,0:T(8,128)(2,1)}, u32[]{:S(2)}) copy-start(bf16[256,1024]{1,0:T(8,128)(2,1)} %q_ref.1) | copy-start | bytes 1572868
  26.4 27.3 %collective-permute-start.2 = (bf16[256,1024]{1,0:T(8,128)(2,1)S(1)}, bf16[256,1024]{1,0:T(8,128)(2,1)S(1)}, u32[]{:S(2)}, u32[]{:S(2)}) collective-permute-start(bf16[256,1024]{1,0:T(8,128)(2,1)S(1)} %share.1.rest_0_), channel_id=1, source_target_pairs={{0,12},{4,0},{8,4},{12,8},{1,13},{5,1},{9,5},{13,9},{2,14},{6,2},{... | collective-permute-start | bytes 1572872 | tf_op jit(solution)/shard_map/ppermute | solution.py:498
  30.8 22.9 %collective-permute-start.1 = (bf16[256,1024]{1,0:T(8,128)(2,1)S(1)}, bf16[256,1024]{1,0:T(8,128)(2,1)}, u32[]{:S(2)}, u32[]{:S(2)}) collective-permute-start(bf16[256,1024]{1,0:T(8,128)(2,1)S(1)} %share.1.rest_0_), channel_id=1, source_target_pairs={{0,8},{4,12},{8,0},{12,4},{1,9},{5,13},{9,1},{13,5},{2,10},{6,14},... | collective-permute-start | bytes 1572872 | tf_op jit(solution)/shard_map/ppermute | solution.py:498
  33.2 26.1 %collective-permute-start = (bf16[256,1024]{1,0:T(8,128)(2,1)S(1)}, bf16[256,1024]{1,0:T(8,128)(2,1)}, u32[]{:S(2)}, u32[]{:S(2)}) collective-permute-start(bf16[256,1024]{1,0:T(8,128)(2,1)S(1)} %share.1.rest_0_), channel_id=1, source_target_pairs={{0,4},{4,8},{8,12},{12,0},{1,5},{5,9},{9,13},{13,1},{2,6},{6,10},{... | collective-permute-start | bytes 1572872 | tf_op jit(solution)/shard_map/ppermute | solution.py:498
  49.4 13.3 %all-to-all-start.1 = ((bf16[4,8,8,1024]{3,2,1,0:T(8,128)(2,1)}), bf16[4,8,8,1024]{3,2,1,0:T(8,128)(2,1)S(1)}, u32[]{:S(2)}, u32[]{:S(2)}) async-start(bf16[4,8,8,1024]{3,2,1,0:T(8,128)(2,1)} %place.1), calls=%async_computation.1 | async-start | bytes 1048576 | tf_op jit(solution)/shard_map/all_to_all | solution.py:507
  64.7 18.5 %copy-start.15 = (bf16[256,1024]{1,0:T(8,128)(2,1)S(1)}, bf16[256,1024]{1,0:T(8,128)(2,1)}, u32[]{:S(2)}) copy-start(bf16[256,1024]{1,0:T(8,128)(2,1)} %constant.107.clone.sel2_hbm) | copy-start | bytes 1572868
  64.7 18.5 %copy-start.16 = (bf16[1024,256]{1,0:T(8,128)(2,1)S(1)}, bf16[1024,256]{1,0:T(8,128)(2,1)}, u32[]{:S(2)}) copy-start(bf16[1024,256]{1,0:T(8,128)(2,1)} %constant.106.clone.sel1_hbm) | copy-start | bytes 1572868
  76.7 20.0 %collective-permute-start.4 = (bf16[256,128]{1,0:T(8,128)(2,1)S(1)}, bf16[256,128]{1,0:T(8,128)(2,1)S(1)}, u32[]{:S(2)}, u32[]{:S(2)}) collective-permute-start(bf16[256,128]{1,0:T(8,128)(2,1)S(1)} %get-tuple-element.25), channel_id=1, source_target_pairs={{16,0},{32,16},{48,32},{64,48},{80,64},{96,80},{112,96},{128,112},... | collective-permute-start | bytes 196616 | tf_op jit(solution)/shard_map/ppermute | solution.py:514
  81.2 15.6 %copy-start.8 = (bf16[128,256]{1,0:T(8,128)(2,1)S(1)}, bf16[128,256]{1,0:T(8,128)(2,1)}, u32[]{:S(2)}) copy-start(bf16[128,256]{1,0:T(8,128)(2,1)} %constant.109.clone.sel3_ref) | copy-start | bytes 196612
  81.2 15.6 %copy-start.9 = (bf16[256,128]{1,0:T(8,128)(2,1)S(1)}, bf16[256,128]{1,0:T(8,128)(2,1)}, u32[]{:S(2)}) copy-start(bf16[256,128]{1,0:T(8,128)(2,1)} %constant.108.clone.selx_ref) | copy-start | bytes 196612
  81.2 15.6 %collective-permute-start.3 = (bf16[256,128]{1,0:T(8,128)(2,1)S(1)}, bf16[256,128]{1,0:T(8,128)(2,1)S(1)}, u32[]{:S(2)}, u32[]{:S(2)}) collective-permute-start(bf16[256,128]{1,0:T(8,128)(2,1)S(1)} %get-tuple-element.26), channel_id=1, source_target_pairs={{0,16},{16,32},{32,48},{48,64},{64,80},{80,96},{96,112},{112,128},... | collective-permute-start | bytes 196616 | tf_op jit(solution)/shard_map/ppermute | solution.py:513
  (3 other events, 2.0 us)

commit v4 on v3

--- a/solution.py
+++ b/solution.py
@@ -40,24 +40,15 @@
 
 
 def refine_body(
-    mask_ref, score_ref, sel1_hbm, w1_hbm, w2_hbm, sel2_hbm,
-    out_ref, own_ref, part_ref, sims, gg, xs, hs, acc, ee, sel1_ref, w1_ref, w2_ref, sel2_ref, sems,
+    mask_ref, score_ref, sel1_ref, w1_ref, w2_ref, sel2_ref,
+    out_ref, own_ref, part_ref, sims, gg, xs, hs, acc, ee,
 ):
-    loads = [
-        pltpu.make_async_copy(src, dst, sems.at[n])
-        for n, (src, dst) in enumerate(
-            zip((sel1_hbm, w1_hbm, w2_hbm, sel2_hbm), (sel1_ref, w1_ref, w2_ref, sel2_ref))
-        )
-    ]
-    for load in loads:
-        load.start()
     lane = lax.broadcasted_iota(I, (ROWS, LANES), 1)
     top = lax.broadcasted_iota(I, (ROWS, LANES), 0) < ROWS // 2
     keep = []
     for half in range(2):
         rows = [quarters(lane, [mask_ref[r, 4 * half + j] for j in range(4)]) for r in range(2)]
         keep.append(jnp.where(top, rows[0], rows[1]).astype(F))
-    loads[0].wait()
     g0 = jnp.zeros((ROWS, 2 * LANES), F)
     for n in range(BLOCKS):
         half = n % 2
@@ -69,46 +60,41 @@
     gg[0] = g[:, :LANES]
     gg[1] = g[:, LANES:]
     group = ROWS * BPI
-    for load in loads[1:]:
-        load.wait()
+
+    zero = jnp.zeros((), BF)
 
     def step(it, carry):
-        ge = gg[it]
+        ge = gg[it].astype(BF)
+        one = jnp.ones((), BF)
+        p = []
         for w in range(4):
             s = sims[2 * w + it]
-            up = from_above(s)
-            dn = from_below(s)
+            up = from_above(s).astype(BF)
+            dn = from_below(s).astype(BF)
+            s = s.astype(BF)
             for b in range(BPI):
                 e = pltpu.roll(ge, (96 - 6 * (4 * b + w)) % LANES, 1)
                 parts = (
                     pltpu.roll(up, (LANES - WIN * b) % LANES, 1) if b else up,
                     pltpu.roll(s, (LANES + WIN - WIN * b) % LANES, 1) if b != 1 else s,
                     pltpu.roll(dn, (LANES + 2 * WIN - WIN * b) % LANES, 1) if b != 2 else dn,
-                    jnp.where(lane < 102, e, 1.0),
+                    jnp.where(lane < 102, e, one),
                 )
-                x = quarters(lane, parts).astype(BF)
+                x = quarters(lane, parts)
                 at = group * w + ROWS * b
                 xs[at : at + ROWS, 0:LANES] = x
                 xs[at : at + ROWS, LANES : 2 * LANES] = x
-        x = xs[...]
-        for n in range(4):
-            h = jnp.dot(x, w1_ref[:, 256 * n : 256 * (n + 1)], preferred_element_type=F)
-            hs[:, 256 * n : 256 * (n + 1)] = jnp.maximum(h.astype(BF), jnp.zeros((), BF))
-
-        @pl.when(it == 0)
-        def _():
-            hs[0:ROWS, 0:32] = jnp.zeros((ROWS, 32), BF)
-
-        @pl.when(it == BLOCKS // BPI - 1)
-        def _():
-            hs[4 * group - ROWS : 4 * group, WIN * 32 - 32 : WIN * 32] = jnp.zeros((ROWS, 32), BF)
-
-        p = [
-            jnp.dot(
-                hs[group * w : group * (w + 1), :], w2_ref[:, LANES * w : LANES * (w + 1)], preferred_element_type=F
-            )
-            for w in range(4)
-        ]
+            at = slice(group * w, group * (w + 1))
+            x = xs[at, :]
+            for n in range(2):
+                h = jnp.dot(x, w1_ref[:, 512 * n : 512 * (n + 1)], preferred_element_type=F)
+                hs[at, 512 * n : 512 * (n + 1)] = jnp.maximum(h.astype(BF), zero)
+            if w == 0:
+                hs[0:ROWS, 0:32] = jnp.where(it == 0, zero, hs[0:ROWS, 0:32])
+            if w == 3:
+                end = slice(4 * group - ROWS, 4 * group), slice(WIN * 32 - 32, WIN * 32)
+                hs[end] = jnp.where(it == BLOCKS // BPI - 1, zero, hs[end])
+            p.append(jnp.dot(hs[at, :], w2_ref[:, LANES * w : LANES * (w + 1)], preferred_element_type=F))
         tot = jnp.zeros((ROWS, LANES), F)
         for b in range(BPI):
             k = it * BPI + b
@@ -317,8 +303,6 @@
 
 def refine(mask, scores, tables):
     vmem = pl.BlockSpec(memory_space=pltpu.VMEM)
-    hbm = pl.BlockSpec(memory_space=pltpu.HBM)
-    arrays = tables
     return pl.pallas_call(
         refine_body,
         out_shape=(
@@ -326,7 +310,7 @@
             jax.ShapeDtypeStruct((ROWS, LANES), F),
             jax.ShapeDtypeStruct((2, ROWS, LANES), F),
         ),
-        in_specs=[pl.BlockSpec(memory_space=pltpu.SMEM), vmem] + [hbm] * len(arrays),
+        in_specs=[pl.BlockSpec(memory_space=pltpu.SMEM), vmem] + [vmem] * len(tables),
         out_specs=(vmem, vmem, vmem),
         scratch_shapes=[
             pltpu.VMEM((BLOCKS, ROWS, LANES), F),
@@ -335,13 +319,11 @@
             pltpu.VMEM((4 * ROWS * BPI, WIN * 32), BF),
             pltpu.VMEM((BLOCKS, ROWS, LANES), F),
             pltpu.VMEM((2, ROWS, LANES), F),
-        ]
-        + [pltpu.VMEM(array.shape, BF) for array in arrays]
-        + [pltpu.SemaphoreType.DMA((len(arrays),))],
+        ],
         compiler_params=pltpu.CompilerParams(vmem_limit_bytes=36 * 1024 * 1024),
         cost_estimate=pl.CostEstimate(flops=9_400_000_000, bytes_accessed=8_000_000, transcendentals=0),
         name="refine",
-    )(mask, scores, *arrays)
+    )(mask, scores, *tables)
 
 
 def sides(ends, left, right, own, part, tables, out):
@@ -437,18 +419,15 @@
 
 
 def place_body(source_ref, incoming_ref, *rest):
-    out_ref, held, in_sems, out_sems = rest[-4:]
-    gets = [
-        pltpu.make_async_copy(incoming_ref.at[source_ref[k]], held.at[k], in_sems.at[k]) for k in range(BLOCKS)
+    out_ref, sems = rest[-2:]
+    copies = [
+        pltpu.make_async_copy(incoming_ref.at[source_ref[k]], out_ref.at[d, k], sems.at[d, k])
+        for k in range(BLOCKS)
+        for d in range(out_ref.shape[0])
     ]
-    for copy in gets:
+    for copy in copies:
         copy.start()
-    for copy in gets:
-        copy.wait()
-    puts = [pltpu.make_async_copy(held, out_ref.at[d], out_sems.at[d]) for d in range(out_ref.shape[0])]
-    for copy in puts:
-        copy.start()
-    for copy in puts:
+    for copy in copies:
         copy.wait()
 
 
@@ -460,11 +439,7 @@
         out_shape=jax.ShapeDtypeStruct((copies, BLOCKS) + piece, BF),
         in_specs=[pl.BlockSpec(memory_space=pltpu.SMEM)] + [any_space] * (1 + len(ready)),
         out_specs=any_space,
-        scratch_shapes=[
-            pltpu.VMEM((BLOCKS,) + piece, BF),
-            pltpu.SemaphoreType.DMA((BLOCKS,)),
-            pltpu.SemaphoreType.DMA((copies,)),
-        ],
+        scratch_shapes=[pltpu.SemaphoreType.DMA((copies, BLOCKS))],
         compiler_params=pltpu.CompilerParams(vmem_limit_bytes=4 * 1024 * 1024),
         cost_estimate=pl.CostEstimate(flops=0, bytes_accessed=400_000_000, transcendentals=0),
         name="place",

time: 99.5 us -> 97.8 us (0.983)
  Pallas kernels: 22.1 us -> 20.9 us
    pallas_call x1, Pallas kernels: 13.5 us -> 12.3 us  [refine(): pl.pallas_call(refine_body, out_shape=(jax.ShapeDtypeStruct((ROWS, COLS),...]
  transfers between devices with their start and end apart: 7 -> 7, of which waited for: 3 -> 3; matrix products, arithmetic and copies ran while one was open for 1% -> 1% of each run, Pallas kernels for 17% -> 16%
where the time goes in v4:
time: 97.8 us; the launch traced here: 97.1 us
  starting transfers between devices  30 us (31%)
  Pallas kernels  20.9 us (21%)
  blocking collectives  20.5 us (21%)
  waiting for transfers between devices  19.3 us (20%)
  local copies, waits for them, and re-layouts  5.65 us (6%)
    pallas_call x1, Pallas kernels, refine(): pl.pallas_call(refine_body, out_shape=(jax.ShapeDtypeStruct((ROWS, COLS),...  12.3 us
    all_to_all x1, blocking collectives, shards(): lax.all_to_all(score(seat[None], slab, videos), 'qry', 0, 0, tiled=True,...  11.7 us
    all_to_all x1, waiting for transfers between devices, shards(): lax.all_to_all(packed, 'ref', 0, 0, tiled=True, axis_index_groups=lines)  10.3 us
    all_to_all x1, starting transfers between devices, shards(): lax.all_to_all(packed, 'ref', 0, 0, tiled=True, axis_index_groups=lines)  9.83 us
    ppermute x3, starting transfers between devices, shards(): lax.ppermute(shared, 'qry', [(g[i], g[(i + step) % side]) for g in outer...  9.33 us
    all_gather x1, blocking collectives, shards(): lax.all_gather(ref_panels, 'ref', axis=0, tiled=True, axis_index_groups=p...  8.84 us
    ppermute x3, waiting for transfers between devices, shards(): lax.ppermute(shared, 'qry', [(g[i], g[(i + step) % side]) for g in outer...  5.95 us
    unnamed x45, local copies, waits for them, and re-layouts  5.3 us
  transfers between devices with their start and end apart: 7, of which 3 were waited for; matrix products, arithmetic and copies ran while one was open for 1% of the time, Pallas kernels for 16%

profile of v4, /device:TPU:1, one launch (start us, length us, event | category | flops | bytes accessed | tf_op | source)
XLA Modules:
  0.0 97.1 jit_solution(1996303552128666082)
XLA Ops:
  0.0 8.8 %all_gather.3.panels_ref = bf16[16,8,1024]{2,1,0:T(8,128)(2,1)S(1)} all-gather(bf16[8,8,1024]{2,1,0:T(8,128)(2,1)} %param.22), channel_id=1, replica_groups={{0,16},{32,48},{64,80},{96,112},{128,144},{160,176},{192,208},{224,240}..., dimensions={0}, use_global_device_ids=true | all-gather | bytes 393216 | tf_op jit(solution)/shard_map/all_gather | solution.py:460
  8.8 1.5 %pack.1 = (bf16[32,8,1024]{2,1,0:T(8,128)(2,1)}, f32[8,128]{1,0:T(8,128)S(1)}) custom-call(s32[1]{0:T(128)} %bitcast.3.me_ref, s32[256]{0:T(256)S(1)} %copy-done.13, bf16[16,8,1024]{2,1,0:T(8,128)(2,1)S(1)} %all_gather.3.panels_ref), custom_call_target="tpu_custom_call" | custom-call | bytes 600000 | tf_op jit(solution)/shard_map/pack/pallas_call | solution.py:388
  10.4 9.8 %all-to-all-start = ((bf16[32,8,1024]{2,1,0:T(8,128)(2,1)}), bf16[32,8,1024]{2,1,0:T(8,128)(2,1)S(1)}, u32[]{:S(2)}, u32[]{:S(2)}) async-start(bf16[32,8,1024]{2,1,0:T(8,128)(2,1)} %get-tuple-element.14), calls=%async_computation | async-start | bytes 1048576 | tf_op jit(solution)/shard_map/all_to_all | solution.py:462
  20.4 0.6 copy-done.19
  21.2 0.6 copy-done.11
  21.8 1.1 %copy-done.1 = bf16[3,128,1024]{2,1,0:T(8,128)(2,1)S(1)} copy-done((bf16[3,128,1024]{2,1,0:T(8,128)(2,1)S(1)}, bf16[3,128,1024]{2,1,0:T(8,128)(2,1)}, u32[]{:S(2)}) %copy-start.1) | copy-done | bytes 786456
  22.9 0.9 copy-done.6
  23.8 0.9 copy-done.7
  24.7 1.5 %tables.1 = (bf16[256,1024]{1,0:T(8,128)(2,1)S(1)}, bf16[1024,512]{1,0:T(8,128)(2,1)S(1)}, bf16[256,128]{1,0:T(8,128)(2,1)S(1)}, bf16[128,128]{1,0:T(8,128)(2,1)S(1)}) custom-call(f32[16,32]{1,0:T(8,128)S(1)} %maximum_maximum_fusion.first_ref, bf16[32,16]{1,0:T(8,128)(2,1)S(1)} %pad.4.second_ref, bf16[32,1024]{1,0:T(8,128)(2,1)S(1)} %copy-done.10, ...), custom_call_target="tpu_custom_call" | custom-call | bytes 60000000 | tf_op jit(solution)/shard_map/tables/pallas_call | solution.py:293
  26.3 4.4 %collective-permute-start.2 = (bf16[256,1024]{1,0:T(8,128)(2,1)S(1)}, bf16[256,1024]{1,0:T(8,128)(2,1)S(1)}, u32[]{:S(2)}, u32[]{:S(2)}) collective-permute-start(bf16[256,1024]{1,0:T(8,128)(2,1)S(1)} %share.1.rest_0_), channel_id=1, source_target_pairs={{0,12},{4,0},{8,4},{12,8},{1,13},{5,1},{9,5},{13,9},{2,14},{6,2},{... | collective-permute-start | bytes 1572872 | tf_op jit(solution)/shard_map/ppermute | solution.py:473
  30.7 2.4 %collective-permute-start.1 = (bf16[256,1024]{1,0:T(8,128)(2,1)S(1)}, bf16[256,1024]{1,0:T(8,128)(2,1)}, u32[]{:S(2)}, u32[]{:S(2)}) collective-permute-start(bf16[256,1024]{1,0:T(8,128)(2,1)S(1)} %share.1.rest_0_), channel_id=1, source_target_pairs={{0,8},{4,12},{8,0},{12,4},{1,9},{5,13},{9,1},{13,5},{2,10},{6,14},... | collective-permute-start | bytes 1572872 | tf_op jit(solution)/shard_map/ppermute | solution.py:473
  33.1 2.5 %collective-permute-start = (bf16[256,1024]{1,0:T(8,128)(2,1)S(1)}, bf16[256,1024]{1,0:T(8,128)(2,1)}, u32[]{:S(2)}, u32[]{:S(2)}) collective-permute-start(bf16[256,1024]{1,0:T(8,128)(2,1)S(1)} %share.1.rest_0_), channel_id=1, source_target_pairs={{0,4},{4,8},{8,12},{12,0},{1,5},{5,9},{9,13},{13,1},{2,6},{6,10},{... | collective-permute-start | bytes 1572872 | tf_op jit(solution)/shard_map/ppermute | solution.py:473
  35.7 0.7 copy-done.14
  37.2 10.3 %all-to-all-done.incoming_ref = bf16[32,8,1024]{2,1,0:T(8,128)(2,1)S(1)} async-done(((bf16[32,8,1024]{2,1,0:T(8,128)(2,1)}), bf16[32,8,1024]{2,1,0:T(8,128)(2,1)S(1)}, u32[]{:S(2)}, u32[]{:S(2)}) %all-to-all-start) | async-done | bytes 524320 | tf_op jit(solution)/shard_map/all_to_all | solution.py:462
  47.5 1.6 %place.1 = bf16[4,8,8,1024]{3,2,1,0:T(8,128)(2,1)} custom-call(s32[8]{0:T(128)S(1)} %broadcast_select_fusion.source_ref, bf16[32,8,1024]{2,1,0:T(8,128)(2,1)S(1)} %all-to-all-done.incoming_ref, bf16[256,1024]{1,0:T(8,128)(2,1)S(1)} %get-tuple-element.15.rest_0_.rest_1_.w1_ref, bf16[1024,512]{1,0:T(8,128)(2,1)S(1)} %get-tuple-element.16.rest_1_.rest_2_.w2_ref, ...), custom_call_target="tpu_custom_call" | custom-call | bytes 400000000 | tf_op jit(solution)/shard_map/place/pallas_call | solution.py:437
  49.1 4.2 %all-to-all-start.1 = ((bf16[4,8,8,1024]{3,2,1,0:T(8,128)(2,1)}), bf16[4,8,8,1024]{3,2,1,0:T(8,128)(2,1)S(1)}, u32[]{:S(2)}, u32[]{:S(2)}) async-start(bf16[4,8,8,1024]{3,2,1,0:T(8,128)(2,1)} %place.1), calls=%async_computation.1 | async-start | bytes 1048576 | tf_op jit(solution)/shard_map/all_to_all | solution.py:482
  53.3 5.9 %collective-permute-done.rest_1_ = bf16[256,1024]{1,0:T(8,128)(2,1)} collective-permute-done((bf16[256,1024]{1,0:T(8,128)(2,1)S(1)}, bf16[256,1024]{1,0:T(8,128)(2,1)}, u32[]{:S(2)}, u32[]{:S(2)}) %collective-permute-start) | collective-permute-done | bytes 524320 | tf_op jit(solution)/shard_map/ppermute | solution.py:473
  59.3 3.0 %all-to-all-done.1.slab_ref = bf16[4,8,8,1024]{3,2,1,0:T(8,128)(2,1)S(1)} async-done(((bf16[4,8,8,1024]{3,2,1,0:T(8,128)(2,1)}), bf16[4,8,8,1024]{3,2,1,0:T(8,128)(2,1)S(1)}, u32[]{:S(2)}, u32[]{:S(2)}) %all-to-all-start.1) | async-done | bytes 524320 | tf_op jit(solution)/shard_map/all_to_all | solution.py:482
  62.3 1.9 %score.1 = bf16[4,256,256]{2,1,0:T(8,128)(2,1)S(1)} custom-call(s32[1]{0:T(128)} %bitcast.2.seat_ref, bf16[4,8,8,1024]{3,2,1,0:T(8,128)(2,1)S(1)} %all-to-all-done.1.slab_ref, bf16[256,1024]{1,0:T(8,128)(2,1)S(1)} %share.1.rest_0_, bf16[256,1024]{1,0:T(8,128)(2,1)} %collective-permute-done.rest_1_, bf16[256,1024]{1,0:T(8,128)(2,1)} %collective-permute-done.1.rest_2_, ...), custom_call_target="tpu_custom_call" | custom-call | flops 540000000 | bytes 3100000 | tf_op jit(solution)/shard_map/score/pallas_call | solution.py:356
  64.3 11.7 %all_to_all.15.score_ref = bf16[4,256,256]{2,1,0:T(8,128)(2,1)S(1)} all-to-all(bf16[4,256,256]{2,1,0:T(8,128)(2,1)S(1)} %score.1), channel_id=1, replica_groups={{0,4,8,12},{1,5,9,13},{2,6,10,14},{3,7,11,15},{16,20,24,28},{17,21,25,2..., dimensions={0} | all-to-all | bytes 1048576 | tf_op jit(solution)/shard_map/all_to_all | solution.py:485
  76.1 4.6 %collective-permute-start.4 = (bf16[256,128]{1,0:T(8,128)(2,1)S(1)}, bf16[256,128]{1,0:T(8,128)(2,1)S(1)}, u32[]{:S(2)}, u32[]{:S(2)}) collective-permute-start(bf16[256,128]{1,0:T(8,128)(2,1)S(1)} %get-tuple-element.25), channel_id=1, source_target_pairs={{16,0},{32,16},{48,32},{64,48},{80,64},{96,80},{112,96},{128,112},... | collective-permute-start | bytes 196616 | tf_op jit(solution)/shard_map/ppermute | solution.py:489
  80.7 2.1 %collective-permute-start.3 = (bf16[256,128]{1,0:T(8,128)(2,1)S(1)}, bf16[256,128]{1,0:T(8,128)(2,1)S(1)}, u32[]{:S(2)}, u32[]{:S(2)}) collective-permute-start(bf16[256,128]{1,0:T(8,128)(2,1)S(1)} %get-tuple-element.26), channel_id=1, source_target_pairs={{0,16},{16,32},{32,48},{48,64},{64,80},{80,96},{96,112},{112,128},... | collective-permute-start | bytes 196616 | tf_op jit(solution)/shard_map/ppermute | solution.py:488
  82.8 12.3 %refine.1 = (bf16[256,1024]{1,0:T(8,128)(2,1)}, f32[256,128]{1,0:T(8,128)S(1)}, f32[2,256,128]{2,1,0:T(8,128)S(1)}) custom-call(s32[2,8]{1,0:T(2,128)S(1)} %copy-done.14, bf16[4,256,256]{2,1,0:T(8,128)(2,1)S(1)} %all_to_all.15.score_ref, bf16[1024,256]{1,0:T(8,128)(2,1)S(1)} %copy-done.16, bf16[256,1024]{1,0:T(8,128)(2,1)S(1)} %get-tuple-element.15.rest_0_.rest_1_.w1_ref, ...), custom_call_target="tpu_custom_call" | custom-call | flops 9400000512 | bytes 8000000 | tf_op jit(solution)/shard_map/refine/pallas_call | solution.py:306
  95.1 2.0 %sides.1 = bf16[256,1024]{1,0:T(8,128)(2,1)} custom-call(s32[2]{0:T(128)S(1)} %add_convert_fusion.rest_4_.ends_ref, bf16[256,128]{1,0:T(8,128)(2,1)S(1)} %collective-permute-done.3.left_ref, bf16[256,128]{1,0:T(8,128)(2,1)S(1)} %collective-permute-done.4.right_ref, f32[256,128]{1,0:T(8,128)S(1)} %get-tuple-element.20.own_ref, ...), custom_call_target="tpu_custom_call", output_to_operand_aliasing={{}: (9, {})} | custom-call | flops 60000000 | bytes 1500000 | tf_op jit(solution)/shard_map/sides/pallas_call | solution.py:332
  (58 shorter events, 1.4 us)
Async XLA Ops:
  0.0 8.8 %copy-start.13 = (s32[256]{0:T(256)S(1)}, s32[256]{0:T(256)}, u32[]{:S(2)}) copy-start(s32[256]{0:T(256)} %time_ref.1) | copy-start | bytes 3076
  0.0 21.2 %copy-start = (bf16[3,1024,128]{2,1,0:T(8,128)(2,1)S(1)}, bf16[3,1024,128]{2,1,0:T(8,128)(2,1)}, u32[]{:S(2)}) copy-start(bf16[3,1024,128]{2,1,0:T(8,128)(2,1)} %constant.103.clone.hit2) | copy-start | bytes 2359300
  10.3 9.9 %copy-start.18 = (bf16[9,32]{1,0:T(8,128)(2,1)S(1)}, bf16[9,32]{1,0:T(8,128)(2,1)}, u32[]{:S(2)}) copy-start(bf16[9,32]{1,0:T(8,128)(2,1)} %param.27) | copy-start | bytes 1732
  10.4 10.8 %copy-start.3 = (bf16[1024,32]{1,0:T(8,128)(2,1)S(1)}, bf16[1024,32]{1,0:T(8,128)(2,1)}, u32[]{:S(2)}) copy-start(bf16[1024,32]{1,0:T(8,128)(2,1)} %constant.97.clone.tall_ref) | copy-start | bytes 196612
  10.4 10.8 %copy-start.4 = (bf16[3,128,128]{2,1,0:T(8,128)(2,1)S(1)}, bf16[3,128,128]{2,1,0:T(8,128)(2,1)}, u32[]{:S(2)}) copy-start(bf16[3,128,128]{2,1,0:T(8,128)(2,1)} %constant.105.clone.hity) | copy-start | bytes 294916
  10.4 10.8 %copy-start.5 = (bf16[3,128,128]{2,1,0:T(8,128)(2,1)S(1)}, bf16[3,128,128]{2,1,0:T(8,128)(2,1)}, u32[]{:S(2)}) copy-start(bf16[3,128,128]{2,1,0:T(8,128)(2,1)} %constant.101.clone.hitx) | copy-start | bytes 294916
  10.4 10.8 %copy-start.10 = (bf16[32,1024]{1,0:T(8,128)(2,1)S(1)}, bf16[32,1024]{1,0:T(8,128)(2,1)}, u32[]{:S(2)}) copy-start(bf16[32,1024]{1,0:T(8,128)(2,1)} %constant.96.clone.spread_ref) | copy-start | bytes 196612
  10.4 37.1 %all-to-all-start = ((bf16[32,8,1024]{2,1,0:T(8,128)(2,1)}), bf16[32,8,1024]{2,1,0:T(8,128)(2,1)S(1)}, u32[]{:S(2)}, u32[]{:S(2)}) async-start(bf16[32,8,1024]{2,1,0:T(8,128)(2,1)} %get-tuple-element.14), calls=%async_computation | async-start | bytes 1048576 | tf_op jit(solution)/shard_map/all_to_all | solution.py:462
  20.2 0.9 copy-start.17
  20.4 0.8 copy-start.12
  21.8 1.1 %copy-start.1 = (bf16[3,128,1024]{2,1,0:T(8,128)(2,1)S(1)}, bf16[3,128,1024]{2,1,0:T(8,128)(2,1)}, u32[]{:S(2)}) copy-start(bf16[3,128,1024]{2,1,0:T(8,128)(2,1)} %constant.99.clone.hit1) | copy-start | bytes 2359300
  22.9 0.9 copy-start.6
  23.8 0.9 copy-start.7
  24.7 1.5 %copy-start.2 = (bf16[256,1024]{1,0:T(8,128)(2,1)S(1)}, bf16[256,1024]{1,0:T(8,128)(2,1)}, u32[]{:S(2)}) copy-start(bf16[256,1024]{1,0:T(8,128)(2,1)} %q_ref.1) | copy-start | bytes 1572868
  26.3 27.0 %collective-permute-start.2 = (bf16[256,1024]{1,0:T(8,128)(2,1)S(1)}, bf16[256,1024]{1,0:T(8,128)(2,1)S(1)}, u32[]{:S(2)}, u32[]{:S(2)}) collective-permute-start(bf16[256,1024]{1,0:T(8,128)(2,1)S(1)} %share.1.rest_0_), channel_id=1, source_target_pairs={{0,12},{4,0},{8,4},{12,8},{1,13},{5,1},{9,5},{13,9},{2,14},{6,2},{... | collective-permute-start | bytes 1572872 | tf_op jit(solution)/shard_map/ppermute | solution.py:473
  30.7 22.6 %collective-permute-start.1 = (bf16[256,1024]{1,0:T(8,128)(2,1)S(1)}, bf16[256,1024]{1,0:T(8,128)(2,1)}, u32[]{:S(2)}, u32[]{:S(2)}) collective-permute-start(bf16[256,1024]{1,0:T(8,128)(2,1)S(1)} %share.1.rest_0_), channel_id=1, source_target_pairs={{0,8},{4,12},{8,0},{12,4},{1,9},{5,13},{9,1},{13,5},{2,10},{6,14},... | collective-permute-start | bytes 1572872 | tf_op jit(solution)/shard_map/ppermute | solution.py:473
  33.1 26.2 %collective-permute-start = (bf16[256,1024]{1,0:T(8,128)(2,1)S(1)}, bf16[256,1024]{1,0:T(8,128)(2,1)}, u32[]{:S(2)}, u32[]{:S(2)}) collective-permute-start(bf16[256,1024]{1,0:T(8,128)(2,1)S(1)} %share.1.rest_0_), channel_id=1, source_target_pairs={{0,4},{4,8},{8,12},{12,0},{1,5},{5,9},{9,13},{13,1},{2,6},{6,10},{... | collective-permute-start | bytes 1572872 | tf_op jit(solution)/shard_map/ppermute | solution.py:473
  49.1 13.1 %all-to-all-start.1 = ((bf16[4,8,8,1024]{3,2,1,0:T(8,128)(2,1)}), bf16[4,8,8,1024]{3,2,1,0:T(8,128)(2,1)S(1)}, u32[]{:S(2)}, u32[]{:S(2)}) async-start(bf16[4,8,8,1024]{3,2,1,0:T(8,128)(2,1)} %place.1), calls=%async_computation.1 | async-start | bytes 1048576 | tf_op jit(solution)/shard_map/all_to_all | solution.py:482
  64.2 18.5 %copy-start.15 = (bf16[256,1024]{1,0:T(8,128)(2,1)S(1)}, bf16[256,1024]{1,0:T(8,128)(2,1)}, u32[]{:S(2)}) copy-start(bf16[256,1024]{1,0:T(8,128)(2,1)} %constant.107.clone.sel2_ref) | copy-start | bytes 1572868
  64.2 18.5 %copy-start.16 = (bf16[1024,256]{1,0:T(8,128)(2,1)S(1)}, bf16[1024,256]{1,0:T(8,128)(2,1)}, u32[]{:S(2)}) copy-start(bf16[1024,256]{1,0:T(8,128)(2,1)} %constant.106.clone.sel1_ref) | copy-start | bytes 1572868
  76.1 19.0 %collective-permute-start.4 = (bf16[256,128]{1,0:T(8,128)(2,1)S(1)}, bf16[256,128]{1,0:T(8,128)(2,1)S(1)}, u32[]{:S(2)}, u32[]{:S(2)}) collective-permute-start(bf16[256,128]{1,0:T(8,128)(2,1)S(1)} %get-tuple-element.25), channel_id=1, source_target_pairs={{16,0},{32,16},{48,32},{64,48},{80,64},{96,80},{112,96},{128,112},... | collective-permute-start | bytes 196616 | tf_op jit(solution)/shard_map/ppermute | solution.py:489
  80.7 14.4 %copy-start.8 = (bf16[128,256]{1,0:T(8,128)(2,1)S(1)}, bf16[128,256]{1,0:T(8,128)(2,1)}, u32[]{:S(2)}) copy-start(bf16[128,256]{1,0:T(8,128)(2,1)} %constant.109.clone.sel3_ref) | copy-start | bytes 196612
  80.7 14.4 %copy-start.9 = (bf16[256,128]{1,0:T(8,128)(2,1)S(1)}, bf16[256,128]{1,0:T(8,128)(2,1)}, u32[]{:S(2)}) copy-start(bf16[256,128]{1,0:T(8,128)(2,1)} %constant.108.clone.selx_ref) | copy-start | bytes 196612
  80.7 14.4 %collective-permute-start.3 = (bf16[256,128]{1,0:T(8,128)(2,1)S(1)}, bf16[256,128]{1,0:T(8,128)(2,1)S(1)}, u32[]{:S(2)}, u32[]{:S(2)}) collective-permute-start(bf16[256,128]{1,0:T(8,128)(2,1)S(1)} %get-tuple-element.26), channel_id=1, source_target_pairs={{0,16},{16,32},{32,48},{48,64},{64,80},{80,96},{96,112},{112,128},... | collective-permute-start | bytes 196616 | tf_op jit(solution)/shard_map/ppermute | solution.py:488
  (3 other events, 2.0 us)

commit v5 on v4

--- a/solution.py
+++ b/solution.py
@@ -295,7 +295,7 @@
         out_shape=tuple(jax.ShapeDtypeStruct(shape, BF) for shape in shapes),
         in_specs=[vmem] * (2 + len(consts)),
         out_specs=(vmem,) * 4,
-        compiler_params=pltpu.CompilerParams(vmem_limit_bytes=24 * 1024 * 1024),
+        compiler_params=pltpu.CompilerParams(vmem_limit_bytes=61 * 1024 * 1024),
         cost_estimate=pl.CostEstimate(flops=0, bytes_accessed=60_000_000, transcendentals=0),
         name="tables",
     )(first, second, *consts)
@@ -468,7 +468,7 @@
     w1, w2, w1x, w2x = weights(w_first, b_first, w_second)
     sel1, sel2, selx, sel3 = selectors()
 
-    shared = share(queries, (zero, w1, w2, w1x, w2x))
+    shared = share(queries, (zero, w2x))
     videos = [shared] + [
         lax.ppermute(
             shared, "qry", [(g[i], g[(i + step) % side]) for g in outer for i in range(side)]
@@ -478,7 +478,7 @@
     seat = lax.axis_index("qry") // (fan // side)
 
     rows = [jnp.repeat(cand_mask[:, c].astype(BF), ROWS // 2)[:, None] for c in (0, BLOCKS - 1)]
-    ready = (w1, w2, w1x, w2x, ends) + tuple(rows)
+    ready = (ends,) + tuple(rows)
     slab = lax.all_to_all(
         place(source, incoming, side, ready), "qry", 0, 0, tiled=True, axis_index_groups=inner
     )

time: 97.8 us -> 97.1 us (level)
  local copies, waits for them, and re-layouts: 5.65 us -> 3.61 us
  Pallas kernels: 20.9 us -> 22.3 us
    pallas_call x1, Pallas kernels: 1.53 us -> 4.17 us  [weights(): pl.pallas_call(tables_body, out_shape=tuple((jax.ShapeDtypeStruct(shape,...]
    unnamed x45 -> x35, local copies, waits for them, and re-layouts: 5.3 us -> 2.67 us
    pallas_call x1, Pallas kernels: 1.94 us -> 0.73 us  [score(): pl.pallas_call(score_body, out_shape=jax.ShapeDtypeStruct((len(videos), R...]
  transfers between devices with their start and end apart: 7 -> 7, of which waited for: 3 -> 3; matrix products, arithmetic and copies ran while one was open for 1% -> 2% of each run, Pallas kernels for 16% -> 19%
where the time goes in v5:
time: 97.1 us; the launch traced here: 96.5 us
  starting transfers between devices  29.6 us (30%)
  Pallas kernels  22.3 us (23%)
  blocking collectives  20.5 us (21%)
  waiting for transfers between devices  19 us (20%)
  local copies, waits for them, and re-layouts  3.61 us (4%)
  other arithmetic  1.07 us (1%)
    pallas_call x1, Pallas kernels, refine(): pl.pallas_call(refine_body, out_shape=(jax.ShapeDtypeStruct((ROWS, COLS),...  12.3 us
    all_to_all x1, blocking collectives, shards(): lax.all_to_all(score(seat[None], slab, videos), 'qry', 0, 0, tiled=True,...  11.8 us
    all_to_all x1, waiting for transfers between devices, shards(): lax.all_to_all(packed, 'ref', 0, 0, tiled=True, axis_index_groups=lines)  9.97 us
    all_to_all x1, starting transfers between devices, shards(): lax.all_to_all(packed, 'ref', 0, 0, tiled=True, axis_index_groups=lines)  9.74 us
    ppermute x3, starting transfers between devices, shards(): lax.ppermute(shared, 'qry', [(g[i], g[(i + step) % side]) for g in outer...  9.32 us
    all_gather x1, blocking collectives, shards(): lax.all_gather(ref_panels, 'ref', axis=0, tiled=True, axis_index_groups=p...  8.71 us
    ppermute x3, waiting for transfers between devices, shards(): lax.ppermute(shared, 'qry', [(g[i], g[(i + step) % side]) for g in outer...  6.19 us
    ppermute x1, starting transfers between devices, shards(): from_right = lax.ppermute(head, 'ref', down)  4.48 us
  transfers between devices with their start and end apart: 7, of which 3 were waited for; matrix products, arithmetic and copies ran while one was open for 2% of the time, Pallas kernels for 19%

profile of v5, /device:TPU:1, one launch (start us, length us, event | category | flops | bytes accessed | tf_op | source)
XLA Modules:
  0.0 96.5 jit_solution(14546571692199281688)
XLA Ops:
  0.0 8.7 %all_gather.3.panels_ref = bf16[16,8,1024]{2,1,0:T(8,128)(2,1)S(1)} all-gather(bf16[8,8,1024]{2,1,0:T(8,128)(2,1)} %param.22), channel_id=1, replica_groups={{0,16},{32,48},{64,80},{96,112},{128,144},{160,176},{192,208},{224,240}..., dimensions={0}, use_global_device_ids=true | all-gather | bytes 393216 | tf_op jit(solution)/shard_map/all_gather | solution.py:460
  8.7 0.7 copy-done.6
  9.4 1.5 %pack.1 = (bf16[32,8,1024]{2,1,0:T(8,128)(2,1)}, f32[8,128]{1,0:T(8,128)S(1)}) custom-call(s32[1]{0:T(128)} %bitcast.3.me_ref, s32[256]{0:T(256)S(1)} %copy-done.6, bf16[16,8,1024]{2,1,0:T(8,128)(2,1)S(1)} %all_gather.3.panels_ref), custom_call_target="tpu_custom_call" | custom-call | bytes 600000 | tf_op jit(solution)/shard_map/pack/pallas_call | solution.py:388
  10.9 9.7 %all-to-all-start = ((bf16[32,8,1024]{2,1,0:T(8,128)(2,1)}), bf16[32,8,1024]{2,1,0:T(8,128)(2,1)S(1)}, u32[]{:S(2)}, u32[]{:S(2)}) async-start(bf16[32,8,1024]{2,1,0:T(8,128)(2,1)} %get-tuple-element.14), calls=%async_computation | async-start | bytes 1048576 | tf_op jit(solution)/shard_map/all_to_all | solution.py:462
  20.8 0.6 pad.4.second_ref
  21.5 0.7 maximum_maximum_fusion.first_ref
  22.2 4.2 %tables.1 = (bf16[256,1024]{1,0:T(8,128)(2,1)}, bf16[1024,512]{1,0:T(8,128)(2,1)}, bf16[256,128]{1,0:T(8,128)(2,1)}, bf16[128,128]{1,0:T(8,128)(2,1)}) custom-call(f32[16,32]{1,0:T(8,128)} %maximum_maximum_fusion.first_ref, bf16[32,16]{1,0:T(8,128)(2,1)} %pad.4.second_ref, bf16[32,1024]{1,0:T(8,128)(2,1)} %constant.96.clone.spread_ref, ...), custom_call_target="tpu_custom_call" | custom-call | bytes 60000000 | tf_op jit(solution)/shard_map/tables/pallas_call | solution.py:293
  26.4 0.8 copy-done.1
  27.2 4.4 %collective-permute-start.2 = (bf16[256,1024]{1,0:T(8,128)(2,1)S(1)}, bf16[256,1024]{1,0:T(8,128)(2,1)S(1)}, u32[]{:S(2)}, u32[]{:S(2)}) collective-permute-start(bf16[256,1024]{1,0:T(8,128)(2,1)S(1)} %share.1.rest_0_), channel_id=1, source_target_pairs={{0,12},{4,0},{8,4},{12,8},{1,13},{5,1},{9,5},{13,9},{2,14},{6,2},{... | collective-permute-start | bytes 1572872 | tf_op jit(solution)/shard_map/ppermute | solution.py:473
  31.6 2.4 %collective-permute-start.1 = (bf16[256,1024]{1,0:T(8,128)(2,1)S(1)}, bf16[256,1024]{1,0:T(8,128)(2,1)S(1)}, u32[]{:S(2)}, u32[]{:S(2)}) collective-permute-start(bf16[256,1024]{1,0:T(8,128)(2,1)S(1)} %share.1.rest_0_), channel_id=1, source_target_pairs={{0,8},{4,12},{8,0},{12,4},{1,9},{5,13},{9,1},{13,5},{2,10},{6,14},... | collective-permute-start | bytes 1572872 | tf_op jit(solution)/shard_map/ppermute | solution.py:473
  34.0 2.5 %collective-permute-start = (bf16[256,1024]{1,0:T(8,128)(2,1)S(1)}, bf16[256,1024]{1,0:T(8,128)(2,1)S(1)}, u32[]{:S(2)}, u32[]{:S(2)}) collective-permute-start(bf16[256,1024]{1,0:T(8,128)(2,1)S(1)} %share.1.rest_0_), channel_id=1, source_target_pairs={{0,4},{4,8},{8,12},{12,0},{1,5},{5,9},{9,13},{13,1},{2,6},{6,10},{... | collective-permute-start | bytes 1572872 | tf_op jit(solution)/shard_map/ppermute | solution.py:473
  36.5 0.7 copy-done.9
  37.2 0.2 slice_reduce_fusion
  38.1 10.0 %all-to-all-done.incoming_ref = bf16[32,8,1024]{2,1,0:T(8,128)(2,1)S(1)} async-done(((bf16[32,8,1024]{2,1,0:T(8,128)(2,1)}), bf16[32,8,1024]{2,1,0:T(8,128)(2,1)S(1)}, u32[]{:S(2)}, u32[]{:S(2)}) %all-to-all-start) | async-done | bytes 524320 | tf_op jit(solution)/shard_map/all_to_all | solution.py:462
  48.1 1.6 %place.1 = bf16[4,8,8,1024]{3,2,1,0:T(8,128)(2,1)} custom-call(s32[8]{0:T(128)S(1)} %broadcast_select_fusion.source_ref, bf16[32,8,1024]{2,1,0:T(8,128)(2,1)S(1)} %all-to-all-done.incoming_ref, s32[2]{0:T(128)S(1)} %add_convert_fusion.rest_0_.ends_ref, bf16[256,1]{1,0:T(8,128)(2,1)S(1)} %bitcast.31, bf16[256,1]{1,0:T(8,128)(2,1)S(1)} %bitcast.32), custom_call_target="tpu_custom_call" | custom-call | bytes 400000000 | tf_op jit(solution)/shard_map/place/pallas_call | solution.py:437
  49.7 4.2 %all-to-all-start.1 = ((bf16[4,8,8,1024]{3,2,1,0:T(8,128)(2,1)}), bf16[4,8,8,1024]{3,2,1,0:T(8,128)(2,1)S(1)}, u32[]{:S(2)}, u32[]{:S(2)}) async-start(bf16[4,8,8,1024]{3,2,1,0:T(8,128)(2,1)} %place.1), calls=%async_computation.1 | async-start | bytes 1048576 | tf_op jit(solution)/shard_map/all_to_all | solution.py:482
  53.9 6.2 %collective-permute-done.rest_1_ = bf16[256,1024]{1,0:T(8,128)(2,1)S(1)} collective-permute-done((bf16[256,1024]{1,0:T(8,128)(2,1)S(1)}, bf16[256,1024]{1,0:T(8,128)(2,1)S(1)}, u32[]{:S(2)}, u32[]{:S(2)}) %collective-permute-start) | collective-permute-done | bytes 524320 | tf_op jit(solution)/shard_map/ppermute | solution.py:473
  60.0 2.9 %all-to-all-done.1.slab_ref = bf16[4,8,8,1024]{3,2,1,0:T(8,128)(2,1)S(1)} async-done(((bf16[4,8,8,1024]{3,2,1,0:T(8,128)(2,1)}), bf16[4,8,8,1024]{3,2,1,0:T(8,128)(2,1)S(1)}, u32[]{:S(2)}, u32[]{:S(2)}) %all-to-all-start.1) | async-done | bytes 524320 | tf_op jit(solution)/shard_map/all_to_all | solution.py:482
  62.9 0.7 score.1
  63.7 11.8 %all_to_all.15.score_ref = bf16[4,256,256]{2,1,0:T(8,128)(2,1)S(1)} all-to-all(bf16[4,256,256]{2,1,0:T(8,128)(2,1)S(1)} %score.1), channel_id=1, replica_groups={{0,4,8,12},{1,5,9,13},{2,6,10,14},{3,7,11,15},{16,20,24,28},{17,21,25,2..., dimensions={0} | all-to-all | bytes 1048576 | tf_op jit(solution)/shard_map/all_to_all | solution.py:485
  75.6 4.5 %collective-permute-start.4 = (bf16[256,128]{1,0:T(8,128)(2,1)S(1)}, bf16[256,128]{1,0:T(8,128)(2,1)S(1)}, u32[]{:S(2)}, u32[]{:S(2)}) collective-permute-start(bf16[256,128]{1,0:T(8,128)(2,1)S(1)} %get-tuple-element.25), channel_id=1, source_target_pairs={{16,0},{32,16},{48,32},{64,48},{80,64},{96,80},{112,96},{128,112},... | collective-permute-start | bytes 196616 | tf_op jit(solution)/shard_map/ppermute | solution.py:489
  80.1 1.9 %collective-permute-start.3 = (bf16[256,128]{1,0:T(8,128)(2,1)S(1)}, bf16[256,128]{1,0:T(8,128)(2,1)S(1)}, u32[]{:S(2)}, u32[]{:S(2)}) collective-permute-start(bf16[256,128]{1,0:T(8,128)(2,1)S(1)} %get-tuple-element.26), channel_id=1, source_target_pairs={{0,16},{16,32},{32,48},{48,64},{64,80},{80,96},{96,112},{112,128},... | collective-permute-start | bytes 196616 | tf_op jit(solution)/shard_map/ppermute | solution.py:488
  82.1 12.3 %refine.1 = (bf16[256,1024]{1,0:T(8,128)(2,1)}, f32[256,128]{1,0:T(8,128)S(1)}, f32[2,256,128]{2,1,0:T(8,128)S(1)}) custom-call(s32[2,8]{1,0:T(2,128)S(1)} %copy-done.9, bf16[4,256,256]{2,1,0:T(8,128)(2,1)S(1)} %all_to_all.15.score_ref, bf16[1024,256]{1,0:T(8,128)(2,1)S(1)} %copy-done.11, bf16[256,1024]{1,0:T(8,128)(2,1)S(1)} %copy-done.8, ...), custom_call_target="tpu_custom_call" | custom-call | flops 9400000512 | bytes 8000000 | tf_op jit(solution)/shard_map/refine/pallas_call | solution.py:306
  94.5 2.0 %sides.1 = bf16[256,1024]{1,0:T(8,128)(2,1)} custom-call(s32[2]{0:T(128)S(1)} %add_convert_fusion.rest_0_.ends_ref, bf16[256,128]{1,0:T(8,128)(2,1)S(1)} %collective-permute-done.3.left_ref, bf16[256,128]{1,0:T(8,128)(2,1)S(1)} %collective-permute-done.4.right_ref, f32[256,128]{1,0:T(8,128)S(1)} %get-tuple-element.19.own_ref, ...), custom_call_target="tpu_custom_call", output_to_operand_aliasing={{}: (9, {})} | custom-call | flops 60000000 | bytes 1500000 | tf_op jit(solution)/shard_map/sides/pallas_call | solution.py:332
  (48 shorter events, 1.2 us)
Async XLA Ops:
  8.7 0.7 copy-start.6
  10.9 9.8 %copy-start.13 = (bf16[9,32]{1,0:T(8,128)(2,1)S(1)}, bf16[9,32]{1,0:T(8,128)(2,1)}, u32[]{:S(2)}) copy-start(bf16[9,32]{1,0:T(8,128)(2,1)} %param.27) | copy-start | bytes 1732
  10.9 37.2 %all-to-all-start = ((bf16[32,8,1024]{2,1,0:T(8,128)(2,1)}), bf16[32,8,1024]{2,1,0:T(8,128)(2,1)S(1)}, u32[]{:S(2)}, u32[]{:S(2)}) async-start(bf16[32,8,1024]{2,1,0:T(8,128)(2,1)} %get-tuple-element.14), calls=%async_computation | async-start | bytes 1048576 | tf_op jit(solution)/shard_map/all_to_all | solution.py:462
  20.8 0.7 copy-start.14
  20.8 0.7 copy-start.12
  22.2 4.2 %copy-start = (bf16[256,1024]{1,0:T(8,128)(2,1)S(1)}, bf16[256,1024]{1,0:T(8,128)(2,1)}, u32[]{:S(2)}) copy-start(bf16[256,1024]{1,0:T(8,128)(2,1)} %q_ref.1) | copy-start | bytes 1572868
  26.4 0.8 copy-start.1
  27.2 26.7 %collective-permute-start.2 = (bf16[256,1024]{1,0:T(8,128)(2,1)S(1)}, bf16[256,1024]{1,0:T(8,128)(2,1)S(1)}, u32[]{:S(2)}, u32[]{:S(2)}) collective-permute-start(bf16[256,1024]{1,0:T(8,128)(2,1)S(1)} %share.1.rest_0_), channel_id=1, source_target_pairs={{0,12},{4,0},{8,4},{12,8},{1,13},{5,1},{9,5},{13,9},{2,14},{6,2},{... | collective-permute-start | bytes 1572872 | tf_op jit(solution)/shard_map/ppermute | solution.py:473
  31.6 22.3 %collective-permute-start.1 = (bf16[256,1024]{1,0:T(8,128)(2,1)S(1)}, bf16[256,1024]{1,0:T(8,128)(2,1)S(1)}, u32[]{:S(2)}, u32[]{:S(2)}) collective-permute-start(bf16[256,1024]{1,0:T(8,128)(2,1)S(1)} %share.1.rest_0_), channel_id=1, source_target_pairs={{0,8},{4,12},{8,0},{12,4},{1,9},{5,13},{9,1},{13,5},{2,10},{6,14},... | collective-permute-start | bytes 1572872 | tf_op jit(solution)/shard_map/ppermute | solution.py:473
  34.0 26.0 %collective-permute-start = (bf16[256,1024]{1,0:T(8,128)(2,1)S(1)}, bf16[256,1024]{1,0:T(8,128)(2,1)S(1)}, u32[]{:S(2)}, u32[]{:S(2)}) collective-permute-start(bf16[256,1024]{1,0:T(8,128)(2,1)S(1)} %share.1.rest_0_), channel_id=1, source_target_pairs={{0,4},{4,8},{8,12},{12,0},{1,5},{5,9},{9,13},{13,1},{2,6},{6,10},{... | collective-permute-start | bytes 1572872 | tf_op jit(solution)/shard_map/ppermute | solution.py:473
  36.5 0.7 copy-start.9
  49.7 13.3 %all-to-all-start.1 = ((bf16[4,8,8,1024]{3,2,1,0:T(8,128)(2,1)}), bf16[4,8,8,1024]{3,2,1,0:T(8,128)(2,1)S(1)}, u32[]{:S(2)}, u32[]{:S(2)}) async-start(bf16[4,8,8,1024]{3,2,1,0:T(8,128)(2,1)} %place.1), calls=%async_computation.1 | async-start | bytes 1048576 | tf_op jit(solution)/shard_map/all_to_all | solution.py:482
  62.9 19.1 %copy-start.8 = (bf16[256,1024]{1,0:T(8,128)(2,1)S(1)}, bf16[256,1024]{1,0:T(8,128)(2,1)}, u32[]{:S(2)}) copy-start(bf16[256,1024]{1,0:T(8,128)(2,1)} %get-tuple-element.17.w1_ref) | copy-start | bytes 1572868
  62.9 19.1 %copy-start.10 = (bf16[256,1024]{1,0:T(8,128)(2,1)S(1)}, bf16[256,1024]{1,0:T(8,128)(2,1)}, u32[]{:S(2)}) copy-start(bf16[256,1024]{1,0:T(8,128)(2,1)} %constant.107.clone.sel2_ref) | copy-start | bytes 1572868
  62.9 19.1 %copy-start.11 = (bf16[1024,256]{1,0:T(8,128)(2,1)S(1)}, bf16[1024,256]{1,0:T(8,128)(2,1)}, u32[]{:S(2)}) copy-start(bf16[1024,256]{1,0:T(8,128)(2,1)} %constant.106.clone.sel1_ref) | copy-start | bytes 1572868
  63.7 18.4 %copy-start.7 = (bf16[1024,512]{1,0:T(8,128)(2,1)S(1)}, bf16[1024,512]{1,0:T(8,128)(2,1)}, u32[]{:S(2)}) copy-start(bf16[1024,512]{1,0:T(8,128)(2,1)} %get-tuple-element.18.w2_ref) | copy-start | bytes 3145732
  75.6 18.8 %collective-permute-start.4 = (bf16[256,128]{1,0:T(8,128)(2,1)S(1)}, bf16[256,128]{1,0:T(8,128)(2,1)S(1)}, u32[]{:S(2)}, u32[]{:S(2)}) collective-permute-start(bf16[256,128]{1,0:T(8,128)(2,1)S(1)} %get-tuple-element.25), channel_id=1, source_target_pairs={{16,0},{32,16},{48,32},{64,48},{80,64},{96,80},{112,96},{128,112},... | collective-permute-start | bytes 196616 | tf_op jit(solution)/shard_map/ppermute | solution.py:489
  80.1 14.3 %collective-permute-start.3 = (bf16[256,128]{1,0:T(8,128)(2,1)S(1)}, bf16[256,128]{1,0:T(8,128)(2,1)S(1)}, u32[]{:S(2)}, u32[]{:S(2)}) collective-permute-start(bf16[256,128]{1,0:T(8,128)(2,1)S(1)} %get-tuple-element.26), channel_id=1, source_target_pairs={{0,16},{16,32},{32,48},{48,64},{64,80},{80,96},{96,112},{112,128},... | collective-permute-start | bytes 196616 | tf_op jit(solution)/shard_map/ppermute | solution.py:488
  82.1 12.4 %copy-start.2 = (bf16[128,128]{1,0:T(8,128)(2,1)S(1)}, bf16[128,128]{1,0:T(8,128)(2,1)}, u32[]{:S(2)}) copy-start(bf16[128,128]{1,0:T(8,128)(2,1)} %get-tuple-element.16.rest_1_.w2x_ref) | copy-start | bytes 98308
  82.1 12.4 %copy-start.3 = (bf16[128,256]{1,0:T(8,128)(2,1)S(1)}, bf16[128,256]{1,0:T(8,128)(2,1)}, u32[]{:S(2)}) copy-start(bf16[128,256]{1,0:T(8,128)(2,1)} %constant.109.clone.sel3_ref) | copy-start | bytes 196612
  82.1 12.4 %copy-start.4 = (bf16[256,128]{1,0:T(8,128)(2,1)S(1)}, bf16[256,128]{1,0:T(8,128)(2,1)}, u32[]{:S(2)}) copy-start(bf16[256,128]{1,0:T(8,128)(2,1)} %constant.108.clone.selx_ref) | copy-start | bytes 196612
  82.1 12.4 %copy-start.5 = (bf16[256,128]{1,0:T(8,128)(2,1)S(1)}, bf16[256,128]{1,0:T(8,128)(2,1)}, u32[]{:S(2)}) copy-start(bf16[256,128]{1,0:T(8,128)(2,1)} %get-tuple-element.21.w1x_ref) | copy-start | bytes 196612

commit v6 on v5

--- a/solution.py
+++ b/solution.py
@@ -370,9 +370,7 @@
     jobs = []
     for i in range(2 * BLOCKS):
         owner = time_ref[first * BLOCKS + i] // BLOCKS
-        chip = owner // 2
-        chip = jnp.where(lax.rem(me, 2) == 0, chip, out_ref.shape[0] // 2 - 1 - chip)
-        slot = 2 * chip + i // BLOCKS
+        slot = owner - lax.rem(owner, 2) + i // BLOCKS
         copy = pltpu.make_async_copy(panels_ref.at[i], out_ref.at[slot], sems.at[i])
         jobs.append((lax.rem(owner, 2) == lax.rem(me, 2), copy))
     for wanted, copy in jobs:
@@ -453,7 +451,7 @@
     up = [(i, i + 1) for i in range(owners - 1)]
     down = [(i + 1, i) for i in range(owners - 1)]
     pairs = [[2 * z, 2 * z + 1] for z in range(owners // 2)]
-    lines = [[2 * z + c for z in range(owners // 2)][:: 1 - 2 * c] for c in range(2)]
+    lines = [[2 * z + c for z in range(owners // 2)] for c in range(2)]
     side = LANES // WIN
     outer = [[i + side * j for j in range(side)] for i in range(fan // side)]
     inner = [[side * j + i for i in range(side)] for j in range(fan // side)]
@@ -463,7 +461,6 @@
     holder = jnp.arange(owners * BLOCKS, dtype=I) // BLOCKS
     mine = panel_time[None, :] == me * BLOCKS + jnp.arange(BLOCKS, dtype=I)[:, None]
     source = jnp.sum(jnp.where(mine, holder[None, :], 0), axis=1)
-    source = jnp.where(me % 2 == 0, source, owners - 2 - source + 2 * (source % 2))
     ends = jnp.stack([(me > 0).astype(I), (me < owners - 1).astype(I)])
     w1, w2, w1x, w2x = weights(w_first, b_first, w_second)
     sel1, sel2, selx, sel3 = selectors()

time: 97.1 us -> 98.3 us (1.012)
  starting transfers between devices: 29.6 us -> 36.1 us
  waiting for transfers between devices: 19 us -> 16.2 us
  blocking collectives: 20.5 us -> 18.2 us
    ppermute x1, starting transfers between devices: 4.48 us -> 9.39 us  [shards(): from_right = lax.ppermute(head, 'ref', down)]
    ppermute x3, waiting for transfers between devices: 6.19 us -> 10.9 us  [shards(): lax.ppermute(shared, 'qry', [(g[i], g[(i + step) % side]) for g in outer...]
    all_to_all x1, waiting for transfers between devices: 9.97 us -> 5.32 us  [shards(): lax.all_to_all(packed, 'ref', 0, 0, tiled=True, axis_index_groups=lines)]
    all_to_all x1, waiting for transfers between devices: 2.87 us -> 0.01 us  [shards(): lax.all_to_all(place(source, incoming, side, ready), 'qry', 0, 0, tiled=T...]
    all_to_all x1, blocking collectives: 11.8 us -> 9.46 us  [shards(): lax.all_to_all(score(seat[None], slab, videos), 'qry', 0, 0, tiled=True,...]
    ppermute x1, starting transfers between devices: 1.92 us -> 3.57 us  [shards(): from_left = lax.ppermute(tail, 'ref', up)]
  transfers between devices with their start and end apart: 7 -> 7, of which waited for: 3 -> 2; matrix products, arithmetic and copies ran while one was open for 2% -> 2% of each run, Pallas kernels for 19% -> 19%
where the time goes in v6:
time: 98.3 us; the launch traced here: 97.6 us
  starting transfers between devices  36.1 us (37%)
  Pallas kernels  22.3 us (23%)
  blocking collectives  18.2 us (19%)
  waiting for transfers between devices  16.2 us (16%)
  local copies, waits for them, and re-layouts  3.61 us (4%)
  other arithmetic  1.06 us (1%)
    pallas_call x1, Pallas kernels, refine(): pl.pallas_call(refine_body, out_shape=(jax.ShapeDtypeStruct((ROWS, COLS),...  12.3 us
    ppermute x3, waiting for transfers between devices, shards(): lax.ppermute(shared, 'qry', [(g[i], g[(i + step) % side]) for g in outer...  10.9 us
    all_to_all x1, starting transfers between devices, shards(): lax.all_to_all(packed, 'ref', 0, 0, tiled=True, axis_index_groups=lines)  9.58 us
    all_to_all x1, blocking collectives, shards(): lax.all_to_all(score(seat[None], slab, videos), 'qry', 0, 0, tiled=True,...  9.46 us
    ppermute x1, starting transfers between devices, shards(): from_right = lax.ppermute(head, 'ref', down)  9.39 us
    ppermute x3, starting transfers between devices, shards(): lax.ppermute(shared, 'qry', [(g[i], g[(i + step) % side]) for g in outer...  9.32 us
    all_gather x1, blocking collectives, shards(): lax.all_gather(ref_panels, 'ref', axis=0, tiled=True, axis_index_groups=p...  8.71 us
    all_to_all x1, waiting for transfers between devices, shards(): lax.all_to_all(packed, 'ref', 0, 0, tiled=True, axis_index_groups=lines)  5.32 us
  transfers between devices with their start and end apart: 7, of which 2 were waited for; matrix products, arithmetic and copies ran while one was open for 2% of the time, Pallas kernels for 19%

profile of v6, /device:TPU:1, one launch (start us, length us, event | category | flops | bytes accessed | tf_op | source)
XLA Modules:
  0.0 97.6 jit_solution(9924966036375039353)
XLA Ops:
  0.0 8.7 %all_gather.3.panels_ref = bf16[16,8,1024]{2,1,0:T(8,128)(2,1)S(1)} all-gather(bf16[8,8,1024]{2,1,0:T(8,128)(2,1)} %param.22), channel_id=1, replica_groups={{0,16},{32,48},{64,80},{96,112},{128,144},{160,176},{192,208},{224,240}..., dimensions={0}, use_global_device_ids=true | all-gather | bytes 393216 | tf_op jit(solution)/shard_map/all_gather | solution.py:458
  8.7 0.7 copy-done.6
  9.4 1.4 %pack.1 = (bf16[32,8,1024]{2,1,0:T(8,128)(2,1)}, f32[8,128]{1,0:T(8,128)S(1)}) custom-call(s32[1]{0:T(128)} %bitcast.3.me_ref, s32[256]{0:T(256)S(1)} %copy-done.6, bf16[16,8,1024]{2,1,0:T(8,128)(2,1)S(1)} %all_gather.3.panels_ref), custom_call_target="tpu_custom_call" | custom-call | bytes 600000 | tf_op jit(solution)/shard_map/pack/pallas_call | solution.py:386
  10.8 9.6 %all-to-all-start = ((bf16[32,8,1024]{2,1,0:T(8,128)(2,1)}), bf16[32,8,1024]{2,1,0:T(8,128)(2,1)S(1)}, u32[]{:S(2)}, u32[]{:S(2)}) async-start(bf16[32,8,1024]{2,1,0:T(8,128)(2,1)} %get-tuple-element.14), calls=%async_computation | async-start | bytes 1048576 | tf_op jit(solution)/shard_map/all_to_all | solution.py:460
  20.6 0.6 pad.4.second_ref
  21.3 0.7 maximum_maximum_fusion.first_ref
  22.0 4.2 %tables.1 = (bf16[256,1024]{1,0:T(8,128)(2,1)}, bf16[1024,512]{1,0:T(8,128)(2,1)}, bf16[256,128]{1,0:T(8,128)(2,1)}, bf16[128,128]{1,0:T(8,128)(2,1)}) custom-call(f32[16,32]{1,0:T(8,128)} %maximum_maximum_fusion.first_ref, bf16[32,16]{1,0:T(8,128)(2,1)} %pad.4.second_ref, bf16[32,1024]{1,0:T(8,128)(2,1)} %constant.75.clone.spread_ref, ...), custom_call_target="tpu_custom_call" | custom-call | bytes 60000000 | tf_op jit(solution)/shard_map/tables/pallas_call | solution.py:293
  26.2 0.8 copy-done.1
  26.9 4.4 %collective-permute-start.2 = (bf16[256,1024]{1,0:T(8,128)(2,1)S(1)}, bf16[256,1024]{1,0:T(8,128)(2,1)S(1)}, u32[]{:S(2)}, u32[]{:S(2)}) collective-permute-start(bf16[256,1024]{1,0:T(8,128)(2,1)S(1)} %share.1.rest_0_), channel_id=1, source_target_pairs={{0,12},{4,0},{8,4},{12,8},{1,13},{5,1},{9,5},{13,9},{2,14},{6,2},{... | collective-permute-start | bytes 1572872 | tf_op jit(solution)/shard_map/ppermute | solution.py:470
  31.3 2.4 %collective-permute-start.1 = (bf16[256,1024]{1,0:T(8,128)(2,1)S(1)}, bf16[256,1024]{1,0:T(8,128)(2,1)S(1)}, u32[]{:S(2)}, u32[]{:S(2)}) collective-permute-start(bf16[256,1024]{1,0:T(8,128)(2,1)S(1)} %share.1.rest_0_), channel_id=1, source_target_pairs={{0,8},{4,12},{8,0},{12,4},{1,9},{5,13},{9,1},{13,5},{2,10},{6,14},... | collective-permute-start | bytes 1572872 | tf_op jit(solution)/shard_map/ppermute | solution.py:470
  33.8 2.5 %collective-permute-start = (bf16[256,1024]{1,0:T(8,128)(2,1)S(1)}, bf16[256,1024]{1,0:T(8,128)(2,1)S(1)}, u32[]{:S(2)}, u32[]{:S(2)}) collective-permute-start(bf16[256,1024]{1,0:T(8,128)(2,1)S(1)} %share.1.rest_0_), channel_id=1, source_target_pairs={{0,4},{4,8},{8,12},{12,0},{1,5},{5,9},{9,13},{13,1},{2,6},{6,10},{... | collective-permute-start | bytes 1572872 | tf_op jit(solution)/shard_map/ppermute | solution.py:470
  36.3 0.7 copy-done.9
  37.0 0.2 slice_reduce_fusion
  37.6 0.2 select_reduce_fusion.source_ref
  37.8 5.3 %all-to-all-done.incoming_ref = bf16[32,8,1024]{2,1,0:T(8,128)(2,1)S(1)} async-done(((bf16[32,8,1024]{2,1,0:T(8,128)(2,1)}), bf16[32,8,1024]{2,1,0:T(8,128)(2,1)S(1)}, u32[]{:S(2)}, u32[]{:S(2)}) %all-to-all-start) | async-done | bytes 524320 | tf_op jit(solution)/shard_map/all_to_all | solution.py:460
  43.1 1.6 %place.1 = bf16[4,8,8,1024]{3,2,1,0:T(8,128)(2,1)} custom-call(s32[8]{0:T(128)S(1)} %select_reduce_fusion.source_ref, bf16[32,8,1024]{2,1,0:T(8,128)(2,1)S(1)} %all-to-all-done.incoming_ref, s32[2]{0:T(128)S(1)} %add_convert_fusion.rest_0_.ends_ref, bf16[256,1]{1,0:T(8,128)(2,1)S(1)} %bitcast.31, bf16[256,1]{1,0:T(8,128)(2,1)S(1)} %bitcast.32), custom_call_target="tpu_custom_call" | custom-call | bytes 400000000 | tf_op jit(solution)/shard_map/place/pallas_call | solution.py:435
  44.7 4.2 %all-to-all-start.1 = ((bf16[4,8,8,1024]{3,2,1,0:T(8,128)(2,1)}), bf16[4,8,8,1024]{3,2,1,0:T(8,128)(2,1)S(1)}, u32[]{:S(2)}, u32[]{:S(2)}) async-start(bf16[4,8,8,1024]{3,2,1,0:T(8,128)(2,1)} %place.1), calls=%async_computation.1 | async-start | bytes 1048576 | tf_op jit(solution)/shard_map/all_to_all | solution.py:479
  48.9 10.9 %collective-permute-done.rest_1_ = bf16[256,1024]{1,0:T(8,128)(2,1)S(1)} collective-permute-done((bf16[256,1024]{1,0:T(8,128)(2,1)S(1)}, bf16[256,1024]{1,0:T(8,128)(2,1)S(1)}, u32[]{:S(2)}, u32[]{:S(2)}) %collective-permute-start) | collective-permute-done | bytes 524320 | tf_op jit(solution)/shard_map/ppermute | solution.py:470
  59.8 0.7 score.1
  60.6 9.5 %all_to_all.15.score_ref = bf16[4,256,256]{2,1,0:T(8,128)(2,1)S(1)} all-to-all(bf16[4,256,256]{2,1,0:T(8,128)(2,1)S(1)} %score.1), channel_id=1, replica_groups={{0,4,8,12},{1,5,9,13},{2,6,10,14},{3,7,11,15},{16,20,24,28},{17,21,25,2..., dimensions={0} | all-to-all | bytes 1048576 | tf_op jit(solution)/shard_map/all_to_all | solution.py:482
  70.2 9.4 %collective-permute-start.4 = (bf16[256,128]{1,0:T(8,128)(2,1)S(1)}, bf16[256,128]{1,0:T(8,128)(2,1)S(1)}, u32[]{:S(2)}, u32[]{:S(2)}) collective-permute-start(bf16[256,128]{1,0:T(8,128)(2,1)S(1)} %get-tuple-element.25), channel_id=1, source_target_pairs={{16,0},{32,16},{48,32},{64,48},{80,64},{96,80},{112,96},{128,112},... | collective-permute-start | bytes 196616 | tf_op jit(solution)/shard_map/ppermute | solution.py:486
  79.6 3.6 %collective-permute-start.3 = (bf16[256,128]{1,0:T(8,128)(2,1)S(1)}, bf16[256,128]{1,0:T(8,128)(2,1)S(1)}, u32[]{:S(2)}, u32[]{:S(2)}) collective-permute-start(bf16[256,128]{1,0:T(8,128)(2,1)S(1)} %get-tuple-element.26), channel_id=1, source_target_pairs={{0,16},{16,32},{32,48},{48,64},{64,80},{80,96},{96,112},{112,128},... | collective-permute-start | bytes 196616 | tf_op jit(solution)/shard_map/ppermute | solution.py:485
  83.3 12.3 %refine.1 = (bf16[256,1024]{1,0:T(8,128)(2,1)}, f32[256,128]{1,0:T(8,128)S(1)}, f32[2,256,128]{2,1,0:T(8,128)S(1)}) custom-call(s32[2,8]{1,0:T(2,128)S(1)} %copy-done.9, bf16[4,256,256]{2,1,0:T(8,128)(2,1)S(1)} %all_to_all.15.score_ref, bf16[1024,256]{1,0:T(8,128)(2,1)S(1)} %copy-done.11, bf16[256,1024]{1,0:T(8,128)(2,1)S(1)} %copy-done.8, ...), custom_call_target="tpu_custom_call" | custom-call | flops 9400000512 | bytes 8000000 | tf_op jit(solution)/shard_map/refine/pallas_call | solution.py:306
  95.6 2.0 %sides.1 = bf16[256,1024]{1,0:T(8,128)(2,1)} custom-call(s32[2]{0:T(128)S(1)} %add_convert_fusion.rest_0_.ends_ref, bf16[256,128]{1,0:T(8,128)(2,1)S(1)} %collective-permute-done.3.left_ref, bf16[256,128]{1,0:T(8,128)(2,1)S(1)} %collective-permute-done.4.right_ref, f32[256,128]{1,0:T(8,128)S(1)} %get-tuple-element.19.own_ref, ...), custom_call_target="tpu_custom_call", output_to_operand_aliasing={{}: (9, {})} | custom-call | flops 60000000 | bytes 1500000 | tf_op jit(solution)/shard_map/sides/pallas_call | solution.py:332
  (47 shorter events, 1.0 us)
Async XLA Ops:
  8.7 0.7 copy-start.6
  10.8 9.6 %copy-start.13 = (bf16[9,32]{1,0:T(8,128)(2,1)S(1)}, bf16[9,32]{1,0:T(8,128)(2,1)}, u32[]{:S(2)}) copy-start(bf16[9,32]{1,0:T(8,128)(2,1)} %param.27) | copy-start | bytes 1732
  10.8 32.3 %all-to-all-start = ((bf16[32,8,1024]{2,1,0:T(8,128)(2,1)}), bf16[32,8,1024]{2,1,0:T(8,128)(2,1)S(1)}, u32[]{:S(2)}, u32[]{:S(2)}) async-start(bf16[32,8,1024]{2,1,0:T(8,128)(2,1)} %get-tuple-element.14), calls=%async_computation | async-start | bytes 1048576 | tf_op jit(solution)/shard_map/all_to_all | solution.py:460
  20.6 0.7 copy-start.14
  20.6 0.7 copy-start.12
  22.0 4.2 %copy-start = (bf16[256,1024]{1,0:T(8,128)(2,1)S(1)}, bf16[256,1024]{1,0:T(8,128)(2,1)}, u32[]{:S(2)}) copy-start(bf16[256,1024]{1,0:T(8,128)(2,1)} %q_ref.1) | copy-start | bytes 1572868
  26.2 0.8 copy-start.1
  26.9 22.0 %collective-permute-start.2 = (bf16[256,1024]{1,0:T(8,128)(2,1)S(1)}, bf16[256,1024]{1,0:T(8,128)(2,1)S(1)}, u32[]{:S(2)}, u32[]{:S(2)}) collective-permute-start(bf16[256,1024]{1,0:T(8,128)(2,1)S(1)} %share.1.rest_0_), channel_id=1, source_target_pairs={{0,12},{4,0},{8,4},{12,8},{1,13},{5,1},{9,5},{13,9},{2,14},{6,2},{... | collective-permute-start | bytes 1572872 | tf_op jit(solution)/shard_map/ppermute | solution.py:470
  31.3 17.6 %collective-permute-start.1 = (bf16[256,1024]{1,0:T(8,128)(2,1)S(1)}, bf16[256,1024]{1,0:T(8,128)(2,1)S(1)}, u32[]{:S(2)}, u32[]{:S(2)}) collective-permute-start(bf16[256,1024]{1,0:T(8,128)(2,1)S(1)} %share.1.rest_0_), channel_id=1, source_target_pairs={{0,8},{4,12},{8,0},{12,4},{1,9},{5,13},{9,1},{13,5},{2,10},{6,14},... | collective-permute-start | bytes 1572872 | tf_op jit(solution)/shard_map/ppermute | solution.py:470
  33.8 26.0 %collective-permute-start = (bf16[256,1024]{1,0:T(8,128)(2,1)S(1)}, bf16[256,1024]{1,0:T(8,128)(2,1)S(1)}, u32[]{:S(2)}, u32[]{:S(2)}) collective-permute-start(bf16[256,1024]{1,0:T(8,128)(2,1)S(1)} %share.1.rest_0_), channel_id=1, source_target_pairs={{0,4},{4,8},{8,12},{12,0},{1,5},{5,9},{9,13},{13,1},{2,6},{6,10},{... | collective-permute-start | bytes 1572872 | tf_op jit(solution)/shard_map/ppermute | solution.py:470
  36.3 0.7 copy-start.9
  44.7 15.1 %all-to-all-start.1 = ((bf16[4,8,8,1024]{3,2,1,0:T(8,128)(2,1)}), bf16[4,8,8,1024]{3,2,1,0:T(8,128)(2,1)S(1)}, u32[]{:S(2)}, u32[]{:S(2)}) async-start(bf16[4,8,8,1024]{3,2,1,0:T(8,128)(2,1)} %place.1), calls=%async_computation.1 | async-start | bytes 1048576 | tf_op jit(solution)/shard_map/all_to_all | solution.py:479
  59.8 23.4 %copy-start.8 = (bf16[256,1024]{1,0:T(8,128)(2,1)S(1)}, bf16[256,1024]{1,0:T(8,128)(2,1)}, u32[]{:S(2)}) copy-start(bf16[256,1024]{1,0:T(8,128)(2,1)} %get-tuple-element.17.w1_ref) | copy-start | bytes 1572868
  59.8 23.4 %copy-start.10 = (bf16[256,1024]{1,0:T(8,128)(2,1)S(1)}, bf16[256,1024]{1,0:T(8,128)(2,1)}, u32[]{:S(2)}) copy-start(bf16[256,1024]{1,0:T(8,128)(2,1)} %constant.86.clone.sel2_ref) | copy-start | bytes 1572868
  59.8 23.4 %copy-start.11 = (bf16[1024,256]{1,0:T(8,128)(2,1)S(1)}, bf16[1024,256]{1,0:T(8,128)(2,1)}, u32[]{:S(2)}) copy-start(bf16[1024,256]{1,0:T(8,128)(2,1)} %constant.85.clone.sel1_ref) | copy-start | bytes 1572868
  60.6 22.6 %copy-start.7 = (bf16[1024,512]{1,0:T(8,128)(2,1)S(1)}, bf16[1024,512]{1,0:T(8,128)(2,1)}, u32[]{:S(2)}) copy-start(bf16[1024,512]{1,0:T(8,128)(2,1)} %get-tuple-element.18.w2_ref) | copy-start | bytes 3145732
  70.2 25.4 %collective-permute-start.4 = (bf16[256,128]{1,0:T(8,128)(2,1)S(1)}, bf16[256,128]{1,0:T(8,128)(2,1)S(1)}, u32[]{:S(2)}, u32[]{:S(2)}) collective-permute-start(bf16[256,128]{1,0:T(8,128)(2,1)S(1)} %get-tuple-element.25), channel_id=1, source_target_pairs={{16,0},{32,16},{48,32},{64,48},{80,64},{96,80},{112,96},{128,112},... | collective-permute-start | bytes 196616 | tf_op jit(solution)/shard_map/ppermute | solution.py:486
  79.6 16.0 %collective-permute-start.3 = (bf16[256,128]{1,0:T(8,128)(2,1)S(1)}, bf16[256,128]{1,0:T(8,128)(2,1)S(1)}, u32[]{:S(2)}, u32[]{:S(2)}) collective-permute-start(bf16[256,128]{1,0:T(8,128)(2,1)S(1)} %get-tuple-element.26), channel_id=1, source_target_pairs={{0,16},{16,32},{32,48},{48,64},{64,80},{80,96},{96,112},{112,128},... | collective-permute-start | bytes 196616 | tf_op jit(solution)/shard_map/ppermute | solution.py:485
  83.2 12.4 %copy-start.2 = (bf16[128,128]{1,0:T(8,128)(2,1)S(1)}, bf16[128,128]{1,0:T(8,128)(2,1)}, u32[]{:S(2)}) copy-start(bf16[128,128]{1,0:T(8,128)(2,1)} %get-tuple-element.16.rest_1_.w2x_ref) | copy-start | bytes 98308
  83.2 12.3 %copy-start.3 = (bf16[128,256]{1,0:T(8,128)(2,1)S(1)}, bf16[128,256]{1,0:T(8,128)(2,1)}, u32[]{:S(2)}) copy-start(bf16[128,256]{1,0:T(8,128)(2,1)} %constant.88.clone.sel3_ref) | copy-start | bytes 196612
  83.2 12.3 %copy-start.4 = (bf16[256,128]{1,0:T(8,128)(2,1)S(1)}, bf16[256,128]{1,0:T(8,128)(2,1)}, u32[]{:S(2)}) copy-start(bf16[256,128]{1,0:T(8,128)(2,1)} %constant.87.clone.selx_ref) | copy-start | bytes 196612
  83.3 12.3 %copy-start.5 = (bf16[256,128]{1,0:T(8,128)(2,1)S(1)}, bf16[256,128]{1,0:T(8,128)(2,1)}, u32[]{:S(2)}) copy-start(bf16[256,128]{1,0:T(8,128)(2,1)} %get-tuple-element.21.w1x_ref) | copy-start | bytes 196612
